TPU v7x, 256 devices: a whole 4x4x8 slice. The times are simulated.
256 devices in a mesh: occ: 32 (over x, z_hi, y), grp: 8 (over z_lo, core).
Axes of the slice: x: 4, y: 4, z: 8 (z_hi: 2, z_lo: 4; z = z_hi * 4 + z_lo), core: 2. Of those that a mesh axis runs over, the one named last changes fastest.
Arguments:
- b_factors: bfloat16 [256, 512, 768], P(('occ', 'grp')), may hold values from -0.29882812 to 0.29882812
- occ_energy: float32 [256], replicated, may hold values from -2 to -0.5
- vir_energy: float32 [512], replicated, may hold values from 0.2 to 3
- integrals: bfloat16 [512, 768, 1024], P('grp', 'occ'), may hold values from -0.0625 to 0.0625
- window_start: int32 [1], replicated, may hold values from 0 to 31
Outputs:
- aux_metric: float32 [768, 768], P('occ', 'grp')
- lagrangian: float32 [256, 1024], P('occ', 'grp')
Inputs may be any that keep to these rules, and one draw needn't show every extreme that they name: `window_start`: the cycle offset of the window's first pair.
All inputs are finite; a program needn't handle non-finite values.
Results may differ from a plain program's by a relative error of at most 0.0034.
Values may be sent and summed in bfloat16 or wider, within the bound.
No kernel may reach another device: no remote copies, remote signals or barrier semaphores. Data moves between devices by JAX's collectives and lax.ppermute only.
A program may use at most 64 MiB of HBM per device.

v0:
```python
import jax
import jax.numpy as jnp
from jax import lax
from jax.sharding import PartitionSpec as P

SHIFTS = 3


def shifted(x, axis, by):
    size = lax.axis_size(axis)
    return lax.ppermute(x, axis, [(i, (i + by) % size) for i in range(size)])


def local(b_factors, occ_energy, vir_energy, integrals, window_start):
    n_cycle = lax.axis_size("occ")
    n_group = lax.axis_size("grp")
    cycle_pos = lax.axis_index("occ")
    group_pos = lax.axis_index("grp")
    offset = window_start[0]
    every_orbital = jnp.arange(occ_energy.shape[0], dtype=jnp.int32)
    own_index = cycle_pos * n_group + group_pos
    own_energy = jnp.sum(jnp.where(every_orbital == own_index, occ_energy, 0.0))
    own_rows = b_factors[0]
    rotated = b_factors
    for bit_no in range(n_cycle.bit_length() - 1):
        arrived = shifted(rotated, "occ", 1 << bit_no)
        bit_set = jnp.bitwise_and(jnp.right_shift(offset, bit_no), 1) == 1
        rotated = jnp.where(bit_set, arrived, rotated)
    total = jnp.zeros(own_rows.shape, jnp.float32)
    current = rotated
    for step_no in range(SHIFTS):
        if step_no > 0:
            current = shifted(current, "occ", 1)
        other_rows = current[0]
        partner = jnp.mod(cycle_pos - offset - step_no, n_cycle) * n_group + group_pos
        other_energy = jnp.sum(jnp.where(every_orbital == partner, occ_energy, 0.0))
        intersection = lax.dot_general(
            own_rows, other_rows, (((1,), (1,)), ((), ())), preferred_element_type=jnp.float32
        )
        denominator = own_energy + other_energy - vir_energy[:, None] - vir_energy[None, :]
        amplitude = intersection / denominator
        combined = (2.0 * amplitude - amplitude.T).astype(jnp.bfloat16)
        total = total + jnp.dot(combined, other_rows, preferred_element_type=jnp.float32)
    density = total.astype(jnp.bfloat16)
    aux_term = lax.dot_general(
        density, own_rows, (((0,), (0,)), ((), ())), preferred_element_type=jnp.float32
    )
    moved = lax.all_to_all(
        lax.all_to_all(density[None], "occ", split_axis=2, concat_axis=0, tiled=True),
        "grp",
        split_axis=1,
        concat_axis=0,
        tiled=True,
    )
    vir_local = moved.shape[1]
    aux_local = moved.shape[2]
    dens_rows = moved.reshape(n_group * n_cycle, vir_local * aux_local)
    int_rows = integrals.reshape(vir_local * aux_local, integrals.shape[2])
    lag_term = jnp.dot(dens_rows, int_rows, preferred_element_type=jnp.float32)
    n_orb = int_rows.shape[1]
    orb_block = n_orb // n_group
    n_aux = aux_term.shape[0]
    row_block = n_aux // n_cycle
    col_block = n_aux // n_group
    lag_parts = (
        lag_term.reshape(n_group, n_cycle, n_group, orb_block)
        .transpose(1, 2, 0, 3)
        .reshape(n_cycle * n_group, n_group, orb_block)
    )
    aux_parts = (
        aux_term.reshape(n_cycle, row_block, n_group, col_block)
        .transpose(0, 2, 1, 3)
        .reshape(n_cycle * n_group, row_block, col_block)
    )
    aux_sum, lag_sum = (
        lax.psum_scatter(aux_parts, ("occ", "grp"), scatter_dimension=0, tiled=True),
        lax.psum_scatter(lag_parts, ("occ", "grp"), scatter_dimension=0, tiled=True),
    )
    aux_metric = aux_sum.reshape(row_block, col_block)
    lagrangian = lag_sum.reshape(n_group, orb_block)
    return (aux_metric, lagrangian)


def solution(mesh):
    placed = (P(("occ", "grp"), None, None), P(), P(), P("grp", "occ", None), P())
    return jax.shard_map(
        local,
        mesh=mesh,
        in_specs=placed,
        out_specs=(P("occ", "grp"), P("occ", "grp")),
        check_vma=False,
    )
```

profile of v0, /device:TPU:1, one launch (start us, length us, event | category | flops | bytes accessed | tf_op | source)
XLA Modules:
  0.0 1873.0 jit_solution(11634753418466072335)
XLA Ops:
  7.2 2.2 collective-permute-start
  10.0 32.3 %collective-permute-done = bf16[1,512,768]{2,1,0:T(8,128)(2,1)S(1)} collective-permute-done((bf16[1,512,768]{2,1,0:T(8,128)(2,1)}, bf16[1,512,768]{2,1,0:T(8,128)(2,1)S(1)}, u32[]{:S(2)}, u32[]{:S(2)}) %collective-permute-start) | collective-permute-done | bytes 786464 | tf_op jit(solution)/shard_map/ppermute | solution.py:11
  42.3 1.2 broadcast_select_fusion
  43.5 0.1 collective-permute-start.1
  43.6 25.6 %collective-permute-done.1 = bf16[1,512,768]{2,1,0:T(8,128)(2,1)S(1)} collective-permute-done((bf16[1,512,768]{2,1,0:T(8,128)(2,1)S(1)}, bf16[1,512,768]{2,1,0:T(8,128)(2,1)S(1)}, u32[]{:S(2)}, u32[]{:S(2)}) %collective-permute-start.1) | collective-permute-done | bytes 786464 | tf_op jit(solution)/shard_map/ppermute | solution.py:11
  69.2 0.1 broadcast_select_fusion.1
  69.3 0.1 collective-permute-start.2
  69.4 22.0 %collective-permute-done.2 = bf16[1,512,768]{2,1,0:T(8,128)(2,1)S(1)} collective-permute-done((bf16[1,512,768]{2,1,0:T(8,128)(2,1)S(1)}, bf16[1,512,768]{2,1,0:T(8,128)(2,1)S(1)}, u32[]{:S(2)}, u32[]{:S(2)}) %collective-permute-start.2) | collective-permute-done | bytes 786464 | tf_op jit(solution)/shard_map/ppermute | solution.py:11
  91.4 0.1 broadcast_select_fusion.2
  91.5 0.1 collective-permute-start.3
  91.6 16.3 collective-permute-done.3
  107.8 0.1 broadcast_select_fusion.3
  107.9 0.0 copy-start.4
  107.9 0.0 copy-start.3
  107.9 0.0 copy-start
  107.9 0.1 collective-permute-start.4
  108.1 15.7 collective-permute-done.4
  123.7 0.1 broadcast_select_fusion.4
  123.8 0.1 collective-permute-start.5
  123.9 0.0 copy-done.4
  124.0 0.7 fusion.43
  128.5 0.0 copy-done.3
  128.5 0.0 copy-done
  128.5 0.6 fusion.13
  129.1 1.3 copy.34
  130.4 19.6 %collective-permute-done.5 = bf16[1,512,768]{2,1,0:T(8,128)(2,1)} collective-permute-done((bf16[1,512,768]{2,1,0:T(8,128)(2,1)S(1)}, bf16[1,512,768]{2,1,0:T(8,128)(2,1)}, u32[]{:S(2)}, u32[]{:S(2)}) %collective-permute-start.5) | collective-permute-done | bytes 786464 | tf_op jit(solution)/shard_map/ppermute | solution.py:11
  150.0 0.0 collective-permute-start.6
  150.0 3.2 fusion.21
  153.2 1.7 fusion.11
  155.0 0.3 copy.35
  155.3 3.1 fusion.18
  158.4 12.1 collective-permute-done.6
  170.5 1.7 fusion.9
  172.2 1.3 copy.36
  173.5 3.2 add_convert_fusion
  176.8 0.0 copy-start.1
  176.8 1.3 copy.38
  178.1 0.5 broadcast.32
  178.6 5.4 reduce
  184.1 0.3 reshape.45
  184.4 21.5 %all_to_all.33 = bf16[32,2,6144]{2,1,0:T(2,128)(2,1)S(1)} all-to-all(bf16[32,2,6144]{2,1,0:T(2,128)(2,1)S(1)} %reshape.45), channel_id=1, replica_groups=mesh['occ'=32,'grp'=8] {'occ'}, dimensions={0} | all-to-all | bytes 1572864 | tf_op jit(solution)/shard_map/all_to_all | solution.py:49
  205.9 0.7 reshape.46
  206.7 0.2 copy.45
  206.9 3.7 copy.39
  210.6 5.3 reshape.47
  215.9 82.9 %all-to-all-start.1 = ((bf16[8,2,24576]{2,1,0:T(2,128)(2,1)}), bf16[8,2,24576]{2,1,0:T(2,128)(2,1)S(1)}, u32[]{:S(2)}, u32[]{:S(2)}) async-start(bf16[8,2,24576]{2,1,0:T(2,128)(2,1)} %reshape.47), calls=%async_computation.1 | async-start | bytes 1572864 | tf_op jit(solution)/shard_map/all_to_all | solution.py:48
  298.8 0.0 all-reduce.4.cloned.1.call-start
  298.8 4.7 copy.41
  303.5 15.4 all-to-all-done.1
  318.9 3.0 reshape.48
  321.9 9.0 copy.40
  330.9 6.6 reshape.42
  337.4 2.9 convolution_bitcast_fusion
  340.3 1.6 copy.42
  341.9 0.0 all-reduce.4.cloned.1.call-update
  341.9 0.0 reduce-scatter.5.cloned.1.call-start
  342.0 0.3 copy.33
  342.3 0.8 copy-done.2
  343.0 0.3 copy.37
  343.3 2.7 fusion.47
  346.0 0.0 reduce-scatter.5.cloned.1.call-update
  346.0 249.0 %all-reduce.4.cloned.1.call-done = f32[256,8,128]{2,1,0:T(8,128)} async-done(((f32[256,8,128]{2,1,0:T(8,128)}), f32[256,8,128]{2,1,0:T(8,128)}) %all-reduce.4.cloned.1.call-update) | async-done | bytes 1048592
  595.1 1.3 dynamic-slice_bitcast_fusion
  596.4 1269.8 %reduce-scatter.5.cloned.1.call-done = f32[1,24,96]{2,1,0:T(8,128)} async-done(((f32[256,24,96]{2,1,0:T(8,128)}), f32[1,24,96]{2,1,0:T(8,128)}) %reduce-scatter.5.cloned.1.call-update) | async-done | bytes 9232
  (3 shorter events, 0.0 us)
Async XLA Ops:
  7.2 35.1 %collective-permute-start = (bf16[1,512,768]{2,1,0:T(8,128)(2,1)}, bf16[1,512,768]{2,1,0:T(8,128)(2,1)S(1)}, u32[]{:S(2)}, u32[]{:S(2)}) collective-permute-start(bf16[1,512,768]{2,1,0:T(8,128)(2,1)} %param.5), channel_id=1, source_target_pairs={{0,8},{8,16},{16,24},{24,32},{32,40},{40,48},{48,56},{56,64},{64,7... | collective-permute-start | bytes 2359304 | tf_op jit(solution)/shard_map/ppermute | solution.py:11
  43.5 25.7 %collective-permute-start.1 = (bf16[1,512,768]{2,1,0:T(8,128)(2,1)S(1)}, bf16[1,512,768]{2,1,0:T(8,128)(2,1)S(1)}, u32[]{:S(2)}, u32[]{:S(2)}) collective-permute-start(bf16[1,512,768]{2,1,0:T(8,128)(2,1)S(1)} %broadcast_select_fusion), channel_id=1, source_target_pairs={{0,16},{8,24},{16,32},{24,40},{32,48},{40,56},{48,64},{56,72},{64,... | collective-permute-start | bytes 2359304 | tf_op jit(solution)/shard_map/ppermute | solution.py:11
  69.3 22.1 %collective-permute-start.2 = (bf16[1,512,768]{2,1,0:T(8,128)(2,1)S(1)}, bf16[1,512,768]{2,1,0:T(8,128)(2,1)S(1)}, u32[]{:S(2)}, u32[]{:S(2)}) collective-permute-start(bf16[1,512,768]{2,1,0:T(8,128)(2,1)S(1)} %broadcast_select_fusion.1), channel_id=1, source_target_pairs={{0,32},{8,40},{16,48},{24,56},{32,64},{40,72},{48,80},{56,88},{64,... | collective-permute-start | bytes 2359304 | tf_op jit(solution)/shard_map/ppermute | solution.py:11
  91.5 16.3 collective-permute-start.3
  107.9 16.0 copy-start.4
  107.9 20.5 %copy-start.3 = (f32[512]{0:T(512)S(1)}, f32[512]{0:T(512)}, u32[]{:S(2)}) copy-start(f32[512]{0:T(512)} %param.7) | copy-start | bytes 6148
  107.9 20.6 %copy-start = (bf16[1,512,768]{2,1,0:T(8,128)(2,1)S(1)}, bf16[1,512,768]{2,1,0:T(8,128)(2,1)}, u32[]{:S(2)}) copy-start(bf16[1,512,768]{2,1,0:T(8,128)(2,1)} %param.5) | copy-start | bytes 2359300
  107.9 15.8 collective-permute-start.4
  123.8 26.2 %collective-permute-start.5 = (bf16[1,512,768]{2,1,0:T(8,128)(2,1)S(1)}, bf16[1,512,768]{2,1,0:T(8,128)(2,1)}, u32[]{:S(2)}, u32[]{:S(2)}) collective-permute-start(bf16[1,512,768]{2,1,0:T(8,128)(2,1)S(1)} %broadcast_select_fusion.4), channel_id=1, source_target_pairs={{0,8},{8,16},{16,24},{24,32},{32,40},{40,48},{48,56},{56,64},{64,7... | collective-permute-start | bytes 2359304 | tf_op jit(solution)/shard_map/ppermute | solution.py:11
  150.0 20.4 %collective-permute-start.6 = (bf16[1,512,768]{2,1,0:T(8,128)(2,1)}, bf16[1,512,768]{2,1,0:T(8,128)(2,1)}, u32[]{:S(2)}, u32[]{:S(2)}) collective-permute-start(bf16[1,512,768]{2,1,0:T(8,128)(2,1)} %collective-permute-done.5), channel_id=1, source_target_pairs={{0,8},{8,16},{16,24},{24,32},{32,40},{40,48},{48,56},{56,64},{64,7... | collective-permute-start | bytes 2359304 | tf_op jit(solution)/shard_map/ppermute | solution.py:11
  176.8 1.3 copy-start.1
  215.9 103.0 %all-to-all-start.1 = ((bf16[8,2,24576]{2,1,0:T(2,128)(2,1)}), bf16[8,2,24576]{2,1,0:T(2,128)(2,1)S(1)}, u32[]{:S(2)}, u32[]{:S(2)}) async-start(bf16[8,2,24576]{2,1,0:T(2,128)(2,1)} %reshape.47), calls=%async_computation.1 | async-start | bytes 1572864 | tf_op jit(solution)/shard_map/all_to_all | solution.py:48
  298.8 296.3 %all-reduce.4.cloned.1.call-start = ((), (), s32[]{:S(2)}) async-start(), calls=%async_computation.3 | async-start | bytes 2097152
  341.9 1.1 copy-start.2
  341.9 1524.2 %reduce-scatter.5.cloned.1.call-start = ((), (), s32[]{:S(2)}) async-start(), calls=%async_computation.4 | async-start | bytes 3158016
Sparse Core Ops, SparseCore 0:
  342.1 252.9 all-reduce.3
  598.3 1267.8 reduce-scatter.4
where the time goes:
time: 1880 us; the launch traced here: 1870 us
  waiting for transfers between devices  1680 us (89%)
  starting transfers between devices  85.6 us (5%)
  local copies, waits for them, and re-layouts  42.4 us (2%)
  blocking collectives  21.5 us (1%)
  matrix products  19.1 us (1%)
  between operations  18.8 us (1%)
    unnamed x4, waiting for transfers between devices  1520 us
    ppermute x7, waiting for transfers between devices, shifted(): return lax.ppermute(x, axis, [(i, (i + by) % size) for i in range(size)])  144 us
    all_to_all x1, starting transfers between devices, local(): lax.all_to_all(lax.all_to_all(density[None], 'occ', split_axis=2, concat_...  82.9 us
  transfers between devices with their start and end apart: 10, of which 10 were waited for; matrix products, arithmetic and copies ran while one was open for 1% of the time, Pallas kernels for 0%

commit v1 on v0

v1 whole, which is shorter than its diff:
```python
import jax
import jax.numpy as jnp
from jax import lax
from jax.sharding import Mesh, PartitionSpec as P

BF16 = jnp.bfloat16
F32 = jnp.float32


def exchange_all(x, axes):
    return lax.all_to_all(x, axes, split_axis=0, concat_axis=0, tiled=True)


def swap_cores(x):
    return lax.ppermute(x, "core", [(0, 1), (1, 0)])


def local(b_factors, occ_energy, vir_energy, integrals, window_start):
    n_cyc = lax.axis_size("occ")
    n_zl = lax.axis_size("zl")
    cyc = lax.axis_index("occ")
    core = lax.axis_index("core")
    grp = lax.axis_index("zl") * 2 + core
    n_grp = n_zl * 2
    own = b_factors[0]
    n_vir, n_aux = own.shape
    shift = jnp.mod(window_start[0] + 1, n_cyc)

    ring = [(i, (i + 1) % n_cyc) for i in range(n_cyc)]
    prev_rows = lax.ppermute(own, "occ", ring)
    next_rows = lax.ppermute(own, "occ", [(b, a) for a, b in ring])

    ints = jnp.transpose(integrals, (1, 0, 2))
    other_ints = swap_cores(ints)
    first = jnp.where(core == 0, ints, other_ints)
    second = jnp.where(core == 0, other_ints, ints)
    chip_ints = jnp.concatenate([first, second], axis=1)

    spread = exchange_all(own.reshape(n_cyc, n_vir // n_cyc, n_aux), "occ")
    turned = lax.dynamic_slice_in_dim(jnp.concatenate([spread, spread], axis=0), shift, n_cyc, axis=0)
    rows_i = exchange_all(turned, "occ").reshape(n_vir, n_aux)

    i_cyc = jnp.mod(cyc + shift, n_cyc)
    energy_i = occ_energy[i_cyc * n_grp + grp]
    vir_sum = vir_energy[:, None] + vir_energy[None, :]

    total = jnp.zeros((n_aux, n_vir), F32)
    for delta, rows_j in ((0, own), (1, next_rows), (-1, prev_rows)):
        energy_j = occ_energy[jnp.mod(cyc + delta, n_cyc) * n_grp + grp]
        inter = lax.dot_general(rows_i, rows_j, (((1,), (1,)), ((), ())), preferred_element_type=F32)
        inter_t = lax.dot_general(rows_j, rows_i, (((1,), (1,)), ((), ())), preferred_element_type=F32)
        combined_t = ((2.0 * inter_t - inter) / (energy_i + energy_j - vir_sum)).astype(BF16)
        total = total + lax.dot_general(
            rows_j, combined_t, (((0,), (0,)), ((), ())), preferred_element_type=F32
        )
    density_t = total.astype(BF16)

    aux_blk = n_aux // n_cyc
    chip_vir = n_vir // n_zl
    moved = exchange_all(
        density_t.reshape(n_cyc, aux_blk, n_zl, chip_vir).transpose(0, 2, 1, 3).reshape(n_cyc * n_zl, aux_blk, chip_vir),
        ("occ", "zl"),
    )

    col_blk = n_aux // n_grp
    cols = rows_i.reshape(n_vir, n_zl, 2, col_blk)
    even = jnp.pad(cols[:, :, 0], ((0, 0), (0, 0), (0, 128 - col_blk))).reshape(n_vir, n_zl * 128)
    odd = jnp.pad(cols[:, :, 1], ((0, 0), (0, 0), (0, 128 - col_blk))).reshape(n_vir, n_zl * 128)
    keep_cols = jnp.where(core == 0, even, odd)
    send_cols = jnp.where(core == 0, odd, even)
    aux_send = jnp.dot(density_t, send_cols, preferred_element_type=F32).astype(BF16)
    aux_keep = jnp.dot(density_t, keep_cols, preferred_element_type=F32)
    aux_chip = (aux_keep + swap_cores(aux_send).astype(F32)).astype(BF16)
    aux_parts = aux_chip.reshape(n_cyc, aux_blk, n_zl, 128).transpose(0, 2, 1, 3)

    lag = lax.dot_general(moved, chip_ints, (((1, 2), (0, 1)), ((), ())), preferred_element_type=F32).astype(BF16)
    orb_blk = lag.shape[1] // n_grp
    lag = lag.reshape(n_cyc, n_zl, n_zl, 2, orb_blk).transpose(0, 2, 1, 3, 4)
    lag_keep = jnp.where(core == 0, lag[:, :, :, 0], lag[:, :, :, 1])
    lag_send = jnp.where(core == 0, lag[:, :, :, 1], lag[:, :, :, 0])
    lag_parts = jnp.concatenate([lag_keep, swap_cores(lag_send)], axis=2)
    lag_parts = lax.dynamic_slice_in_dim(
        jnp.concatenate([lag_parts, lag_parts], axis=0), jnp.mod(-shift, n_cyc), n_cyc, axis=0
    )

    parts = jnp.concatenate([lag_parts, aux_parts], axis=2).reshape(n_cyc * n_zl, 2 * n_zl + aux_blk, 128)
    sums = jnp.sum(exchange_all(parts, ("occ", "zl")).astype(F32), axis=0)
    aux_metric = sums[2 * n_zl :, :col_blk]
    same, cross = sums[:n_zl], sums[n_zl : 2 * n_zl]
    low = jnp.where(core == 0, same, cross)
    high = jnp.where(core == 0, cross, same)
    lagrangian = jnp.stack([low, high], axis=1).reshape(2 * n_zl, orb_blk)
    return (aux_metric, lagrangian)


def solution(mesh):
    n_occ, n_grp = mesh.shape["occ"], mesh.shape["grp"]
    fine = Mesh(mesh.devices.reshape(n_occ, n_grp // 2, 2), ("occ", "zl", "core"))
    grp = ("zl", "core")
    placed = (P(("occ", "zl", "core"), None, None), P(), P(), P(grp, "occ", None), P())
    return jax.shard_map(
        local,
        mesh=fine,
        in_specs=placed,
        out_specs=(P("occ", grp), P("occ", grp)),
        check_vma=False,
    )
```

time: 1880 us -> 195 us (0.10)
  waiting for transfers between devices: 1680 us -> 26.8 us
  local copies, waits for them, and re-layouts: 42.4 us -> 21.6 us
    unnamed x4 -> x0, waiting for transfers between devices: 1520 us -> none
    ppermute x7 -> x5, waiting for transfers between devices: 144 us -> 4.15 us  [the longest x1 4.09 us: local(): next_rows = lax.ppermute(own, 'occ', [(b, a) for a, b in ring])]
    all_to_all x1 -> x3, starting transfers between devices: 82.9 us -> 51.9 us  [exchange_all(): return lax.all_to_all(x, axes, split_axis=0, concat_axis=0, tiled=True)]
    ppermute x7 -> x5, starting transfers between devices: 2.63 us -> 22.3 us  [the longest x3 12.7 us: swap_cores(): return lax.ppermute(x, 'core', [(0, 1), (1, 0)])]
  transfers between devices with their start and end apart: 10 -> 8, of which waited for: 10 -> 4; matrix products, arithmetic and copies ran while one was open for 1% -> 25% of each run, Pallas kernels for 0% -> 0%
where the time goes in v1:
time: 195 us; the launch traced here: 194 us
  starting transfers between devices  74.3 us (38%)
  blocking collectives  36.1 us (19%)
  waiting for transfers between devices  26.8 us (14%)
  local copies, waits for them, and re-layouts  21.6 us (11%)
  matrix products  19 us (10%)
  other arithmetic  11.1 us (6%)
  between operations  5.35 us (3%)
    all_to_all x3, starting transfers between devices, exchange_all(): return lax.all_to_all(x, axes, split_axis=0, concat_axis=0, tiled=True)  51.9 us
    all_to_all x1, blocking collectives, exchange_all(): return lax.all_to_all(x, axes, split_axis=0, concat_axis=0, tiled=True)  36.1 us
    all_to_all x3, waiting for transfers between devices, exchange_all(): return lax.all_to_all(x, axes, split_axis=0, concat_axis=0, tiled=True)  22.7 us
    ppermute x3, starting transfers between devices, swap_cores(): return lax.ppermute(x, 'core', [(0, 1), (1, 0)])  12.7 us
    select_n x1, other arithmetic, local(): first = jnp.where(core == 0, ints, other_ints)  8.99 us
    ppermute x1, starting transfers between devices, local(): next_rows = lax.ppermute(own, 'occ', [(b, a) for a, b in ring])  8.36 us
    dot_general x3, matrix products, local(): lax.dot_general(rows_j, combined_t, (((0,), (0,)), ((), ())), preferred_e...  6.55 us
    dot_general x3, matrix products, local(): lax.dot_general(rows_j, rows_i, (((1,), (1,)), ((), ())), preferred_eleme...  6.27 us
  transfers between devices with their start and end apart: 8, of which 4 were waited for; matrix products, arithmetic and copies ran while one was open for 25% of the time, Pallas kernels for 0%

profile of v1, /device:TPU:1, one launch (start us, length us, event | category | flops | bytes accessed | tf_op | source)
XLA Modules:
  0.0 194.3 jit_solution(8539202901979110044)
XLA Ops:
  0.6 14.5 %all-to-all-start = ((bf16[32,16,768]{2,1,0:T(8,128)(2,1)}), bf16[32,16,768]{2,1,0:T(8,128)(2,1)S(1)}, u32[]{:S(2)}, u32[]{:S(2)}) async-start(bf16[32,16,768]{2,1,0:T(8,128)(2,1)} %bitcast), calls=%async_computation | async-start | bytes 1572864 | tf_op jit(solution)/shard_map/all_to_all | solution.py:11
  15.8 17.2 %all-to-all-done = bf16[32,16,768]{2,1,0:T(8,128)(2,1)S(1)} async-done(((bf16[32,16,768]{2,1,0:T(8,128)(2,1)}), bf16[32,16,768]{2,1,0:T(8,128)(2,1)S(1)}, u32[]{:S(2)}, u32[]{:S(2)}) %all-to-all-start) | async-done | bytes 786464 | tf_op jit(solution)/shard_map/all_to_all | solution.py:11
  33.0 1.2 fusion.16
  34.2 4.3 %all-to-all-start.1 = ((bf16[32,16,768]{2,1,0:T(8,128)(2,1)}), bf16[32,16,768]{2,1,0:T(8,128)(2,1)S(1)}, u32[]{:S(2)}, u32[]{:S(2)}) async-start(bf16[32,16,768]{2,1,0:T(8,128)(2,1)} %fusion.16), calls=%async_computation.1 | async-start | bytes 1572864 | tf_op jit(solution)/shard_map/all_to_all | solution.py:11
  38.5 0.0 copy-start.5
  38.5 1.3 collective-permute-start.1
  39.8 8.4 %collective-permute-start = (bf16[512,768]{1,0:T(8,128)(2,1)}, bf16[512,768]{1,0:T(8,128)(2,1)}, u32[]{:S(2)}, u32[]{:S(2)}) collective-permute-start(bf16[512,768]{1,0:T(8,128)(2,1)} %bitcast.3), channel_id=1, source_target_pairs={{8,0},{16,8},{24,16},{32,24},{40,32},{48,40},{56,48},{64,56},{72,6... | collective-permute-start | bytes 2359304 | tf_op jit(solution)/shard_map/ppermute | solution.py:31
  48.2 5.3 %copy.76 = bf16[64,24,1024]{2,0,1:T(8,128)(2,1)} copy(bf16[64,24,1024]{2,1,0:T(8,128)(2,1)} %param.8) | data formatting | bytes 6291456 | tf_op args[3]
  53.5 9.0 %collective-permute-start.2 = (bf16[24,64,1024]{2,1,0:T(8,128)(2,1)}, bf16[24,64,1024]{2,1,0:T(8,128)(2,1)}, u32[]{:S(2)}, u32[]{:S(2)}) collective-permute-start(bf16[24,64,1024]{2,1,0:T(8,128)(2,1)} %bitcast.68), channel_id=1, source_target_pairs={{0,1},{1,0},{2,3},{3,2},{4,5},{5,4},{6,7},{7,6},{8,9},{9,8},{10,11... | collective-permute-start | bytes 9437192 | tf_op jit(solution)/shard_map/ppermute | solution.py:15
  62.5 0.0 copy-done.5
  62.5 0.6 fusion.46
  66.9 0.0 all-to-all-done.1
  66.9 1.7 fusion.40
  68.7 1.4 copy.54
  70.1 0.0 collective-permute-done.1
  70.1 1.7 fusion.48
  71.8 0.0 copy-start.6
  71.8 1.3 copy.56
  73.1 4.1 %collective-permute-done = bf16[512,768]{1,0:T(8,128)(2,1)} collective-permute-done((bf16[512,768]{1,0:T(8,128)(2,1)}, bf16[512,768]{1,0:T(8,128)(2,1)}, u32[]{:S(2)}, u32[]{:S(2)}) %collective-permute-start) | collective-permute-done | bytes 786464 | tf_op jit(solution)/shard_map/ppermute | solution.py:31
  77.2 2.8 %fusion.47 = f32[512,512]{1,0:T(8,128)} fusion(bf16[512,768]{1,0:T(8,128)(2,1)S(1)} %bitcast.73, bf16[512,768]{1,0:T(8,128)(2,1)} %collective-permute-done), kind=kOutput, calls=%fused_computation.69 | convolution fusion | flops 402653184 | bytes 2621440 | tf_op jit(solution)/shard_map/dot_general | solution.py:51
  80.0 2.6 %copy.55 = f32[512,512]{0,1:T(8,128)} copy(f32[512,512]{1,0:T(8,128)} %fusion.47) | data formatting | bytes 2097152 | tf_op jit(solution)/shard_map/dot_general | solution.py:51
  82.6 0.0 copy-done.6
  82.6 0.0 copy-start
  82.6 0.0 copy-start.2
  82.6 2.4 %fusion.21 = f32[512,768]{1,0:T(8,128)S(1)} fusion(f32[512,512]{1,0:T(8,128)S(1)} %fusion.40, f32[512,512]{0,1:T(8,128)} %copy.54, f32[512]{0:T(512)S(1)} %copy-done.6, f32[]{:T(128)} %bitcast.5, bf16[1,512,768]{2,1,0:T(8,128)(2,1)} %param.5), kind=kOutput, calls=%fused_computation.34 | convolution fusion | flops 404226048 | bytes 4458500 | tf_op jit(solution)/shard_map/dot_general | solution.py:53
  85.0 0.0 copy-done
  85.1 0.0 copy-done.2
  85.1 0.0 copy-start.1
  85.1 2.1 %fusion.19 = f32[512,768]{1,0:T(8,128)S(1)} fusion(bf16[512,768]{1,0:T(8,128)(2,1)} %collective-permute-done, f32[512,512]{1,0:T(8,128)S(1)} %copy-done, f32[512,512]{0,1:T(8,128)S(1)} %copy-done.2, f32[]{:T(128)} %bitcast.7, f32[512]{0:T(512)S(1)} %copy-done.6), kind=kOutput, calls=%fused_computation.33 | convolution fusion | flops 404226048 | bytes 4458500 | tf_op jit(solution)/shard_map/dot_general | solution.py:53
  87.1 0.0 copy-done.1
  87.2 2.0 %add_convert_fusion.1 = bf16[512,768]{1,0:T(8,128)(2,1)S(1)} fusion(f32[512,768]{1,0:T(8,128)S(1)} %fusion.21, f32[512,768]{1,0:T(8,128)S(1)} %fusion.19, bf16[512,768]{1,0:T(8,128)(2,1)} %collective-permute-done.1, f32[512,512]{1,0:T(8,128)S(1)} %fusion.48, f32[512,512]{0,1:T(8,128)S(1)} %copy-done.1, f32[]{:T(128)} %bitcast.9, f32[512]{0:T(512)S(1)} %copy-done.6), kind=kOutput, calls=%fused_computation.14 | convolution fusion | flops 405405696 | bytes 6817796 | tf_op jit(solution)/shard_map/dot_general | solution.py:53
  89.2 0.0 copy-start.3
  89.2 0.3 copy.57
  89.5 0.2 reshape.43
  89.7 1.0 copy.58
  90.7 0.0 copy-done.3
  90.7 33.1 %all-to-all-start.2 = ((bf16[128,24,128]{2,1,0:T(8,128)(2,1)}), bf16[128,24,128]{2,1,0:T(8,128)(2,1)}, u32[]{:S(2)}, u32[]{:S(2)}) async-start(bf16[128,24,128]{2,1,0:T(8,128)(2,1)} %bitcast.12), calls=%async_computation.2 | async-start | bytes 1572864 | tf_op jit(solution)/shard_map/all_to_all | solution.py:11
  123.8 1.1 reshape_reshape.3
  124.9 2.3 %fusion.45 = (bf16[512,4,1,96]{3,2,1,0:T(2,128)(2,1)}, bf16[512,4,1,96]{3,2,1,0:T(2,128)(2,1)S(1)}) fusion(bf16[512,4,2,96]{3,2,1,0:T(2,128)(2,1)S(1)} %reshape_reshape.3), kind=kLoop, calls=%fused_computation.67 | loop fusion | bytes 1572864 | tf_op jit(solution)/shard_map/slice | solution.py:67
  127.2 2.4 %copy.62 = bf16[512,4,1,96]{0,3,2,1:T(8,128)(2,1)S(1)} copy(bf16[512,4,1,96]{3,2,1,0:T(2,128)(2,1)} %get-tuple-element.4) | data formatting | bytes 786432 | tf_op jit(solution)/shard_map/slice | solution.py:67
  129.6 1.3 copy.63
  130.9 0.2 pad_select_fusion
  131.1 0.0 copy-done.4
  131.1 1.5 convolution_convert_fusion
  132.5 0.8 collective-permute-start.4
  133.4 0.0 collective-permute-done.2
  133.4 9.0 %broadcast_select_fusion.1 = (bf16[24,64,1024]{2,1,0:T(8,128)(2,1)}, bf16[24,64,1024]{2,1,0:T(8,128)(2,1)}) fusion(bf16[24,64,1024]{2,1,0:T(8,128)(2,1)} %collective-permute-done.2, pred[]{:T(512)S(6)} %eq.9, bf16[64,24,1024]{2,1,0:T(8,128)(2,1)} %param.8), kind=kLoop, calls=%fused_computation.6 | loop fusion | flops 3145728 | bytes 12582913 | tf_op jit(solution)/shard_map/jit(_where)/select_n | solution.py:35
  142.4 5.5 %all-to-all-done.2 = bf16[128,24,128]{2,1,0:T(8,128)(2,1)} async-done(((bf16[128,24,128]{2,1,0:T(8,128)(2,1)}), bf16[128,24,128]{2,1,0:T(8,128)(2,1)}, u32[]{:S(2)}, u32[]{:S(2)}) %all-to-all-start.2) | async-done | bytes 786464 | tf_op jit(solution)/shard_map/all_to_all | solution.py:11
  147.8 4.1 %fusion.7 = bf16[128,1024]{1,0:T(8,128)(2,1)S(1)} fusion(bf16[24,64,1024]{2,1,0:T(8,128)(2,1)} %get-tuple-element.3, bf16[24,64,1024]{2,1,0:T(8,128)(2,1)} %get-tuple-element.2, bf16[128,24,128]{2,1,0:T(8,128)(2,1)} %all-to-all-done.2), kind=kOutput, calls=%fused_computation.17 | convolution fusion | flops 818020352 | bytes 7340032 | tf_op jit(solution)/shard_map/dot_general | solution.py:76
  151.9 0.2 reshape.45
  152.1 0.1 copy.78
  152.2 2.9 %collective-permute-start.3 = (bf16[32,4,4,128]{3,0,2,1:T(8,128)(2,1)S(1)}, bf16[32,4,4,128]{3,0,2,1:T(8,128)(2,1)S(1)}, u32[]{:S(2)}, u32[]{:S(2)}) collective-permute-start(bf16[32,4,4,128]{3,0,2,1:T(8,128)(2,1)S(1)} %get-tuple-element.8), channel_id=1, source_target_pairs={{0,1},{1,0},{2,3},{3,2},{4,5},{5,4},{6,7},{7,6},{8,9},{9,8},{10,11... | collective-permute-start | bytes 393224 | tf_op jit(solution)/shard_map/ppermute | solution.py:15
  155.1 0.0 collective-permute-done.4
  155.1 0.6 add_convert_fusion
  155.7 0.2 reshape.46
  155.9 0.1 copy.77
  156.0 0.1 collective-permute-done.3
  156.1 0.3 fusion.36
  156.4 0.1 copy.65
  156.5 0.2 pad_maximum_fusion
  156.7 36.1 %all_to_all.20 = bf16[128,32,128]{2,1,0:T(8,128)(2,1)S(1)} all-to-all(bf16[128,32,128]{2,1,0:T(8,128)(2,1)S(1)} %bitcast.74), channel_id=1, replica_groups=mesh['occ'=32,'zl'=4,'core'=2] {'occ','zl'}, dimensions={0} | all-to-all | bytes 2097152 | tf_op jit(solution)/shard_map/all_to_all | solution.py:11
  192.9 0.2 convert_reduce_fusion
  193.1 0.6 slice.34
  193.7 0.6 copy.66
  (4 shorter events, 0.0 us)
Async XLA Ops:
  0.6 32.4 %all-to-all-start = ((bf16[32,16,768]{2,1,0:T(8,128)(2,1)}), bf16[32,16,768]{2,1,0:T(8,128)(2,1)S(1)}, u32[]{:S(2)}, u32[]{:S(2)}) async-start(bf16[32,16,768]{2,1,0:T(8,128)(2,1)} %bitcast), calls=%async_computation | async-start | bytes 1572864 | tf_op jit(solution)/shard_map/all_to_all | solution.py:11
  34.2 32.7 %all-to-all-start.1 = ((bf16[32,16,768]{2,1,0:T(8,128)(2,1)}), bf16[32,16,768]{2,1,0:T(8,128)(2,1)S(1)}, u32[]{:S(2)}, u32[]{:S(2)}) async-start(bf16[32,16,768]{2,1,0:T(8,128)(2,1)} %fusion.16), calls=%async_computation.1 | async-start | bytes 1572864 | tf_op jit(solution)/shard_map/all_to_all | solution.py:11
  38.5 24.0 %copy-start.5 = (f32[256]{0:T(256)S(1)}, f32[256]{0:T(256)}, u32[]{:S(2)}) copy-start(f32[256]{0:T(256)} %param.6) | copy-start | bytes 3076
  38.5 31.5 %collective-permute-start.1 = (bf16[512,768]{1,0:T(8,128)(2,1)}, bf16[512,768]{1,0:T(8,128)(2,1)}, u32[]{:S(2)}, u32[]{:S(2)}) collective-permute-start(bf16[512,768]{1,0:T(8,128)(2,1)} %bitcast.3), channel_id=1, source_target_pairs={{0,8},{8,16},{16,24},{24,32},{32,40},{40,48},{48,56},{56,64},{64,7... | collective-permute-start | bytes 2359304 | tf_op jit(solution)/shard_map/ppermute | solution.py:30
  39.8 37.4 %collective-permute-start = (bf16[512,768]{1,0:T(8,128)(2,1)}, bf16[512,768]{1,0:T(8,128)(2,1)}, u32[]{:S(2)}, u32[]{:S(2)}) collective-permute-start(bf16[512,768]{1,0:T(8,128)(2,1)} %bitcast.3), channel_id=1, source_target_pairs={{8,0},{16,8},{24,16},{32,24},{40,32},{48,40},{56,48},{64,56},{72,6... | collective-permute-start | bytes 2359304 | tf_op jit(solution)/shard_map/ppermute | solution.py:31
  53.5 79.9 %collective-permute-start.2 = (bf16[24,64,1024]{2,1,0:T(8,128)(2,1)}, bf16[24,64,1024]{2,1,0:T(8,128)(2,1)}, u32[]{:S(2)}, u32[]{:S(2)}) collective-permute-start(bf16[24,64,1024]{2,1,0:T(8,128)(2,1)} %bitcast.68), channel_id=1, source_target_pairs={{0,1},{1,0},{2,3},{3,2},{4,5},{5,4},{6,7},{7,6},{8,9},{9,8},{10,11... | collective-permute-start | bytes 9437192 | tf_op jit(solution)/shard_map/ppermute | solution.py:15
  71.8 10.8 %copy-start.6 = (f32[512]{0:T(512)S(1)}, f32[512]{0:T(512)}, u32[]{:S(2)}) copy-start(f32[512]{0:T(512)} %param.7) | copy-start | bytes 6148
  82.6 2.4 %copy-start = (f32[512,512]{1,0:T(8,128)S(1)}, f32[512,512]{1,0:T(8,128)}, u32[]{:S(2)}) copy-start(f32[512,512]{1,0:T(8,128)} %fusion.47) | copy-start | bytes 3145732
  82.6 2.5 %copy-start.2 = (f32[512,512]{0,1:T(8,128)S(1)}, f32[512,512]{0,1:T(8,128)}, u32[]{:S(2)}) copy-start(f32[512,512]{0,1:T(8,128)} %copy.55) | copy-start | bytes 3145732
  85.1 2.1 %copy-start.1 = (f32[512,512]{0,1:T(8,128)S(1)}, f32[512,512]{0,1:T(8,128)}, u32[]{:S(2)}) copy-start(f32[512,512]{0,1:T(8,128)} %copy.56) | copy-start | bytes 3145732
  89.2 1.5 copy-start.3
  90.7 57.2 %all-to-all-start.2 = ((bf16[128,24,128]{2,1,0:T(8,128)(2,1)}), bf16[128,24,128]{2,1,0:T(8,128)(2,1)}, u32[]{:S(2)}, u32[]{:S(2)}) async-start(bf16[128,24,128]{2,1,0:T(8,128)(2,1)} %bitcast.12), calls=%async_computation.2 | async-start | bytes 1572864 | tf_op jit(solution)/shard_map/all_to_all | solution.py:11
  127.2 3.8 %copy-start.4 = (bf16[512,768]{1,0:T(8,128)(2,1)S(1)}, bf16[512,768]{1,0:T(8,128)(2,1)}, u32[]{:S(2)}) copy-start(bf16[512,768]{1,0:T(8,128)(2,1)} %copy-done.3) | copy-start | bytes 2359300
  132.5 22.6 %collective-permute-start.4 = (bf16[768,512]{1,0:T(8,128)(2,1)}, bf16[768,512]{1,0:T(8,128)(2,1)S(1)}, u32[]{:S(2)}, u32[]{:S(2)}) collective-permute-start(bf16[768,512]{1,0:T(8,128)(2,1)} %convolution_convert_fusion), channel_id=1, source_target_pairs={{0,1},{1,0},{2,3},{3,2},{4,5},{5,4},{6,7},{7,6},{8,9},{9,8},{10,11... | collective-permute-start | bytes 2359304 | tf_op jit(solution)/shard_map/ppermute | solution.py:15
  152.2 3.8 %collective-permute-start.3 = (bf16[32,4,4,128]{3,0,2,1:T(8,128)(2,1)S(1)}, bf16[32,4,4,128]{3,0,2,1:T(8,128)(2,1)S(1)}, u32[]{:S(2)}, u32[]{:S(2)}) collective-permute-start(bf16[32,4,4,128]{3,0,2,1:T(8,128)(2,1)S(1)} %get-tuple-element.8), channel_id=1, source_target_pairs={{0,1},{1,0},{2,3},{3,2},{4,5},{5,4},{6,7},{7,6},{8,9},{9,8},{10,11... | collective-permute-start | bytes 393224 | tf_op jit(solution)/shard_map/ppermute | solution.py:15

commit v2 on v1

v2 whole, which is shorter than its diff:
```python
import jax
import jax.numpy as jnp
from jax import lax
from jax.experimental import pallas as pl
from jax.experimental.pallas import tpu as pltpu
from jax.sharding import Mesh, PartitionSpec as P

BF16 = jnp.bfloat16
F32 = jnp.float32
LANES = 128
VMEM_BYTES = 40 * 1024 * 1024
CYC = ("oh", "yl")
DEST = ("oh", "zl")

vmem = pl.BlockSpec(memory_space=pltpu.VMEM)
smem = pl.BlockSpec(memory_space=pltpu.SMEM)


def exchange_all(x, axes):
    return lax.all_to_all(x, axes, split_axis=0, concat_axis=0, tiled=True)


def swap_cores(x):
    return lax.ppermute(x, "core", [(0, 1), (1, 0)])


def swap_yl(x):
    return lax.ppermute(x, "yl", [(0, 1), (1, 0)])


def swap_both(x):
    return lax.ppermute(x, ("yl", "core"), [(i, 3 - i) for i in range(4)])


def dot(a, b, ca, cb):
    return lax.dot_general(a, b, (((ca,), (cb,)), ((), ())), preferred_element_type=F32)


def call(kernel, outs, scratch, flops, nbytes, *args, specs):
    return pl.pallas_call(
        kernel,
        out_shape=outs,
        in_specs=specs,
        out_specs=jax.tree.map(lambda _: vmem, outs),
        scratch_shapes=scratch,
        compiler_params=pltpu.CompilerParams(vmem_limit_bytes=VMEM_BYTES),
        cost_estimate=pl.CostEstimate(flops=flops, bytes_accessed=nbytes, transcendentals=0),
    )(*args)


def pair_kernel(energy, vir_row, vir_col, rows_i, own, nxt, prv, out):
    n_cyc, n_h, aux_blk, lanes = out.shape
    n_vir, n_aux = rows_i.shape
    blk = 2 * lanes

    def body(step, carry):
        start = pl.multiple_of(step * blk, blk)
        block_i = rows_i[pl.ds(start, blk), :]
        vir_sum = vir_col[pl.ds(start, blk), :] + vir_row[...]
        total = jnp.zeros((blk, n_aux), F32)
        for t, rows_j in enumerate((own, nxt, prv)):
            inter = dot(block_i, rows_j[...], 1, 1)
            inter_t = dot(rows_j[pl.ds(start, blk), :], rows_i[...], 1, 1)
            combined = ((2.0 * inter - inter_t) / (energy[t] - vir_sum)).astype(BF16)
            total = total + dot(combined, rows_j[...], 1, 0)
        for half in range(2):
            turned = jnp.transpose(total[half * lanes : (half + 1) * lanes])
            out[:, step * 2 + half] = turned.reshape(n_cyc, aux_blk, lanes).astype(BF16)
        return carry

    lax.fori_loop(0, n_h // 2, body, 0)


def aux_kernel(place, dens, rows_i, keep, send, acc):
    n_cyc, n_h, aux_blk, lanes = dens.shape
    n_vir, n_aux = rows_i.shape
    n_grp = 2 * n_h
    col_blk = n_aux // n_grp
    yl, core = place[1], place[2]
    pad = jnp.zeros((lanes, lanes - col_blk), BF16)
    for h in range(n_h):
        block = rows_i[h * lanes : (h + 1) * lanes, :]
        pieces = []
        for g in range(n_grp):
            pieces += [block[:, g * col_blk : (g + 1) * col_blk], pad]
        left = dens[:, h].reshape(n_cyc * aux_blk, lanes)
        term = dot(left, jnp.concatenate(pieces, axis=1), 1, 0)
        if h == 0:
            acc[...] = term
        else:
            acc[...] += term

    def body(oh, carry):
        for other in range(2):
            row = pl.multiple_of((2 * oh + jnp.bitwise_xor(yl, other)) * aux_blk, 8)
            for g in range(n_grp):
                value = acc[pl.ds(row, aux_blk), g * lanes : (g + 1) * lanes]
                cross = jnp.bitwise_xor(core, g % 2)
                slot = other * 2 + cross
                send[slot, oh * n_h + g // 2] = value.astype(BF16)
                if other == 0:

                    @pl.when(cross == 0)
                    def _():
                        keep[oh * n_h + g // 2] = value

        return carry

    lax.fori_loop(0, n_cyc // 2, body, 0)


def lag_kernel(place, moved, ints, other_ints, parts, wide, acc):
    n_src, aux_blk, lanes = moved.shape
    n_orb = ints.shape[2]
    n_dest = parts.shape[1]
    n_zl = parts.shape[2]
    n_cyc = n_src // n_zl
    shift, yl, core = place[0], place[1], place[2]
    wide[...] = moved[...].reshape(n_src * aux_blk, lanes).astype(F32)
    for p in range(0, aux_blk, 2):
        left, right = [], []
        for q in (p, p + 1):
            x = wide[pl.ds(q, n_src, stride=aux_blk), :]
            left.append(pltpu.roll(x, core * (lanes // 2), 1).astype(BF16))
            right += [ints[q], other_ints[q]]
        term = dot(jnp.concatenate(left, axis=1), jnp.concatenate(right, axis=0), 1, 0)
        if p == 0:
            acc[...] = term
        else:
            acc[...] += term
    for k in range(n_cyc):
        target = lax.rem(k + shift, n_cyc)
        other = jnp.bitwise_xor(jnp.bitwise_and(target, 1), yl)
        for g in range(n_orb // lanes):
            slot = other * 2 + jnp.bitwise_xor(core, g % 2)
            parts[slot, lax.div(target, 2) * n_zl + g // 2] = acc[
                k * n_zl : (k + 1) * n_zl, g * lanes : (g + 1) * lanes
            ]


def join_kernel(lag_keep, lag_c, lag_y, lag_yc, aux_keep, aux_c, aux_y, aux_yc, out):
    lag = jnp.concatenate([lag_keep[...] + lag_y[...], lag_c[...] + lag_yc[...]], axis=1)
    aux = aux_keep[...] + aux_c[...].astype(F32) + aux_y[...].astype(F32) + aux_yc[...].astype(F32)
    out[...] = jnp.concatenate([lag, aux], axis=1).astype(BF16)


def local(b_factors, occ_energy, vir_energy, integrals, window_start):
    n_cyc = lax.axis_size("oh") * 2
    n_zl = lax.axis_size("zl")
    n_grp = n_zl * 2
    yl = lax.axis_index("yl")
    core = lax.axis_index("core")
    cyc = lax.axis_index("oh") * 2 + yl
    grp = lax.axis_index("zl") * 2 + core
    own = b_factors[0]
    n_vir, n_aux = own.shape
    n_orb = integrals.shape[2]
    aux_blk = n_aux // n_cyc
    col_blk = n_aux // n_grp
    shift = jnp.mod(window_start[0] + 1, n_cyc)
    place = jnp.stack([shift, yl, core]).astype(jnp.int32)

    ring = [(i, (i + 1) % n_cyc) for i in range(n_cyc)]
    prev_rows = lax.ppermute(own, CYC, ring)
    next_rows = lax.ppermute(own, CYC, [(b, a) for a, b in ring])

    ints = jnp.transpose(integrals, (1, 0, 2))
    other_ints = swap_cores(ints)

    spread = exchange_all(own.reshape(n_cyc, n_vir // n_cyc, n_aux), CYC)
    turned = lax.dynamic_slice_in_dim(jnp.concatenate([spread, spread], axis=0), shift, n_cyc, axis=0)
    rows_i = exchange_all(turned, CYC).reshape(n_vir, n_aux)

    energy_i = occ_energy[jnp.mod(cyc + shift, n_cyc) * n_grp + grp]
    energy_j = occ_energy[jnp.mod(cyc + jnp.array([0, 1, -1]), n_cyc) * n_grp + grp]
    dens = call(
        pair_kernel,
        jax.ShapeDtypeStruct((n_cyc, n_vir // LANES, aux_blk, LANES), BF16),
        [],
        18 * n_vir * n_vir * n_aux,
        5 * 2 * n_vir * n_aux,
        energy_i + energy_j,
        vir_energy[None, :],
        vir_energy[:, None],
        rows_i,
        own,
        next_rows,
        prev_rows,
        specs=[smem] + [vmem] * 6,
    )
    n_dest = n_cyc // 2 * n_zl
    moved = exchange_all(dens.reshape(n_cyc * n_zl, aux_blk, LANES), CYC + ("zl",))

    aux_keep, aux_send = call(
        aux_kernel,
        (
            jax.ShapeDtypeStruct((n_dest, aux_blk, LANES), F32),
            jax.ShapeDtypeStruct((4, n_dest, aux_blk, LANES), BF16),
        ),
        [pltpu.VMEM((n_aux, n_grp * LANES), F32)],
        2 * n_vir * n_aux * n_aux,
        10 * n_vir * n_aux,
        place,
        dens,
        rows_i,
        specs=[smem, vmem, vmem],
    )
    aux_c, aux_y, aux_yc = swap_cores(aux_send[1]), swap_yl(aux_send[2]), swap_both(aux_send[3])

    lag = call(
        lag_kernel,
        jax.ShapeDtypeStruct((4, n_dest, n_zl, LANES), F32),
        [pltpu.VMEM((n_vir * n_aux // LANES, LANES), F32), pltpu.VMEM((n_cyc * n_zl, n_orb), F32)],
        2 * n_vir * n_aux * n_orb,
        2 * n_vir * n_aux * 10,
        place,
        moved,
        ints,
        other_ints,
        specs=[smem] + [vmem] * 3,
    )
    lag_c, lag_y, lag_yc = swap_cores(lag[1]), swap_yl(lag[2]), swap_both(lag[3])
    parts = call(
        join_kernel,
        jax.ShapeDtypeStruct((n_dest, 2 * n_zl + aux_blk, LANES), BF16),
        [],
        10 * n_dest * 32 * LANES,
        20 * n_dest * 32 * LANES,
        lag[0],
        lag_c,
        lag_y,
        lag_yc,
        aux_keep,
        aux_c,
        aux_y,
        aux_yc,
        specs=[vmem] * 8,
    )
    sums = jnp.sum(exchange_all(parts, DEST).astype(F32), axis=0)
    aux_metric = sums[2 * n_zl :, :col_blk]
    same, cross = sums[:n_zl], sums[n_zl : 2 * n_zl]
    low = jnp.where(core == 0, same, cross)
    high = jnp.where(core == 0, cross, same)
    lagrangian = jnp.stack([low, high], axis=1).reshape(n_grp, LANES)
    return (aux_metric, lagrangian)


def solution(mesh):
    n_occ, n_grp = mesh.shape["occ"], mesh.shape["grp"]
    fine = Mesh(mesh.devices.reshape(n_occ // 2, 2, n_grp // 2, 2), ("oh", "yl", "zl", "core"))
    grp = ("zl", "core")
    placed = (P(CYC + grp, None, None), P(), P(), P(grp, CYC, None), P())
    return jax.shard_map(
        local,
        mesh=fine,
        in_specs=placed,
        out_specs=(P(CYC, grp), P(CYC, grp)),
        check_vma=False,
    )
```

time: 195 us -> 190 us (0.974)
  waiting for transfers between devices: 26.8 us -> 97.8 us
  blocking collectives: 36.1 us -> 0 us
  matrix products: 19 us -> 0 us
  Pallas kernels: 0 us -> 15.9 us
  starting transfers between devices: 74.3 us -> 61.7 us
  local copies, waits for them, and re-layouts: 21.6 us -> 9.64 us
  other arithmetic: 11.1 us -> 2.1 us
  between operations: 5.35 us -> 1.46 us
    ppermute x2 -> x6, waiting for transfers between devices: 4.1 us -> 47.6 us  [the longest x1 33.6 us: local(): next_rows = lax.ppermute(own, CYC, [(b, a) for a, b in ring])]
    all_to_all x1 -> x0, blocking collectives: 36.1 us -> none  [exchange_all(): return lax.all_to_all(x, axes, split_axis=0, concat_axis=0, tiled=True)]
    all_to_all x3 -> x4, waiting for transfers between devices: 22.7 us -> 50.2 us  [exchange_all(): return lax.all_to_all(x, axes, split_axis=0, concat_axis=0, tiled=True)]
    dot_general x9 -> x0, matrix products: 19 us -> none  [the longest x3 6.55 us: local(): lax.dot_general(rows_j, combined_t, (((0,), (0,)), ((), ())), preferred_e...]
    all_to_all x3 -> x4, starting transfers between devices: 51.9 us -> 36 us  [exchange_all(): return lax.all_to_all(x, axes, split_axis=0, concat_axis=0, tiled=True)]
    pallas_call x0 -> x4, Pallas kernels: none -> 15.9 us  [call(): pl.pallas_call(kernel, out_shape=outs, in_specs=specs, out_specs=jax.tree...]
    select_n x3 -> x1, other arithmetic: 9.17 us -> 0.01 us  [local(): occ_energy[jnp.mod(cyc + jnp.array([0, 1, -1]), n_cyc) * n_grp + grp]]
    slice x3 -> x0, local copies, waits for them, and re-layouts: 5.96 us -> none  [the longest x2 4.67 us: local(): cols[:, :, 0]]
  transfers between devices with their start and end apart: 8 -> 13, of which waited for: 4 -> 7; matrix products, arithmetic and copies ran while one was open for 25% -> 4% of each run, Pallas kernels for 0% -> 7%
where the time goes in v2:
time: 190 us; the launch traced here: 188 us
  waiting for transfers between devices  97.8 us (51%)
  starting transfers between devices  61.7 us (32%)
  Pallas kernels  15.9 us (8%)
  local copies, waits for them, and re-layouts  9.64 us (5%)
  other arithmetic  2.1 us (1%)
    all_to_all x4, waiting for transfers between devices, exchange_all(): return lax.all_to_all(x, axes, split_axis=0, concat_axis=0, tiled=True)  50.2 us
    all_to_all x4, starting transfers between devices, exchange_all(): return lax.all_to_all(x, axes, split_axis=0, concat_axis=0, tiled=True)  36 us
    ppermute x1, waiting for transfers between devices, local(): next_rows = lax.ppermute(own, CYC, [(b, a) for a, b in ring])  33.6 us
    pallas_call x4, Pallas kernels, call(): pl.pallas_call(kernel, out_shape=outs, in_specs=specs, out_specs=jax.tree...  15.9 us
    ppermute x3, starting transfers between devices, swap_cores(): return lax.ppermute(x, 'core', [(0, 1), (1, 0)])  12.6 us
    ppermute x1, starting transfers between devices, local(): next_rows = lax.ppermute(own, CYC, [(b, a) for a, b in ring])  9.68 us
    ppermute x1, waiting for transfers between devices, local(): prev_rows = lax.ppermute(own, CYC, ring)  7.68 us
    unnamed x15, local copies, waits for them, and re-layouts  5.84 us
  transfers between devices with their start and end apart: 13, of which 7 were waited for; matrix products, arithmetic and copies ran while one was open for 4% of the time, Pallas kernels for 7%

profile of v2, /device:TPU:1, one launch (start us, length us, event | category | flops | bytes accessed | tf_op | source)
XLA Modules:
  0.0 188.5 jit_solution(547287789883214125)
XLA Ops:
  0.6 14.5 %all-to-all-start = ((bf16[32,16,768]{2,1,0:T(8,128)(2,1)}), bf16[32,16,768]{2,1,0:T(8,128)(2,1)S(1)}, u32[]{:S(2)}, u32[]{:S(2)}) async-start(bf16[32,16,768]{2,1,0:T(8,128)(2,1)} %bitcast.7), calls=%async_computation | async-start | bytes 1572864 | tf_op jit(solution)/shard_map/all_to_all | solution.py:20
  15.8 17.2 %all-to-all-done = bf16[32,16,768]{2,1,0:T(8,128)(2,1)S(1)} async-done(((bf16[32,16,768]{2,1,0:T(8,128)(2,1)}), bf16[32,16,768]{2,1,0:T(8,128)(2,1)S(1)}, u32[]{:S(2)}, u32[]{:S(2)}) %all-to-all-start) | async-done | bytes 786464 | tf_op jit(solution)/shard_map/all_to_all | solution.py:20
  33.0 1.2 fusion
  34.2 4.6 %all-to-all-start.1 = ((bf16[32,16,768]{2,1,0:T(8,128)(2,1)}), bf16[32,16,768]{2,1,0:T(8,128)(2,1)}, u32[]{:S(2)}, u32[]{:S(2)}) async-start(bf16[32,16,768]{2,1,0:T(8,128)(2,1)} %fusion), calls=%async_computation.1 | async-start | bytes 1572864 | tf_op jit(solution)/shard_map/all_to_all | solution.py:20
  38.8 0.0 copy-start.5
  38.8 0.0 copy-start.6
  38.8 0.0 copy-start.4
  38.8 3.6 %copy.14 = bf16[64,24,1024]{2,0,1:T(8,128)(2,1)S(1)} copy(bf16[64,24,1024]{2,1,0:T(8,128)(2,1)} %param.9) | data formatting | bytes 6291456 | tf_op args[3]
  42.5 8.3 %collective-permute-start.2 = (bf16[24,64,1024]{2,1,0:T(8,128)(2,1)S(1)}, bf16[24,64,1024]{2,1,0:T(8,128)(2,1)}, u32[]{:S(2)}, u32[]{:S(2)}) collective-permute-start(bf16[24,64,1024]{2,1,0:T(8,128)(2,1)S(1)} %bitcast.33), channel_id=1, source_target_pairs={{0,1},{1,0},{2,3},{3,2},{4,5},{5,4},{6,7},{7,6},{8,9},{9,8},{10,11... | collective-permute-start | bytes 9437192 | tf_op jit(solution)/shard_map/ppermute | solution.py:24
  50.8 9.7 %collective-permute-start = (bf16[512,768]{1,0:T(8,128)(2,1)}, bf16[512,768]{1,0:T(8,128)(2,1)}, u32[]{:S(2)}, u32[]{:S(2)}) collective-permute-start(bf16[512,768]{1,0:T(8,128)(2,1)} %bitcast.9.own), channel_id=1, source_target_pairs={{8,0},{16,8},{24,16},{32,24},{40,32},{48,40},{56,48},{64,56},{72,6... | collective-permute-start | bytes 2359304 | tf_op jit(solution)/shard_map/ppermute | solution.py:165
  60.5 0.0 collective-permute-start.1
  60.5 0.0 copy-done.5
  60.5 0.7 dynamic_slice.6
  61.1 0.0 copy-done.6
  61.2 0.6 gather_fusion
  61.8 0.0 copy-done.4
  61.8 0.1 copy.10.vir_col
  62.0 0.7 broadcast_add_fusion.energy
  62.7 33.6 %collective-permute-done.nxt = bf16[512,768]{1,0:T(8,128)(2,1)} collective-permute-done((bf16[512,768]{1,0:T(8,128)(2,1)}, bf16[512,768]{1,0:T(8,128)(2,1)}, u32[]{:S(2)}, u32[]{:S(2)}) %collective-permute-start) | collective-permute-done | bytes 786464 | tf_op jit(solution)/shard_map/ppermute | solution.py:165
  96.2 7.7 %collective-permute-done.1.prv = bf16[512,768]{1,0:T(8,128)(2,1)} collective-permute-done((bf16[512,768]{1,0:T(8,128)(2,1)}, bf16[512,768]{1,0:T(8,128)(2,1)}, u32[]{:S(2)}, u32[]{:S(2)}) %collective-permute-start.1) | collective-permute-done | bytes 786464 | tf_op jit(solution)/shard_map/ppermute | solution.py:164
  103.9 0.0 all-to-all-done.1
  103.9 6.6 %shard_map.77.dens = bf16[32,4,24,128]{3,2,1,0:T(8,128)(2,1)S(1)} custom-call(f32[3]{0:T(128)S(1)} %broadcast_add_fusion.energy, f32[1,512]{1,0:T(1,128)S(1)} %bitcast.37, f32[512,1]{1,0:T(8,128)S(1)} %copy.10.vir_col, bf16[512,768]{1,0:T(8,128)(2,1)} %bitcast.8.rows_i, bf16[512,768]{1,0:T(8,128)(2,1)} %bitcast.9.own, ...), custom_call_target="tpu_custom_call" | custom-call | flops 3623878656 | bytes 3932160 | tf_op jit(solution)/shard_map/pallas_call | solution.py:40
  110.5 0.0 copy-start
  110.5 0.9 copy-done
  111.4 7.5 %all-to-all-start.2 = ((bf16[128,24,128]{2,1,0:T(8,128)(2,1)}), bf16[128,24,128]{2,1,0:T(8,128)(2,1)}, u32[]{:S(2)}, u32[]{:S(2)}) async-start(bf16[128,24,128]{2,1,0:T(8,128)(2,1)} %bitcast.35), calls=%async_computation.2 | async-start | bytes 1572864 | tf_op jit(solution)/shard_map/all_to_all | solution.py:20
  118.9 0.1 pad_add_fusion.place
  119.0 0.0 copy-start.1
  119.0 1.1 copy-done.1
  120.2 3.7 %shard_map.79 = (f32[64,24,128]{2,1,0:T(8,128)S(1)}, bf16[4,64,24,128]{3,2,1,0:T(8,128)(2,1)S(1)}) custom-call(s32[3]{0:T(128)S(1)} %pad_add_fusion.place, bf16[32,4,24,128]{3,2,1,0:T(8,128)(2,1)S(1)} %copy-done.1, bf16[512,768]{1,0:T(8,128)(2,1)} %bitcast.8.rows_i), custom_call_target="tpu_custom_call" | custom-call | flops 603979776 | bytes 3932160 | tf_op jit(solution)/shard_map/pallas_call | solution.py:40
  123.9 0.0 copy-start.2
  123.9 1.1 slice_bitcast_fusion
  125.0 0.2 copy-done.2
  125.2 1.1 collective-permute-start.6
  126.3 0.8 collective-permute-start.7
  127.1 0.8 collective-permute-start.8
  128.0 0.0 collective-permute-done.2.other_ints
  128.0 14.8 %all-to-all-done.2.moved = bf16[128,24,128]{2,1,0:T(8,128)(2,1)} async-done(((bf16[128,24,128]{2,1,0:T(8,128)(2,1)}), bf16[128,24,128]{2,1,0:T(8,128)(2,1)}, u32[]{:S(2)}, u32[]{:S(2)}) %all-to-all-start.2) | async-done | bytes 786464 | tf_op jit(solution)/shard_map/all_to_all | solution.py:20
  142.7 3.4 %shard_map.78 = f32[4,64,4,128]{3,2,1,0:T(4,128)S(1)} custom-call(s32[3]{0:T(128)S(1)} %pad_add_fusion.place, bf16[128,24,128]{2,1,0:T(8,128)(2,1)} %all-to-all-done.2.moved, bf16[24,64,1024]{2,1,0:T(8,128)(2,1)S(1)} %bitcast.34, bf16[24,64,1024]{2,1,0:T(8,128)(2,1)} %collective-permute-done.2.other_ints), custom_call_target="tpu_custom_call" | custom-call | flops 805306368 | bytes 7864320 | tf_op jit(solution)/shard_map/pallas_call | solution.py:40
  146.2 0.0 copy-start.3
  146.2 3.1 %collective-permute-start.3 = (f32[64,4,128]{2,1,0:T(4,128)S(1)}, f32[64,4,128]{2,1,0:T(4,128)S(1)}, u32[]{:S(2)}, u32[]{:S(2)}) collective-permute-start(f32[64,4,128]{2,1,0:T(4,128)S(1)} %get-tuple-element.11), channel_id=1, source_target_pairs={{0,1},{1,0},{2,3},{3,2},{4,5},{5,4},{6,7},{7,6},{8,9},{9,8},{10,11... | collective-permute-start | bytes 393224 | tf_op jit(solution)/shard_map/ppermute | solution.py:24
  149.3 0.0 collective-permute-start.4
  149.3 0.0 collective-permute-done.6.aux_c
  149.3 1.7 collective-permute-start.5
  151.1 0.0 collective-permute-done.7.aux_y
  151.1 0.0 collective-permute-done.8.aux_yc
  151.1 0.0 collective-permute-done.3.lag_c
  151.1 3.3 %collective-permute-done.4.lag_y = f32[64,4,128]{2,1,0:T(4,128)S(1)} collective-permute-done((f32[64,4,128]{2,1,0:T(4,128)S(1)}, f32[64,4,128]{2,1,0:T(4,128)S(1)}, u32[]{:S(2)}, u32[]{:S(2)}) %collective-permute-start.4) | collective-permute-done | bytes 131104 | tf_op jit(solution)/shard_map/ppermute | solution.py:28
  154.4 3.0 %collective-permute-done.5.lag_yc = f32[64,4,128]{2,1,0:T(4,128)S(1)} collective-permute-done((f32[64,4,128]{2,1,0:T(4,128)S(1)}, f32[64,4,128]{2,1,0:T(4,128)S(1)}, u32[]{:S(2)}, u32[]{:S(2)}) %collective-permute-start.5) | collective-permute-done | bytes 131104 | tf_op jit(solution)/shard_map/ppermute | solution.py:32
  157.4 0.0 copy-done.3
  157.4 2.1 %shard_map.80 = bf16[64,32,128]{2,1,0:T(8,128)(2,1)} custom-call(f32[64,4,128]{2,1,0:T(4,128)S(1)} %get-tuple-element.12.lag_keep, f32[64,4,128]{2,1,0:T(4,128)S(1)} %collective-permute-done.3.lag_c, f32[64,4,128]{2,1,0:T(4,128)S(1)} %collective-permute-done.4.lag_y, f32[64,4,128]{2,1,0:T(4,128)S(1)} %collective-permute-done.5.lag_yc, ...), custom_call_target="tpu_custom_call" | custom-call | flops 2621440 | bytes 5242880 | tf_op jit(solution)/shard_map/pallas_call | solution.py:40
  159.5 9.4 %all-to-all-start.3 = ((bf16[64,32,128]{2,1,0:T(8,128)(2,1)}), bf16[64,32,128]{2,1,0:T(8,128)(2,1)S(1)}, u32[]{:S(2)}, u32[]{:S(2)}) async-start(bf16[64,32,128]{2,1,0:T(8,128)(2,1)} %shard_map.80), calls=%async_computation.3 | async-start | bytes 1048576 | tf_op jit(solution)/shard_map/all_to_all | solution.py:20
  168.9 18.3 %all-to-all-done.3 = bf16[64,32,128]{2,1,0:T(8,128)(2,1)S(1)} async-done(((bf16[64,32,128]{2,1,0:T(8,128)(2,1)}), bf16[64,32,128]{2,1,0:T(8,128)(2,1)S(1)}, u32[]{:S(2)}, u32[]{:S(2)}) %all-to-all-start.3) | async-done | bytes 524320 | tf_op jit(solution)/shard_map/all_to_all | solution.py:20
  187.2 0.1 convert_reduce_fusion
  187.3 0.6 slice.46
  187.9 0.6 copy.12
  (5 shorter events, 0.1 us)
Async XLA Ops:
  0.6 32.4 %all-to-all-start = ((bf16[32,16,768]{2,1,0:T(8,128)(2,1)}), bf16[32,16,768]{2,1,0:T(8,128)(2,1)S(1)}, u32[]{:S(2)}, u32[]{:S(2)}) async-start(bf16[32,16,768]{2,1,0:T(8,128)(2,1)} %bitcast.7), calls=%async_computation | async-start | bytes 1572864 | tf_op jit(solution)/shard_map/all_to_all | solution.py:20
  34.2 69.8 %all-to-all-start.1 = ((bf16[32,16,768]{2,1,0:T(8,128)(2,1)}), bf16[32,16,768]{2,1,0:T(8,128)(2,1)}, u32[]{:S(2)}, u32[]{:S(2)}) async-start(bf16[32,16,768]{2,1,0:T(8,128)(2,1)} %fusion), calls=%async_computation.1 | async-start | bytes 1572864 | tf_op jit(solution)/shard_map/all_to_all | solution.py:20
  38.8 21.7 %copy-start.5 = (f32[256]{0:T(256)S(1)}, f32[256]{0:T(256)}, u32[]{:S(2)}) copy-start(f32[256]{0:T(256)} %param.7) | copy-start | bytes 3076
  38.8 22.3 %copy-start.6 = (s32[3]{0:T(128)S(1)}, s32[3]{0:T(128)}, u32[]{:S(2)}) copy-start(s32[3]{0:T(128)} %constant.60.clone) | copy-start | bytes 40
  38.8 23.0 %copy-start.4 = (f32[512]{0:T(512)S(1)}, f32[512]{0:T(512)}, u32[]{:S(2)}) copy-start(f32[512]{0:T(512)} %param.8) | copy-start | bytes 6148
  42.5 85.5 %collective-permute-start.2 = (bf16[24,64,1024]{2,1,0:T(8,128)(2,1)S(1)}, bf16[24,64,1024]{2,1,0:T(8,128)(2,1)}, u32[]{:S(2)}, u32[]{:S(2)}) collective-permute-start(bf16[24,64,1024]{2,1,0:T(8,128)(2,1)S(1)} %bitcast.33), channel_id=1, source_target_pairs={{0,1},{1,0},{2,3},{3,2},{4,5},{5,4},{6,7},{7,6},{8,9},{9,8},{10,11... | collective-permute-start | bytes 9437192 | tf_op jit(solution)/shard_map/ppermute | solution.py:24
  50.8 45.5 %collective-permute-start = (bf16[512,768]{1,0:T(8,128)(2,1)}, bf16[512,768]{1,0:T(8,128)(2,1)}, u32[]{:S(2)}, u32[]{:S(2)}) collective-permute-start(bf16[512,768]{1,0:T(8,128)(2,1)} %bitcast.9.own), channel_id=1, source_target_pairs={{8,0},{16,8},{24,16},{32,24},{40,32},{48,40},{56,48},{64,56},{72,6... | collective-permute-start | bytes 2359304 | tf_op jit(solution)/shard_map/ppermute | solution.py:165
  60.5 43.5 %collective-permute-start.1 = (bf16[512,768]{1,0:T(8,128)(2,1)}, bf16[512,768]{1,0:T(8,128)(2,1)}, u32[]{:S(2)}, u32[]{:S(2)}) collective-permute-start(bf16[512,768]{1,0:T(8,128)(2,1)} %bitcast.9.own), channel_id=1, source_target_pairs={{0,8},{8,16},{16,24},{24,32},{32,40},{40,48},{48,56},{56,64},{64,7... | collective-permute-start | bytes 2359304 | tf_op jit(solution)/shard_map/ppermute | solution.py:164
  110.5 0.9 copy-start
  111.4 31.3 %all-to-all-start.2 = ((bf16[128,24,128]{2,1,0:T(8,128)(2,1)}), bf16[128,24,128]{2,1,0:T(8,128)(2,1)}, u32[]{:S(2)}, u32[]{:S(2)}) async-start(bf16[128,24,128]{2,1,0:T(8,128)(2,1)} %bitcast.35), calls=%async_computation.2 | async-start | bytes 1572864 | tf_op jit(solution)/shard_map/all_to_all | solution.py:20
  119.0 1.1 copy-start.1
  123.9 1.3 copy-start.2
  125.2 24.2 %collective-permute-start.6 = (bf16[64,24,128]{2,1,0:T(8,128)(2,1)}, bf16[64,24,128]{2,1,0:T(8,128)(2,1)S(1)}, u32[]{:S(2)}, u32[]{:S(2)}) collective-permute-start(bf16[64,24,128]{2,1,0:T(8,128)(2,1)} %get-tuple-element.8), channel_id=1, source_target_pairs={{0,1},{1,0},{2,3},{3,2},{4,5},{5,4},{6,7},{7,6},{8,9},{9,8},{10,11... | collective-permute-start | bytes 1179656 | tf_op jit(solution)/shard_map/ppermute | solution.py:24
  126.3 24.7 %collective-permute-start.7 = (bf16[64,24,128]{2,1,0:T(8,128)(2,1)}, bf16[64,24,128]{2,1,0:T(8,128)(2,1)}, u32[]{:S(2)}, u32[]{:S(2)}) collective-permute-start(bf16[64,24,128]{2,1,0:T(8,128)(2,1)} %get-tuple-element.7), channel_id=1, source_target_pairs={{0,8},{8,0},{1,9},{9,1},{2,10},{10,2},{3,11},{11,3},{4,12},{12,4},... | collective-permute-start | bytes 1179656 | tf_op jit(solution)/shard_map/ppermute | solution.py:28
  127.1 24.0 %collective-permute-start.8 = (bf16[64,24,128]{2,1,0:T(8,128)(2,1)}, bf16[64,24,128]{2,1,0:T(8,128)(2,1)}, u32[]{:S(2)}, u32[]{:S(2)}) collective-permute-start(bf16[64,24,128]{2,1,0:T(8,128)(2,1)} %get-tuple-element.6), channel_id=1, source_target_pairs={{0,9},{1,8},{8,1},{9,0},{2,11},{3,10},{10,3},{11,2},{4,13},{5,12},... | collective-permute-start | bytes 1179656 | tf_op jit(solution)/shard_map/ppermute | solution.py:32
  146.2 11.2 %copy-start.3 = (f32[64,24,128]{2,1,0:T(8,128)S(1)}, f32[64,24,128]{2,1,0:T(8,128)}, u32[]{:S(2)}) copy-start(f32[64,24,128]{2,1,0:T(8,128)} %copy-done.2) | copy-start | bytes 2359300
  146.2 4.9 %collective-permute-start.3 = (f32[64,4,128]{2,1,0:T(4,128)S(1)}, f32[64,4,128]{2,1,0:T(4,128)S(1)}, u32[]{:S(2)}, u32[]{:S(2)}) collective-permute-start(f32[64,4,128]{2,1,0:T(4,128)S(1)} %get-tuple-element.11), channel_id=1, source_target_pairs={{0,1},{1,0},{2,3},{3,2},{4,5},{5,4},{6,7},{7,6},{8,9},{9,8},{10,11... | collective-permute-start | bytes 393224 | tf_op jit(solution)/shard_map/ppermute | solution.py:24
  149.3 5.1 %collective-permute-start.4 = (f32[64,4,128]{2,1,0:T(4,128)S(1)}, f32[64,4,128]{2,1,0:T(4,128)S(1)}, u32[]{:S(2)}, u32[]{:S(2)}) collective-permute-start(f32[64,4,128]{2,1,0:T(4,128)S(1)} %get-tuple-element.10), channel_id=1, source_target_pairs={{0,8},{8,0},{1,9},{9,1},{2,10},{10,2},{3,11},{11,3},{4,12},{12,4},... | collective-permute-start | bytes 393224 | tf_op jit(solution)/shard_map/ppermute | solution.py:28
  149.3 8.0 %collective-permute-start.5 = (f32[64,4,128]{2,1,0:T(4,128)S(1)}, f32[64,4,128]{2,1,0:T(4,128)S(1)}, u32[]{:S(2)}, u32[]{:S(2)}) collective-permute-start(f32[64,4,128]{2,1,0:T(4,128)S(1)} %get-tuple-element.9), channel_id=1, source_target_pairs={{0,9},{1,8},{8,1},{9,0},{2,11},{3,10},{10,3},{11,2},{4,13},{5,12},... | collective-permute-start | bytes 393224 | tf_op jit(solution)/shard_map/ppermute | solution.py:32
  159.5 27.7 %all-to-all-start.3 = ((bf16[64,32,128]{2,1,0:T(8,128)(2,1)}), bf16[64,32,128]{2,1,0:T(8,128)(2,1)S(1)}, u32[]{:S(2)}, u32[]{:S(2)}) async-start(bf16[64,32,128]{2,1,0:T(8,128)(2,1)} %shard_map.80), calls=%async_computation.3 | async-start | bytes 1048576 | tf_op jit(solution)/shard_map/all_to_all | solution.py:20

commit v3 on v2

--- a/solution.py
+++ b/solution.py
@@ -48,21 +48,42 @@
     )(*args)
 
 
-def pair_kernel(energy, vir_row, vir_col, rows_i, own, nxt, prv, out):
+def turn_kernel(place, spread, out):
+    n_cyc = spread.shape[0]
+    shift = place[0]
+
+    def body(pair, carry):
+        for odd in range(2):
+            d = 2 * pair + odd
+            out[d, 0] = spread[lax.rem(d + shift, n_cyc)]
+            out[d, 1] = spread[lax.rem(d + (2 * odd - 1) + n_cyc, n_cyc)]
+        return carry
+
+    lax.fori_loop(0, n_cyc // 2, body, 0)
+
+
+def pair_kernel(energy, vir_row, vir_col, rows, own, mate, out):
     n_cyc, n_h, aux_blk, lanes = out.shape
-    n_vir, n_aux = rows_i.shape
+    n_vir, n_aux = own.shape
+    sub = rows.shape[2]
     blk = 2 * lanes
+    rows_i = rows[:, 0].reshape(n_vir, n_aux)
+    far = rows[:, 1].reshape(n_vir, n_aux)
 
     def body(step, carry):
         start = pl.multiple_of(step * blk, blk)
-        block_i = rows_i[pl.ds(start, blk), :]
+        chunk = pl.ds(step * (blk // sub), blk // sub)
+        block_i = rows[chunk, 0].reshape(blk, n_aux)
+        block_far = rows[chunk, 1].reshape(blk, n_aux)
         vir_sum = vir_col[pl.ds(start, blk), :] + vir_row[...]
         total = jnp.zeros((blk, n_aux), F32)
-        for t, rows_j in enumerate((own, nxt, prv)):
-            inter = dot(block_i, rows_j[...], 1, 1)
-            inter_t = dot(rows_j[pl.ds(start, blk), :], rows_i[...], 1, 1)
+        for t, (block_j, rows_j) in enumerate(
+            ((own[pl.ds(start, blk), :], own[...]), (mate[pl.ds(start, blk), :], mate[...]), (block_far, far))
+        ):
+            inter = dot(block_i, rows_j, 1, 1)
+            inter_t = dot(block_j, rows_i, 1, 1)
             combined = ((2.0 * inter - inter_t) / (energy[t] - vir_sum)).astype(BF16)
-            total = total + dot(combined, rows_j[...], 1, 0)
+            total = total + dot(combined, rows_j, 1, 0)
         for half in range(2):
             turned = jnp.transpose(total[half * lanes : (half + 1) * lanes])
             out[:, step * 2 + half] = turned.reshape(n_cyc, aux_blk, lanes).astype(BF16)
@@ -71,15 +92,16 @@
     lax.fori_loop(0, n_h // 2, body, 0)
 
 
-def aux_kernel(place, dens, rows_i, keep, send, acc):
+def aux_kernel(place, dens, rows, keep, send, acc):
     n_cyc, n_h, aux_blk, lanes = dens.shape
-    n_vir, n_aux = rows_i.shape
+    sub, n_aux = rows.shape[2:]
+    per = lanes // sub
     n_grp = 2 * n_h
     col_blk = n_aux // n_grp
     yl, core = place[1], place[2]
     pad = jnp.zeros((lanes, lanes - col_blk), BF16)
     for h in range(n_h):
-        block = rows_i[h * lanes : (h + 1) * lanes, :]
+        block = rows[h * per : (h + 1) * per, 0].reshape(lanes, n_aux)
         pieces = []
         for g in range(n_grp):
             pieces += [block[:, g * col_blk : (g + 1) * col_blk], pad]
@@ -160,19 +182,28 @@
     shift = jnp.mod(window_start[0] + 1, n_cyc)
     place = jnp.stack([shift, yl, core]).astype(jnp.int32)
 
-    ring = [(i, (i + 1) % n_cyc) for i in range(n_cyc)]
-    prev_rows = lax.ppermute(own, CYC, ring)
-    next_rows = lax.ppermute(own, CYC, [(b, a) for a, b in ring])
+    mate = swap_yl(own)
 
     ints = jnp.transpose(integrals, (1, 0, 2))
     other_ints = swap_cores(ints)
 
-    spread = exchange_all(own.reshape(n_cyc, n_vir // n_cyc, n_aux), CYC)
-    turned = lax.dynamic_slice_in_dim(jnp.concatenate([spread, spread], axis=0), shift, n_cyc, axis=0)
-    rows_i = exchange_all(turned, CYC).reshape(n_vir, n_aux)
-
+    sub = n_vir // n_cyc
+    spread = exchange_all(own.reshape(n_cyc, sub, n_aux), CYC)
+    turned = call(
+        turn_kernel,
+        jax.ShapeDtypeStruct((n_cyc, 2, sub, n_aux), BF16),
+        [],
+        0,
+        8 * n_vir * n_aux,
+        place,
+        spread,
+        specs=[smem, vmem],
+    )
+    rows = exchange_all(turned, CYC)
+
+    step = 1 - 2 * yl
     energy_i = occ_energy[jnp.mod(cyc + shift, n_cyc) * n_grp + grp]
-    energy_j = occ_energy[jnp.mod(cyc + jnp.array([0, 1, -1]), n_cyc) * n_grp + grp]
+    energy_j = occ_energy[jnp.mod(cyc + jnp.stack([0, step, -step]), n_cyc) * n_grp + grp]
     dens = call(
         pair_kernel,
         jax.ShapeDtypeStruct((n_cyc, n_vir // LANES, aux_blk, LANES), BF16),
@@ -182,11 +213,10 @@
         energy_i + energy_j,
         vir_energy[None, :],
         vir_energy[:, None],
-        rows_i,
+        rows,
         own,
-        next_rows,
-        prev_rows,
-        specs=[smem] + [vmem] * 6,
+        mate,
+        specs=[smem] + [vmem] * 5,
     )
     n_dest = n_cyc // 2 * n_zl
     moved = exchange_all(dens.reshape(n_cyc * n_zl, aux_blk, LANES), CYC + ("zl",))
@@ -202,7 +232,7 @@
         10 * n_vir * n_aux,
         place,
         dens,
-        rows_i,
+        rows,
         specs=[smem, vmem, vmem],
     )
     aux_c, aux_y, aux_yc = swap_cores(aux_send[1]), swap_yl(aux_send[2]), swap_both(aux_send[3])

time: 190 us -> 174 us (0.916)
  waiting for transfers between devices: 97.8 us -> 80.2 us
  Pallas kernels: 15.9 us -> 18.3 us
    ppermute x2 -> x0, waiting for transfers between devices: 41.3 us -> none  [the longest x1 33.6 us: local(): next_rows = lax.ppermute(own, CYC, [(b, a) for a, b in ring])]
    ppermute x2 -> x3, waiting for transfers between devices: 3.31 us -> 27.9 us  [swap_yl(): return lax.ppermute(x, 'yl', [(0, 1), (1, 0)])]
    all_to_all x4, starting transfers between devices: 36 us -> 46.7 us  [exchange_all(): return lax.all_to_all(x, axes, split_axis=0, concat_axis=0, tiled=True)]
    ppermute x2 -> x0, starting transfers between devices: 9.68 us -> none  [the longest x1 9.68 us: local(): next_rows = lax.ppermute(own, CYC, [(b, a) for a, b in ring])]
    ppermute x2 -> x3, starting transfers between devices: 0.79 us -> 5.17 us  [swap_yl(): return lax.ppermute(x, 'yl', [(0, 1), (1, 0)])]
    ppermute x3, starting transfers between devices: 12.6 us -> 8.27 us  [swap_cores(): return lax.ppermute(x, 'core', [(0, 1), (1, 0)])]
    pallas_call x4 -> x5, Pallas kernels: 15.9 us -> 18.3 us  [call(): pl.pallas_call(kernel, out_shape=outs, in_specs=specs, out_specs=jax.tree...]
    unnamed x15 -> x13, local copies, waits for them, and re-layouts: 5.84 us -> 5.86 us
  transfers between devices with their start and end apart: 13 -> 12, of which waited for: 7 -> 6; matrix products, arithmetic and copies ran while one was open for 4% -> 4% of each run, Pallas kernels for 7% -> 8%
where the time goes in v3:
time: 174 us; the launch traced here: 173 us
  waiting for transfers between devices  80.2 us (46%)
  starting transfers between devices  62.7 us (36%)
  Pallas kernels  18.3 us (11%)
  local copies, waits for them, and re-layouts  9.57 us (6%)
    all_to_all x4, waiting for transfers between devices, exchange_all(): return lax.all_to_all(x, axes, split_axis=0, concat_axis=0, tiled=True)  50.9 us
    all_to_all x4, starting transfers between devices, exchange_all(): return lax.all_to_all(x, axes, split_axis=0, concat_axis=0, tiled=True)  46.7 us
    ppermute x3, waiting for transfers between devices, swap_yl(): return lax.ppermute(x, 'yl', [(0, 1), (1, 0)])  27.9 us
    pallas_call x5, Pallas kernels, call(): pl.pallas_call(kernel, out_shape=outs, in_specs=specs, out_specs=jax.tree...  18.3 us
    ppermute x3, starting transfers between devices, swap_cores(): return lax.ppermute(x, 'core', [(0, 1), (1, 0)])  8.27 us
    unnamed x13, local copies, waits for them, and re-layouts  5.86 us
    ppermute x3, starting transfers between devices, swap_yl(): return lax.ppermute(x, 'yl', [(0, 1), (1, 0)])  5.17 us
  transfers between devices with their start and end apart: 12, of which 6 were waited for; matrix products, arithmetic and copies ran while one was open for 4% of the time, Pallas kernels for 8%

profile of v3, /device:TPU:1, one launch (start us, length us, event | category | flops | bytes accessed | tf_op | source)
XLA Modules:
  0.0 173.1 jit_solution(2923458296480417610)
XLA Ops:
  0.6 14.5 %all-to-all-start = ((bf16[32,16,768]{2,1,0:T(8,128)(2,1)}), bf16[32,16,768]{2,1,0:T(8,128)(2,1)S(1)}, u32[]{:S(2)}, u32[]{:S(2)}) async-start(bf16[32,16,768]{2,1,0:T(8,128)(2,1)} %bitcast.10), calls=%async_computation | async-start | bytes 1572864 | tf_op jit(solution)/shard_map/all_to_all | solution.py:20
  15.8 0.1 pad_add_fusion.place
  15.9 17.1 %all-to-all-done.spread = bf16[32,16,768]{2,1,0:T(8,128)(2,1)S(1)} async-done(((bf16[32,16,768]{2,1,0:T(8,128)(2,1)}), bf16[32,16,768]{2,1,0:T(8,128)(2,1)S(1)}, u32[]{:S(2)}, u32[]{:S(2)}) %all-to-all-start) | async-done | bytes 786464 | tf_op jit(solution)/shard_map/all_to_all | solution.py:20
  33.0 2.0 %shard_map.68 = bf16[32,2,16,768]{3,2,1,0:T(8,128)(2,1)} custom-call(s32[3]{0:T(128)S(1)} %pad_add_fusion.place, bf16[32,16,768]{2,1,0:T(8,128)(2,1)S(1)} %all-to-all-done.spread), custom_call_target="tpu_custom_call" | custom-call | bytes 3145728 | tf_op jit(solution)/shard_map/pallas_call | solution.py:40
  35.0 4.7 %all-to-all-start.1 = ((bf16[32,2,16,768]{3,2,1,0:T(8,128)(2,1)}), bf16[32,2,16,768]{3,2,1,0:T(8,128)(2,1)}, u32[]{:S(2)}, u32[]{:S(2)}) async-start(bf16[32,2,16,768]{3,2,1,0:T(8,128)(2,1)} %shard_map.68), calls=%async_computation.1 | async-start | bytes 3145728 | tf_op jit(solution)/shard_map/all_to_all | solution.py:20
  39.7 0.0 copy-start.5
  39.7 0.0 copy-start.4
  39.7 3.6 %copy.13 = bf16[64,24,1024]{2,0,1:T(8,128)(2,1)S(1)} copy(bf16[64,24,1024]{2,1,0:T(8,128)(2,1)} %param.8) | data formatting | bytes 6291456 | tf_op args[3]
  43.3 8.3 %collective-permute-start.1 = (bf16[24,64,1024]{2,1,0:T(8,128)(2,1)S(1)}, bf16[24,64,1024]{2,1,0:T(8,128)(2,1)}, u32[]{:S(2)}, u32[]{:S(2)}) collective-permute-start(bf16[24,64,1024]{2,1,0:T(8,128)(2,1)S(1)} %bitcast.36), channel_id=1, source_target_pairs={{0,1},{1,0},{2,3},{3,2},{4,5},{5,4},{6,7},{7,6},{8,9},{9,8},{10,11... | collective-permute-start | bytes 9437192 | tf_op jit(solution)/shard_map/ppermute | solution.py:24
  51.6 1.5 collective-permute-start
  53.0 0.0 copy-done.5
  53.0 0.6 dynamic_slice.3
  53.6 0.1 fusion.3
  53.7 0.6 gather_fusion
  54.3 0.0 copy-done.4
  54.3 0.1 copy.9.vir_col
  54.5 0.6 broadcast_add_fusion.energy
  55.1 24.0 %collective-permute-done.mate = bf16[512,768]{1,0:T(8,128)(2,1)} collective-permute-done((bf16[512,768]{1,0:T(8,128)(2,1)}, bf16[512,768]{1,0:T(8,128)(2,1)}, u32[]{:S(2)}, u32[]{:S(2)}) %collective-permute-start) | collective-permute-done | bytes 786464 | tf_op jit(solution)/shard_map/ppermute | solution.py:28
  79.1 0.0 all-to-all-done.1.rows
  79.1 6.7 %shard_map.69.dens = bf16[32,4,24,128]{3,2,1,0:T(8,128)(2,1)S(1)} custom-call(f32[3]{0:T(128)S(1)} %broadcast_add_fusion.energy, f32[1,512]{1,0:T(1,128)S(1)} %bitcast.40, f32[512,1]{1,0:T(8,128)S(1)} %copy.9.vir_col, bf16[32,2,16,768]{3,2,1,0:T(8,128)(2,1)} %all-to-all-done.1.rows, bf16[512,768]{1,0:T(8,128)(2,1)} %bitcast.11.own, ...), custom_call_target="tpu_custom_call" | custom-call | flops 3623878656 | bytes 3932160 | tf_op jit(solution)/shard_map/pallas_call | solution.py:40
  85.8 0.0 copy-start
  85.8 0.9 copy-done
  86.7 17.2 %all-to-all-start.2 = ((bf16[128,24,128]{2,1,0:T(8,128)(2,1)}), bf16[128,24,128]{2,1,0:T(8,128)(2,1)}, u32[]{:S(2)}, u32[]{:S(2)}) async-start(bf16[128,24,128]{2,1,0:T(8,128)(2,1)} %bitcast.38), calls=%async_computation.2 | async-start | bytes 1572864 | tf_op jit(solution)/shard_map/all_to_all | solution.py:20
  103.9 0.0 copy-start.1
  103.9 1.2 copy-done.1
  105.1 4.0 %shard_map.71 = (f32[64,24,128]{2,1,0:T(8,128)S(1)}, bf16[4,64,24,128]{3,2,1,0:T(8,128)(2,1)S(1)}) custom-call(s32[3]{0:T(128)S(1)} %pad_add_fusion.place, bf16[32,4,24,128]{3,2,1,0:T(8,128)(2,1)S(1)} %copy-done.1, bf16[32,2,16,768]{3,2,1,0:T(8,128)(2,1)} %all-to-all-done.1.rows), custom_call_target="tpu_custom_call" | custom-call | flops 603979776 | bytes 3932160 | tf_op jit(solution)/shard_map/pallas_call | solution.py:40
  109.1 0.0 copy-start.2
  109.1 1.1 slice_bitcast_fusion
  110.2 0.2 copy-done.2
  110.4 1.5 collective-permute-start.7
  111.8 0.7 collective-permute-start.6
  112.5 0.0 collective-permute-start.5
  112.5 0.0 collective-permute-done.1.other_ints
  112.5 15.5 %all-to-all-done.2.moved = bf16[128,24,128]{2,1,0:T(8,128)(2,1)} async-done(((bf16[128,24,128]{2,1,0:T(8,128)(2,1)}), bf16[128,24,128]{2,1,0:T(8,128)(2,1)}, u32[]{:S(2)}, u32[]{:S(2)}) %all-to-all-start.2) | async-done | bytes 786464 | tf_op jit(solution)/shard_map/all_to_all | solution.py:20
  128.0 3.5 %shard_map.70 = f32[4,64,4,128]{3,2,1,0:T(4,128)S(1)} custom-call(s32[3]{0:T(128)S(1)} %pad_add_fusion.place, bf16[128,24,128]{2,1,0:T(8,128)(2,1)} %all-to-all-done.2.moved, bf16[24,64,1024]{2,1,0:T(8,128)(2,1)S(1)} %bitcast.37, bf16[24,64,1024]{2,1,0:T(8,128)(2,1)} %collective-permute-done.1.other_ints), custom_call_target="tpu_custom_call" | custom-call | flops 805306368 | bytes 7864320 | tf_op jit(solution)/shard_map/pallas_call | solution.py:40
  131.5 0.0 copy-start.3
  131.6 1.1 collective-permute-start.4
  132.7 3.0 %collective-permute-start.3 = (f32[64,4,128]{2,1,0:T(4,128)S(1)}, f32[64,4,128]{2,1,0:T(4,128)S(1)}, u32[]{:S(2)}, u32[]{:S(2)}) collective-permute-start(f32[64,4,128]{2,1,0:T(4,128)S(1)} %get-tuple-element.10), channel_id=1, source_target_pairs={{0,8},{8,0},{1,9},{9,1},{2,10},{10,2},{3,11},{11,3},{4,12},{12,4},... | collective-permute-start | bytes 393224 | tf_op jit(solution)/shard_map/ppermute | solution.py:28
  135.7 0.0 collective-permute-done.7.aux_yc
  135.7 0.0 collective-permute-start.2
  135.7 0.0 collective-permute-done.6.aux_y
  135.8 0.0 collective-permute-done.5.aux_c
  135.8 1.5 collective-permute-done.4.lag_yc
  137.2 3.8 %collective-permute-done.3.lag_y = f32[64,4,128]{2,1,0:T(4,128)S(1)} collective-permute-done((f32[64,4,128]{2,1,0:T(4,128)S(1)}, f32[64,4,128]{2,1,0:T(4,128)S(1)}, u32[]{:S(2)}, u32[]{:S(2)}) %collective-permute-start.3) | collective-permute-done | bytes 131104 | tf_op jit(solution)/shard_map/ppermute | solution.py:28
  141.1 0.0 collective-permute-done.2.lag_c
  141.1 0.0 copy-done.3
  141.1 2.1 %shard_map.72 = bf16[64,32,128]{2,1,0:T(8,128)(2,1)} custom-call(f32[64,4,128]{2,1,0:T(4,128)S(1)} %get-tuple-element.12.lag_keep, f32[64,4,128]{2,1,0:T(4,128)S(1)} %collective-permute-done.2.lag_c, f32[64,4,128]{2,1,0:T(4,128)S(1)} %collective-permute-done.3.lag_y, f32[64,4,128]{2,1,0:T(4,128)S(1)} %collective-permute-done.4.lag_yc, ...), custom_call_target="tpu_custom_call" | custom-call | flops 2621440 | bytes 5242880 | tf_op jit(solution)/shard_map/pallas_call | solution.py:40
  143.2 10.3 %all-to-all-start.3 = ((bf16[64,32,128]{2,1,0:T(8,128)(2,1)}), bf16[64,32,128]{2,1,0:T(8,128)(2,1)S(1)}, u32[]{:S(2)}, u32[]{:S(2)}) async-start(bf16[64,32,128]{2,1,0:T(8,128)(2,1)} %shard_map.72), calls=%async_computation.3 | async-start | bytes 1048576 | tf_op jit(solution)/shard_map/all_to_all | solution.py:20
  153.5 18.3 %all-to-all-done.3 = bf16[64,32,128]{2,1,0:T(8,128)(2,1)S(1)} async-done(((bf16[64,32,128]{2,1,0:T(8,128)(2,1)}), bf16[64,32,128]{2,1,0:T(8,128)(2,1)S(1)}, u32[]{:S(2)}, u32[]{:S(2)}) %all-to-all-start.3) | async-done | bytes 524320 | tf_op jit(solution)/shard_map/all_to_all | solution.py:20
  171.7 0.1 convert_reduce_fusion
  171.8 0.6 slice.46
  172.5 0.6 copy.11
  (4 shorter events, 0.1 us)
Async XLA Ops:
  0.6 32.4 %all-to-all-start = ((bf16[32,16,768]{2,1,0:T(8,128)(2,1)}), bf16[32,16,768]{2,1,0:T(8,128)(2,1)S(1)}, u32[]{:S(2)}, u32[]{:S(2)}) async-start(bf16[32,16,768]{2,1,0:T(8,128)(2,1)} %bitcast.10), calls=%async_computation | async-start | bytes 1572864 | tf_op jit(solution)/shard_map/all_to_all | solution.py:20
  35.0 44.1 %all-to-all-start.1 = ((bf16[32,2,16,768]{3,2,1,0:T(8,128)(2,1)}), bf16[32,2,16,768]{3,2,1,0:T(8,128)(2,1)}, u32[]{:S(2)}, u32[]{:S(2)}) async-start(bf16[32,2,16,768]{3,2,1,0:T(8,128)(2,1)} %shard_map.68), calls=%async_computation.1 | async-start | bytes 3145728 | tf_op jit(solution)/shard_map/all_to_all | solution.py:20
  39.7 13.4 %copy-start.5 = (f32[256]{0:T(256)S(1)}, f32[256]{0:T(256)}, u32[]{:S(2)}) copy-start(f32[256]{0:T(256)} %param.6) | copy-start | bytes 3076
  39.7 14.7 %copy-start.4 = (f32[512]{0:T(512)S(1)}, f32[512]{0:T(512)}, u32[]{:S(2)}) copy-start(f32[512]{0:T(512)} %param.7) | copy-start | bytes 6148
  43.3 69.2 %collective-permute-start.1 = (bf16[24,64,1024]{2,1,0:T(8,128)(2,1)S(1)}, bf16[24,64,1024]{2,1,0:T(8,128)(2,1)}, u32[]{:S(2)}, u32[]{:S(2)}) collective-permute-start(bf16[24,64,1024]{2,1,0:T(8,128)(2,1)S(1)} %bitcast.36), channel_id=1, source_target_pairs={{0,1},{1,0},{2,3},{3,2},{4,5},{5,4},{6,7},{7,6},{8,9},{9,8},{10,11... | collective-permute-start | bytes 9437192 | tf_op jit(solution)/shard_map/ppermute | solution.py:24
  51.6 27.5 %collective-permute-start = (bf16[512,768]{1,0:T(8,128)(2,1)}, bf16[512,768]{1,0:T(8,128)(2,1)}, u32[]{:S(2)}, u32[]{:S(2)}) collective-permute-start(bf16[512,768]{1,0:T(8,128)(2,1)} %bitcast.11.own), channel_id=1, source_target_pairs={{0,8},{8,0},{1,9},{9,1},{2,10},{10,2},{3,11},{11,3},{4,12},{12,4},... | collective-permute-start | bytes 2359304 | tf_op jit(solution)/shard_map/ppermute | solution.py:28
  85.8 0.9 copy-start
  86.7 41.4 %all-to-all-start.2 = ((bf16[128,24,128]{2,1,0:T(8,128)(2,1)}), bf16[128,24,128]{2,1,0:T(8,128)(2,1)}, u32[]{:S(2)}, u32[]{:S(2)}) async-start(bf16[128,24,128]{2,1,0:T(8,128)(2,1)} %bitcast.38), calls=%async_computation.2 | async-start | bytes 1572864 | tf_op jit(solution)/shard_map/all_to_all | solution.py:20
  103.9 1.2 copy-start.1
  109.1 1.3 copy-start.2
  110.4 25.3 %collective-permute-start.7 = (bf16[64,24,128]{2,1,0:T(8,128)(2,1)}, bf16[64,24,128]{2,1,0:T(8,128)(2,1)S(1)}, u32[]{:S(2)}, u32[]{:S(2)}) collective-permute-start(bf16[64,24,128]{2,1,0:T(8,128)(2,1)} %get-tuple-element.6), channel_id=1, source_target_pairs={{0,9},{1,8},{8,1},{9,0},{2,11},{3,10},{10,3},{11,2},{4,13},{5,12},... | collective-permute-start | bytes 1179656 | tf_op jit(solution)/shard_map/ppermute | solution.py:32
  111.8 23.9 %collective-permute-start.6 = (bf16[64,24,128]{2,1,0:T(8,128)(2,1)}, bf16[64,24,128]{2,1,0:T(8,128)(2,1)}, u32[]{:S(2)}, u32[]{:S(2)}) collective-permute-start(bf16[64,24,128]{2,1,0:T(8,128)(2,1)} %get-tuple-element.7), channel_id=1, source_target_pairs={{0,8},{8,0},{1,9},{9,1},{2,10},{10,2},{3,11},{11,3},{4,12},{12,4},... | collective-permute-start | bytes 1179656 | tf_op jit(solution)/shard_map/ppermute | solution.py:28
  112.5 23.3 %collective-permute-start.5 = (bf16[64,24,128]{2,1,0:T(8,128)(2,1)}, bf16[64,24,128]{2,1,0:T(8,128)(2,1)}, u32[]{:S(2)}, u32[]{:S(2)}) collective-permute-start(bf16[64,24,128]{2,1,0:T(8,128)(2,1)} %get-tuple-element.8), channel_id=1, source_target_pairs={{0,1},{1,0},{2,3},{3,2},{4,5},{5,4},{6,7},{7,6},{8,9},{9,8},{10,11... | collective-permute-start | bytes 1179656 | tf_op jit(solution)/shard_map/ppermute | solution.py:24
  131.5 9.5 %copy-start.3 = (f32[64,24,128]{2,1,0:T(8,128)S(1)}, f32[64,24,128]{2,1,0:T(8,128)}, u32[]{:S(2)}) copy-start(f32[64,24,128]{2,1,0:T(8,128)} %copy-done.2) | copy-start | bytes 2359300
  131.6 5.6 %collective-permute-start.4 = (f32[64,4,128]{2,1,0:T(4,128)S(1)}, f32[64,4,128]{2,1,0:T(4,128)S(1)}, u32[]{:S(2)}, u32[]{:S(2)}) collective-permute-start(f32[64,4,128]{2,1,0:T(4,128)S(1)} %get-tuple-element.9), channel_id=1, source_target_pairs={{0,9},{1,8},{8,1},{9,0},{2,11},{3,10},{10,3},{11,2},{4,13},{5,12},... | collective-permute-start | bytes 393224 | tf_op jit(solution)/shard_map/ppermute | solution.py:32
  132.7 8.4 %collective-permute-start.3 = (f32[64,4,128]{2,1,0:T(4,128)S(1)}, f32[64,4,128]{2,1,0:T(4,128)S(1)}, u32[]{:S(2)}, u32[]{:S(2)}) collective-permute-start(f32[64,4,128]{2,1,0:T(4,128)S(1)} %get-tuple-element.10), channel_id=1, source_target_pairs={{0,8},{8,0},{1,9},{9,1},{2,10},{10,2},{3,11},{11,3},{4,12},{12,4},... | collective-permute-start | bytes 393224 | tf_op jit(solution)/shard_map/ppermute | solution.py:28
  135.7 5.3 %collective-permute-start.2 = (f32[64,4,128]{2,1,0:T(4,128)S(1)}, f32[64,4,128]{2,1,0:T(4,128)S(1)}, u32[]{:S(2)}, u32[]{:S(2)}) collective-permute-start(f32[64,4,128]{2,1,0:T(4,128)S(1)} %get-tuple-element.11), channel_id=1, source_target_pairs={{0,1},{1,0},{2,3},{3,2},{4,5},{5,4},{6,7},{7,6},{8,9},{9,8},{10,11... | collective-permute-start | bytes 393224 | tf_op jit(solution)/shard_map/ppermute | solution.py:24
  143.2 28.5 %all-to-all-start.3 = ((bf16[64,32,128]{2,1,0:T(8,128)(2,1)}), bf16[64,32,128]{2,1,0:T(8,128)(2,1)S(1)}, u32[]{:S(2)}, u32[]{:S(2)}) async-start(bf16[64,32,128]{2,1,0:T(8,128)(2,1)} %shard_map.72), calls=%async_computation.3 | async-start | bytes 1048576 | tf_op jit(solution)/shard_map/all_to_all | solution.py:20

commit v4 on v3

--- a/solution.py
+++ b/solution.py
@@ -9,8 +9,10 @@
 F32 = jnp.float32
 LANES = 128
 VMEM_BYTES = 40 * 1024 * 1024
-CYC = ("oh", "yl")
-DEST = ("oh", "zl")
+CYC = ("x", "zh", "yh", "yl")
+PLANE = ("x", "yh", "yl", "core")
+DEPTH = ("zh", "zl")
+N_Y = 4
 
 vmem = pl.BlockSpec(memory_space=pltpu.VMEM)
 smem = pl.BlockSpec(memory_space=pltpu.SMEM)
@@ -26,10 +28,6 @@
 
 def swap_yl(x):
     return lax.ppermute(x, "yl", [(0, 1), (1, 0)])
-
-
-def swap_both(x):
-    return lax.ppermute(x, ("yl", "core"), [(i, 3 - i) for i in range(4)])
 
 
 def dot(a, b, ca, cb):
@@ -92,13 +90,13 @@
     lax.fori_loop(0, n_h // 2, body, 0)
 
 
-def aux_kernel(place, dens, rows, keep, send, acc):
+def aux_kernel(place, dens, rows, near, far, acc):
     n_cyc, n_h, aux_blk, lanes = dens.shape
     sub, n_aux = rows.shape[2:]
     per = lanes // sub
-    n_grp = 2 * n_h
+    n_grp = near.shape[1]
     col_blk = n_aux // n_grp
-    yl, core = place[1], place[2]
+    core = place[2]
     pad = jnp.zeros((lanes, lanes - col_blk), BF16)
     for h in range(n_h):
         block = rows[h * per : (h + 1) * per, 0].reshape(lanes, n_aux)
@@ -112,32 +110,35 @@
         else:
             acc[...] += term
 
-    def body(oh, carry):
-        for other in range(2):
-            row = pl.multiple_of((2 * oh + jnp.bitwise_xor(yl, other)) * aux_blk, 8)
-            for g in range(n_grp):
-                value = acc[pl.ds(row, aux_blk), g * lanes : (g + 1) * lanes]
-                cross = jnp.bitwise_xor(core, g % 2)
-                slot = other * 2 + cross
-                send[slot, oh * n_h + g // 2] = value.astype(BF16)
-                if other == 0:
-
-                    @pl.when(cross == 0)
-                    def _():
-                        keep[oh * n_h + g // 2] = value
-
+    def body(xy, carry):
+        base = lax.div(xy, N_Y) * (2 * N_Y) + lax.rem(xy, N_Y)
+        row = pl.multiple_of((base + N_Y * core) * aux_blk, 8)
+        row_far = pl.multiple_of((base + N_Y * (1 - core)) * aux_blk, 8)
+        for g in range(n_grp):
+            cols = slice(g * lanes, (g + 1) * lanes)
+            near[xy, g] = acc[pl.ds(row, aux_blk), cols]
+            far[xy, g] = acc[pl.ds(row_far, aux_blk), cols].astype(BF16)
         return carry
 
     lax.fori_loop(0, n_cyc // 2, body, 0)
+
+
+def fold_kernel(place, near, far, keep, send):
+    n_half = keep.shape[1]
+    yl = place[1]
+    for g in range(n_half):
+        mine = yl * n_half + g
+        other = (1 - yl) * n_half + g
+        keep[:, g] = near[:, mine] + far[:, mine].astype(F32)
+        send[:, g] = (near[:, other] + far[:, other].astype(F32)).astype(BF16)
 
 
 def lag_kernel(place, moved, ints, other_ints, parts, wide, acc):
     n_src, aux_blk, lanes = moved.shape
     n_orb = ints.shape[2]
-    n_dest = parts.shape[1]
     n_zl = parts.shape[2]
     n_cyc = n_src // n_zl
-    shift, yl, core = place[0], place[1], place[2]
+    shift, core = place[0], place[2]
     wide[...] = moved[...].reshape(n_src * aux_blk, lanes).astype(F32)
     for p in range(0, aux_blk, 2):
         left, right = [], []
@@ -152,33 +153,72 @@
             acc[...] += term
     for k in range(n_cyc):
         target = lax.rem(k + shift, n_cyc)
-        other = jnp.bitwise_xor(jnp.bitwise_and(target, 1), yl)
+        zh = lax.rem(lax.div(target, N_Y), 2)
+        xy = lax.div(target, 2 * N_Y) * N_Y + lax.rem(target, N_Y)
         for g in range(n_orb // lanes):
-            slot = other * 2 + jnp.bitwise_xor(core, g % 2)
-            parts[slot, lax.div(target, 2) * n_zl + g // 2] = acc[
-                k * n_zl : (k + 1) * n_zl, g * lanes : (g + 1) * lanes
-            ]
-
-
-def join_kernel(lag_keep, lag_c, lag_y, lag_yc, aux_keep, aux_c, aux_y, aux_yc, out):
-    lag = jnp.concatenate([lag_keep[...] + lag_y[...], lag_c[...] + lag_yc[...]], axis=1)
-    aux = aux_keep[...] + aux_c[...].astype(F32) + aux_y[...].astype(F32) + aux_yc[...].astype(F32)
-    out[...] = jnp.concatenate([lag, aux], axis=1).astype(BF16)
+            parts[xy * 2 + g % 2, zh, g // 2] = acc[k * n_zl : (k + 1) * n_zl, g * lanes : (g + 1) * lanes]
+
+
+def join_kernel(lag, keep, recv, out):
+    n_dest, n_zh, n_zl = lag.shape[:3]
+    pieces = [lag[:, a, b] for a in range(n_zh) for b in range(n_zl)]
+    n_lag = n_zh * n_zl * lag.shape[3]
+    aux_blk, lanes = keep.shape[2:]
+    n_low = keep.shape[1] // 2
+    out[:, :n_lag] = jnp.concatenate(pieces, axis=1).astype(BF16)
+    for xy in range(n_dest // 2):
+        for low in range(n_low):
+            for c in range(2):
+                g = 2 * low + c
+                out[2 * xy + c, n_lag + low * aux_blk : n_lag + (low + 1) * aux_blk] = (
+                    keep[xy, g] + recv[xy, g].astype(F32)
+                ).astype(BF16)
+
+
+def plane_kernel(got, out):
+    n_src = got.shape[0]
+    n_z, n_rows, lanes = out.shape
+    n_zl = n_z // 2
+    n_lag = n_z * n_zl
+    aux_blk = n_rows - 2 * n_zl
+    n_low = (got.shape[1] - n_lag) // aux_blk
+    for c in range(2):
+        total = got[c, :n_lag].astype(F32)
+        for src in range(c + 2, n_src, 2):
+            total = total + got[src, :n_lag].astype(F32)
+        for z in range(n_z):
+            out[z, c * n_zl : (c + 1) * n_zl] = total[z * n_zl : (z + 1) * n_zl]
+        for yl in range(2):
+            first = 2 * yl + c
+            total = got[first, n_lag:].astype(F32)
+            for src in range(first + 4, n_src, 4):
+                total = total + got[src, n_lag:].astype(F32)
+            for low in range(n_low):
+                z = c * n_zl + n_low * yl + low
+                out[z, 2 * n_zl :] = total[low * aux_blk : (low + 1) * aux_blk]
+
+
+def last_kernel(got, aux, lag):
+    total = jnp.sum(got[...], axis=0)
+    n_zl = lag.shape[0] // 2
+    aux[...] = total[2 * n_zl :, : aux.shape[1]]
+    for z in range(n_zl):
+        for c in range(2):
+            lag[2 * z + c : 2 * z + c + 1] = total[c * n_zl + z : c * n_zl + z + 1]
 
 
 def local(b_factors, occ_energy, vir_energy, integrals, window_start):
-    n_cyc = lax.axis_size("oh") * 2
+    n_cyc = lax.axis_size(CYC)
     n_zl = lax.axis_size("zl")
     n_grp = n_zl * 2
     yl = lax.axis_index("yl")
     core = lax.axis_index("core")
-    cyc = lax.axis_index("oh") * 2 + yl
+    cyc = lax.axis_index(CYC)
     grp = lax.axis_index("zl") * 2 + core
     own = b_factors[0]
     n_vir, n_aux = own.shape
     n_orb = integrals.shape[2]
     aux_blk = n_aux // n_cyc
-    col_blk = n_aux // n_grp
     shift = jnp.mod(window_start[0] + 1, n_cyc)
     place = jnp.stack([shift, yl, core]).astype(jnp.int32)
 
@@ -218,14 +258,14 @@
         mate,
         specs=[smem] + [vmem] * 5,
     )
-    n_dest = n_cyc // 2 * n_zl
     moved = exchange_all(dens.reshape(n_cyc * n_zl, aux_blk, LANES), CYC + ("zl",))
 
-    aux_keep, aux_send = call(
+    n_xy = n_cyc // 2
+    near, far = call(
         aux_kernel,
         (
-            jax.ShapeDtypeStruct((n_dest, aux_blk, LANES), F32),
-            jax.ShapeDtypeStruct((4, n_dest, aux_blk, LANES), BF16),
+            jax.ShapeDtypeStruct((n_xy, n_grp, aux_blk, LANES), F32),
+            jax.ShapeDtypeStruct((n_xy, n_grp, aux_blk, LANES), BF16),
         ),
         [pltpu.VMEM((n_aux, n_grp * LANES), F32)],
         2 * n_vir * n_aux * n_aux,
@@ -235,11 +275,25 @@
         rows,
         specs=[smem, vmem, vmem],
     )
-    aux_c, aux_y, aux_yc = swap_cores(aux_send[1]), swap_yl(aux_send[2]), swap_both(aux_send[3])
+    keep, send = call(
+        fold_kernel,
+        (
+            jax.ShapeDtypeStruct((n_xy, n_grp // 2, aux_blk, LANES), F32),
+            jax.ShapeDtypeStruct((n_xy, n_grp // 2, aux_blk, LANES), BF16),
+        ),
+        [],
+        0,
+        9 * n_vir * n_aux,
+        place,
+        near,
+        swap_cores(far),
+        specs=[smem, vmem, vmem],
+    )
+    recv = swap_yl(send)
 
     lag = call(
         lag_kernel,
-        jax.ShapeDtypeStruct((4, n_dest, n_zl, LANES), F32),
+        jax.ShapeDtypeStruct((n_cyc, 2, n_zl, n_zl, LANES), F32),
         [pltpu.VMEM((n_vir * n_aux // LANES, LANES), F32), pltpu.VMEM((n_cyc * n_zl, n_orb), F32)],
         2 * n_vir * n_aux * n_orb,
         2 * n_vir * n_aux * 10,
@@ -249,35 +303,43 @@
         other_ints,
         specs=[smem] + [vmem] * 3,
     )
-    lag_c, lag_y, lag_yc = swap_cores(lag[1]), swap_yl(lag[2]), swap_both(lag[3])
+    n_rows = 2 * n_zl * n_zl + n_zl // 2 * aux_blk
     parts = call(
         join_kernel,
-        jax.ShapeDtypeStruct((n_dest, 2 * n_zl + aux_blk, LANES), BF16),
-        [],
-        10 * n_dest * 32 * LANES,
-        20 * n_dest * 32 * LANES,
-        lag[0],
-        lag_c,
-        lag_y,
-        lag_yc,
-        aux_keep,
-        aux_c,
-        aux_y,
-        aux_yc,
-        specs=[vmem] * 8,
-    )
-    sums = jnp.sum(exchange_all(parts, DEST).astype(F32), axis=0)
-    aux_metric = sums[2 * n_zl :, :col_blk]
-    same, cross = sums[:n_zl], sums[n_zl : 2 * n_zl]
-    low = jnp.where(core == 0, same, cross)
-    high = jnp.where(core == 0, cross, same)
-    lagrangian = jnp.stack([low, high], axis=1).reshape(n_grp, LANES)
+        jax.ShapeDtypeStruct((n_cyc, n_rows, LANES), BF16),
+        [],
+        0,
+        8 * n_cyc * n_rows * LANES,
+        lag,
+        keep,
+        recv,
+        specs=[vmem] * 3,
+    )
+    plane = call(
+        plane_kernel,
+        jax.ShapeDtypeStruct((2 * n_zl, n_grp + aux_blk, LANES), F32),
+        [],
+        n_cyc * n_rows * LANES,
+        2 * n_cyc * n_rows * LANES,
+        exchange_all(parts, PLANE),
+        specs=[vmem],
+    )
+    aux_metric, lagrangian = call(
+        last_kernel,
+        (jax.ShapeDtypeStruct((aux_blk, n_aux // n_grp), F32), jax.ShapeDtypeStruct((n_grp, LANES), F32)),
+        [],
+        0,
+        4 * 2 * n_zl * 32 * LANES,
+        exchange_all(plane, DEPTH),
+        specs=[vmem],
+    )
     return (aux_metric, lagrangian)
 
 
 def solution(mesh):
     n_occ, n_grp = mesh.shape["occ"], mesh.shape["grp"]
-    fine = Mesh(mesh.devices.reshape(n_occ // 2, 2, n_grp // 2, 2), ("oh", "yl", "zl", "core"))
+    sizes = (n_occ // (2 * N_Y), 2, N_Y // 2, 2, n_grp // 2, 2)
+    fine = Mesh(mesh.devices.reshape(sizes), CYC + ("zl", "core"))
     grp = ("zl", "core")
     placed = (P(CYC + grp, None, None), P(), P(), P(grp, CYC, None), P())
     return jax.shard_map(

time: 174 us -> 164 us (0.943)
  blocking collectives: 0 us -> 30.5 us
  waiting for transfers between devices: 80.2 us -> 56.4 us
  starting transfers between devices: 62.7 us -> 47.8 us
    all_to_all x0 -> x2, blocking collectives: none -> 30.5 us  [exchange_all(): return lax.all_to_all(x, axes, split_axis=0, concat_axis=0, tiled=True)]
    all_to_all x4 -> x3, waiting for transfers between devices: 50.9 us -> 30.5 us  [exchange_all(): return lax.all_to_all(x, axes, split_axis=0, concat_axis=0, tiled=True)]
    all_to_all x4 -> x3, starting transfers between devices: 46.7 us -> 36.5 us  [exchange_all(): return lax.all_to_all(x, axes, split_axis=0, concat_axis=0, tiled=True)]
    ppermute x3 -> x2, waiting for transfers between devices: 27.9 us -> 23.9 us  [swap_yl(): return lax.ppermute(x, 'yl', [(0, 1), (1, 0)])]
    ppermute x3 -> x2, starting transfers between devices: 5.17 us -> 2.25 us  [swap_yl(): return lax.ppermute(x, 'yl', [(0, 1), (1, 0)])]
    ppermute x2 -> x0, starting transfers between devices: 2.55 us -> none  [swap_both(): return lax.ppermute(x, ('yl', 'core'), [(i, 3 - i) for i in range(4)])]
    ppermute x3 -> x2, waiting for transfers between devices: 0.01 us -> 1.91 us  [swap_cores(): return lax.ppermute(x, 'core', [(0, 1), (1, 0)])]
    ppermute x3 -> x2, starting transfers between devices: 8.27 us -> 9.1 us  [swap_cores(): return lax.ppermute(x, 'core', [(0, 1), (1, 0)])]
  transfers between devices with their start and end apart: 12 -> 7, of which waited for: 6 -> 4; matrix products, arithmetic and copies ran while one was open for 4% -> 4% of each run, Pallas kernels for 8% -> 9%
where the time goes in v4:
time: 164 us; the launch traced here: 163 us
  waiting for transfers between devices  56.4 us (34%)
  starting transfers between devices  47.8 us (29%)
  blocking collectives  30.5 us (19%)
  Pallas kernels  18.2 us (11%)
  local copies, waits for them, and re-layouts  7.98 us (5%)
    all_to_all x3, starting transfers between devices, exchange_all(): return lax.all_to_all(x, axes, split_axis=0, concat_axis=0, tiled=True)  36.5 us
    all_to_all x3, waiting for transfers between devices, exchange_all(): return lax.all_to_all(x, axes, split_axis=0, concat_axis=0, tiled=True)  30.5 us
    all_to_all x2, blocking collectives, exchange_all(): return lax.all_to_all(x, axes, split_axis=0, concat_axis=0, tiled=True)  30.5 us
    ppermute x2, waiting for transfers between devices, swap_yl(): return lax.ppermute(x, 'yl', [(0, 1), (1, 0)])  23.9 us
    pallas_call x8, Pallas kernels, call(): pl.pallas_call(kernel, out_shape=outs, in_specs=specs, out_specs=jax.tree...  18.2 us
    ppermute x2, starting transfers between devices, swap_cores(): return lax.ppermute(x, 'core', [(0, 1), (1, 0)])  9.1 us
    unnamed x13, local copies, waits for them, and re-layouts  6.58 us
  transfers between devices with their start and end apart: 7, of which 4 were waited for; matrix products, arithmetic and copies ran while one was open for 4% of the time, Pallas kernels for 9%

profile of v4, /device:TPU:1, one launch (start us, length us, event | category | flops | bytes accessed | tf_op | source)
XLA Modules:
  0.0 163.0 jit_solution(11576913811978818707)
XLA Ops:
  0.6 14.5 %all-to-all-start = ((bf16[32,16,768]{2,1,0:T(8,128)(2,1)}), bf16[32,16,768]{2,1,0:T(8,128)(2,1)S(1)}, u32[]{:S(2)}, u32[]{:S(2)}) async-start(bf16[32,16,768]{2,1,0:T(8,128)(2,1)} %bitcast.10), calls=%async_computation | async-start | bytes 1572864 | tf_op jit(solution)/shard_map/all_to_all | solution.py:22
  15.8 0.1 pad_add_fusion.place
  15.9 17.1 %all-to-all-done.spread = bf16[32,16,768]{2,1,0:T(8,128)(2,1)S(1)} async-done(((bf16[32,16,768]{2,1,0:T(8,128)(2,1)}), bf16[32,16,768]{2,1,0:T(8,128)(2,1)S(1)}, u32[]{:S(2)}, u32[]{:S(2)}) %all-to-all-start) | async-done | bytes 786464 | tf_op jit(solution)/shard_map/all_to_all | solution.py:22
  33.0 2.0 %shard_map.68 = bf16[32,2,16,768]{3,2,1,0:T(8,128)(2,1)} custom-call(s32[3]{0:T(128)S(1)} %pad_add_fusion.place, bf16[32,16,768]{2,1,0:T(8,128)(2,1)S(1)} %all-to-all-done.spread), custom_call_target="tpu_custom_call" | custom-call | bytes 3145728 | tf_op jit(solution)/shard_map/pallas_call | solution.py:38
  35.0 4.7 %all-to-all-start.1 = ((bf16[32,2,16,768]{3,2,1,0:T(8,128)(2,1)}), bf16[32,2,16,768]{3,2,1,0:T(8,128)(2,1)}, u32[]{:S(2)}, u32[]{:S(2)}) async-start(bf16[32,2,16,768]{3,2,1,0:T(8,128)(2,1)} %shard_map.68), calls=%async_computation.1 | async-start | bytes 3145728 | tf_op jit(solution)/shard_map/all_to_all | solution.py:22
  39.7 0.0 copy-start.5
  39.7 0.0 copy-start.4
  39.7 3.6 %copy.11 = bf16[64,24,1024]{2,0,1:T(8,128)(2,1)S(1)} copy(bf16[64,24,1024]{2,1,0:T(8,128)(2,1)} %param.8) | data formatting | bytes 6291456 | tf_op args[3]
  43.3 8.3 %collective-permute-start.1 = (bf16[24,64,1024]{2,1,0:T(8,128)(2,1)S(1)}, bf16[24,64,1024]{2,1,0:T(8,128)(2,1)}, u32[]{:S(2)}, u32[]{:S(2)}) collective-permute-start(bf16[24,64,1024]{2,1,0:T(8,128)(2,1)S(1)} %bitcast.17), channel_id=1, source_target_pairs={{0,1},{1,0},{2,3},{3,2},{4,5},{5,4},{6,7},{7,6},{8,9},{9,8},{10,11... | collective-permute-start | bytes 9437192 | tf_op jit(solution)/shard_map/ppermute | solution.py:26
  51.6 1.5 collective-permute-start
  53.0 0.0 copy-done.5
  53.0 0.6 dynamic_slice.3
  53.7 0.1 fusion.3
  53.8 0.6 gather_fusion
  54.4 0.0 copy-done.4
  54.4 0.1 copy.8.vir_col
  54.5 0.6 broadcast_add_fusion.energy
  55.2 23.9 %collective-permute-done.mate = bf16[512,768]{1,0:T(8,128)(2,1)} collective-permute-done((bf16[512,768]{1,0:T(8,128)(2,1)}, bf16[512,768]{1,0:T(8,128)(2,1)}, u32[]{:S(2)}, u32[]{:S(2)}) %collective-permute-start) | collective-permute-done | bytes 786464 | tf_op jit(solution)/shard_map/ppermute | solution.py:30
  79.1 0.0 all-to-all-done.1.rows
  79.1 6.7 %shard_map.69.dens = bf16[32,4,24,128]{3,2,1,0:T(8,128)(2,1)S(1)} custom-call(f32[3]{0:T(128)S(1)} %broadcast_add_fusion.energy, f32[1,512]{1,0:T(1,128)S(1)} %bitcast.21, f32[512,1]{1,0:T(8,128)S(1)} %copy.8.vir_col, bf16[32,2,16,768]{3,2,1,0:T(8,128)(2,1)} %all-to-all-done.1.rows, bf16[512,768]{1,0:T(8,128)(2,1)} %bitcast.11.own, ...), custom_call_target="tpu_custom_call" | custom-call | flops 3623878656 | bytes 3932160 | tf_op jit(solution)/shard_map/pallas_call | solution.py:38
  85.8 0.0 copy-start
  85.8 0.9 copy-done
  86.7 17.2 %all-to-all-start.2 = ((bf16[128,24,128]{2,1,0:T(8,128)(2,1)}), bf16[128,24,128]{2,1,0:T(8,128)(2,1)}, u32[]{:S(2)}, u32[]{:S(2)}) async-start(bf16[128,24,128]{2,1,0:T(8,128)(2,1)} %bitcast.19), calls=%async_computation.2 | async-start | bytes 1572864 | tf_op jit(solution)/shard_map/all_to_all | solution.py:22
  104.0 0.0 copy-start.1
  104.0 1.2 copy-done.1
  105.1 3.7 %shard_map.71 = (f32[16,8,24,128]{3,2,1,0:T(8,128)S(1)}, bf16[16,8,24,128]{3,2,1,0:T(8,128)(2,1)S(1)}) custom-call(s32[3]{0:T(128)S(1)} %pad_add_fusion.place, bf16[32,4,24,128]{3,2,1,0:T(8,128)(2,1)S(1)} %copy-done.1, bf16[32,2,16,768]{3,2,1,0:T(8,128)(2,1)} %all-to-all-done.1.rows), custom_call_target="tpu_custom_call" | custom-call | flops 603979776 | bytes 3932160 | tf_op jit(solution)/shard_map/pallas_call | solution.py:38
  108.8 0.9 collective-permute-start.2
  109.6 1.9 %collective-permute-done.2.far = bf16[16,8,24,128]{3,2,1,0:T(8,128)(2,1)S(1)} collective-permute-done((bf16[16,8,24,128]{3,2,1,0:T(8,128)(2,1)S(1)}, bf16[16,8,24,128]{3,2,1,0:T(8,128)(2,1)S(1)}, u32[]{:S(2)}, u32[]{:S(2)}) %collective-permute-start.2) | collective-permute-done | bytes 786464 | tf_op jit(solution)/shard_map/ppermute | solution.py:26
  111.6 1.4 shard_map.72
  113.0 0.0 copy-start.2
  113.0 0.9 copy-done.2
  113.9 0.8 collective-permute-start.3
  114.7 0.0 collective-permute-done.1.other_ints
  114.7 13.4 %all-to-all-done.2.moved = bf16[128,24,128]{2,1,0:T(8,128)(2,1)} async-done(((bf16[128,24,128]{2,1,0:T(8,128)(2,1)}), bf16[128,24,128]{2,1,0:T(8,128)(2,1)}, u32[]{:S(2)}, u32[]{:S(2)}) %all-to-all-start.2) | async-done | bytes 786464 | tf_op jit(solution)/shard_map/all_to_all | solution.py:22
  128.1 0.0 copy-start.3
  128.1 3.6 %shard_map.70.lag = f32[32,2,4,4,128]{4,3,2,1,0:T(4,128)S(1)} custom-call(s32[3]{0:T(128)S(1)} %pad_add_fusion.place, bf16[128,24,128]{2,1,0:T(8,128)(2,1)} %all-to-all-done.2.moved, bf16[24,64,1024]{2,1,0:T(8,128)(2,1)S(1)} %bitcast.18, bf16[24,64,1024]{2,1,0:T(8,128)(2,1)} %collective-permute-done.1.other_ints), custom_call_target="tpu_custom_call" | custom-call | flops 805306368 | bytes 7864320 | tf_op jit(solution)/shard_map/pallas_call | solution.py:38
  131.7 0.0 collective-permute-done.3.recv
  131.7 0.0 copy-done.3
  131.8 0.1 shard_map.73
  131.9 18.7 %all_to_all.25.got = bf16[32,80,128]{2,1,0:T(8,128)(2,1)S(1)} all-to-all(bf16[32,80,128]{2,1,0:T(8,128)(2,1)S(1)} %shard_map.73), channel_id=1, replica_groups=mesh['x'=4,'zh'=2,'yh'=2,'yl'=2,'zl'=4,'core'=2] {'x','yh','yl','core'}, dimensions={0} | all-to-all | bytes 1310720 | tf_op jit(solution)/shard_map/all_to_all | solution.py:22
  150.5 0.1 shard_map.74
  150.6 11.8 %all_to_all.26.got = f32[8,32,128]{2,1,0:T(8,128)S(1)} all-to-all(f32[8,32,128]{2,1,0:T(8,128)S(1)} %shard_map.74), channel_id=1, replica_groups=mesh['x'=4,'zh'=2,'yh'=2,'yl'=2,'zl'=4,'core'=2] {'zh','zl'}, dimensions={0} | all-to-all | bytes 262144 | tf_op jit(solution)/shard_map/all_to_all | solution.py:22
  162.4 0.6 shard_map.75
  (1 shorter events, 0.0 us)
Async XLA Ops:
  0.6 32.4 %all-to-all-start = ((bf16[32,16,768]{2,1,0:T(8,128)(2,1)}), bf16[32,16,768]{2,1,0:T(8,128)(2,1)S(1)}, u32[]{:S(2)}, u32[]{:S(2)}) async-start(bf16[32,16,768]{2,1,0:T(8,128)(2,1)} %bitcast.10), calls=%async_computation | async-start | bytes 1572864 | tf_op jit(solution)/shard_map/all_to_all | solution.py:22
  35.0 44.1 %all-to-all-start.1 = ((bf16[32,2,16,768]{3,2,1,0:T(8,128)(2,1)}), bf16[32,2,16,768]{3,2,1,0:T(8,128)(2,1)}, u32[]{:S(2)}, u32[]{:S(2)}) async-start(bf16[32,2,16,768]{3,2,1,0:T(8,128)(2,1)} %shard_map.68), calls=%async_computation.1 | async-start | bytes 3145728 | tf_op jit(solution)/shard_map/all_to_all | solution.py:22
  39.7 13.4 %copy-start.5 = (f32[256]{0:T(256)S(1)}, f32[256]{0:T(256)}, u32[]{:S(2)}) copy-start(f32[256]{0:T(256)} %param.6) | copy-start | bytes 3076
  39.7 14.7 %copy-start.4 = (f32[512]{0:T(512)S(1)}, f32[512]{0:T(512)}, u32[]{:S(2)}) copy-start(f32[512]{0:T(512)} %param.7) | copy-start | bytes 6148
  43.3 71.3 %collective-permute-start.1 = (bf16[24,64,1024]{2,1,0:T(8,128)(2,1)S(1)}, bf16[24,64,1024]{2,1,0:T(8,128)(2,1)}, u32[]{:S(2)}, u32[]{:S(2)}) collective-permute-start(bf16[24,64,1024]{2,1,0:T(8,128)(2,1)S(1)} %bitcast.17), channel_id=1, source_target_pairs={{0,1},{1,0},{2,3},{3,2},{4,5},{5,4},{6,7},{7,6},{8,9},{9,8},{10,11... | collective-permute-start | bytes 9437192 | tf_op jit(solution)/shard_map/ppermute | solution.py:26
  51.6 27.5 %collective-permute-start = (bf16[512,768]{1,0:T(8,128)(2,1)}, bf16[512,768]{1,0:T(8,128)(2,1)}, u32[]{:S(2)}, u32[]{:S(2)}) collective-permute-start(bf16[512,768]{1,0:T(8,128)(2,1)} %bitcast.11.own), channel_id=1, source_target_pairs={{0,8},{8,0},{1,9},{9,1},{2,10},{10,2},{3,11},{11,3},{4,12},{12,4},... | collective-permute-start | bytes 2359304 | tf_op jit(solution)/shard_map/ppermute | solution.py:30
  85.8 0.9 copy-start
  86.7 41.4 %all-to-all-start.2 = ((bf16[128,24,128]{2,1,0:T(8,128)(2,1)}), bf16[128,24,128]{2,1,0:T(8,128)(2,1)}, u32[]{:S(2)}, u32[]{:S(2)}) async-start(bf16[128,24,128]{2,1,0:T(8,128)(2,1)} %bitcast.19), calls=%async_computation.2 | async-start | bytes 1572864 | tf_op jit(solution)/shard_map/all_to_all | solution.py:22
  104.0 1.2 copy-start.1
  108.8 2.8 %collective-permute-start.2 = (bf16[16,8,24,128]{3,2,1,0:T(8,128)(2,1)S(1)}, bf16[16,8,24,128]{3,2,1,0:T(8,128)(2,1)S(1)}, u32[]{:S(2)}, u32[]{:S(2)}) collective-permute-start(bf16[16,8,24,128]{3,2,1,0:T(8,128)(2,1)S(1)} %get-tuple-element.7), channel_id=1, source_target_pairs={{0,1},{1,0},{2,3},{3,2},{4,5},{5,4},{6,7},{7,6},{8,9},{9,8},{10,11... | collective-permute-start | bytes 2359304 | tf_op jit(solution)/shard_map/ppermute | solution.py:26
  113.0 0.9 copy-start.2
  113.9 17.9 %collective-permute-start.3 = (bf16[16,4,24,128]{3,2,1,0:T(8,128)(2,1)}, bf16[16,4,24,128]{3,2,1,0:T(8,128)(2,1)S(1)}, u32[]{:S(2)}, u32[]{:S(2)}) collective-permute-start(bf16[16,4,24,128]{3,2,1,0:T(8,128)(2,1)} %get-tuple-element.9), channel_id=1, source_target_pairs={{0,8},{8,0},{1,9},{9,1},{2,10},{10,2},{3,11},{11,3},{4,12},{12,4},... | collective-permute-start | bytes 1179656 | tf_op jit(solution)/shard_map/ppermute | solution.py:30
  128.1 3.7 %copy-start.3 = (f32[16,4,24,128]{3,2,1,0:T(8,128)S(1)}, f32[16,4,24,128]{3,2,1,0:T(8,128)}, u32[]{:S(2)}) copy-start(f32[16,4,24,128]{3,2,1,0:T(8,128)} %copy-done.2) | copy-start | bytes 2359300

commit v5 on v4

--- a/solution.py
+++ b/solution.py
@@ -46,7 +46,8 @@
     )(*args)
 
 
-def turn_kernel(place, spread, out):
+def turn_kernel(place, spread, mate, out):
+    del mate
     n_cyc = spread.shape[0]
     shift = place[0]
 
@@ -237,7 +238,8 @@
         8 * n_vir * n_aux,
         place,
         spread,
-        specs=[smem, vmem],
+        mate,
+        specs=[smem, vmem, pl.BlockSpec(memory_space=pl.ANY)],
     )
     rows = exchange_all(turned, CYC)
 

time: 164 us -> 180 us (1.098)
  local copies, waits for them, and re-layouts: 7.98 us -> 14.3 us
  starting transfers between devices: 47.8 us -> 54 us
  waiting for transfers between devices: 56.4 us -> 58.6 us
    all_to_all x3, starting transfers between devices: 36.5 us -> 48.9 us  [exchange_all(): return lax.all_to_all(x, axes, split_axis=0, concat_axis=0, tiled=True)]
    unnamed x13 -> x25, local copies, waits for them, and re-layouts: 6.58 us -> 12.9 us
    ppermute x2, starting transfers between devices: 9.1 us -> 3 us  [swap_cores(): return lax.ppermute(x, 'core', [(0, 1), (1, 0)])]
    all_to_all x3, waiting for transfers between devices: 30.5 us -> 32.3 us  [exchange_all(): return lax.all_to_all(x, axes, split_axis=0, concat_axis=0, tiled=True)]
  transfers between devices with their start and end apart: 7 -> 7, of which waited for: 4 -> 4; matrix products, arithmetic and copies ran while one was open for 4% -> 3% of each run, Pallas kernels for 9% -> 8%
where the time goes in v5:
time: 180 us; the launch traced here: 179 us
  waiting for transfers between devices  58.6 us (33%)
  starting transfers between devices  54 us (30%)
  blocking collectives  32.3 us (18%)
  Pallas kernels  17.8 us (10%)
  local copies, waits for them, and re-layouts  14.3 us (8%)
    all_to_all x3, starting transfers between devices, exchange_all(): return lax.all_to_all(x, axes, split_axis=0, concat_axis=0, tiled=True)  48.9 us
    all_to_all x3, waiting for transfers between devices, exchange_all(): return lax.all_to_all(x, axes, split_axis=0, concat_axis=0, tiled=True)  32.3 us
    all_to_all x2, blocking collectives, exchange_all(): return lax.all_to_all(x, axes, split_axis=0, concat_axis=0, tiled=True)  32.3 us
    ppermute x2, waiting for transfers between devices, swap_yl(): return lax.ppermute(x, 'yl', [(0, 1), (1, 0)])  24.3 us
    pallas_call x8, Pallas kernels, call(): pl.pallas_call(kernel, out_shape=outs, in_specs=specs, out_specs=jax.tree...  17.8 us
    unnamed x25, local copies, waits for them, and re-layouts  12.9 us
  transfers between devices with their start and end apart: 7, of which 4 were waited for; matrix products, arithmetic and copies ran while one was open for 3% of the time, Pallas kernels for 8%

profile of v5, /device:TPU:1, one launch (start us, length us, event | category | flops | bytes accessed | tf_op | source)
XLA Modules:
  0.0 179.3 jit_solution(18212503112061790727)
XLA Ops:
  0.6 14.5 %all-to-all-start = ((bf16[32,16,768]{2,1,0:T(8,128)(2,1)}), bf16[32,16,768]{2,1,0:T(8,128)(2,1)S(1)}, u32[]{:S(2)}, u32[]{:S(2)}) async-start(bf16[32,16,768]{2,1,0:T(8,128)(2,1)} %bitcast.20), calls=%async_computation | async-start | bytes 1572864 | tf_op jit(solution)/shard_map/all_to_all | solution.py:22
  15.1 1.3 collective-permute-start
  17.1 0.1 pad_add_fusion.place
  17.2 24.3 %collective-permute-done.mate = bf16[512,768]{1,0:T(8,128)(2,1)S(1)} collective-permute-done((bf16[512,768]{1,0:T(8,128)(2,1)}, bf16[512,768]{1,0:T(8,128)(2,1)S(1)}, u32[]{:S(2)}, u32[]{:S(2)}) %collective-permute-start) | collective-permute-done | bytes 786464 | tf_op jit(solution)/shard_map/ppermute | solution.py:30
  41.5 0.0 copy-start.7
  41.5 0.9 copy-done.7
  42.4 0.0 all-to-all-done.spread
  42.4 0.0 copy-start.2
  42.4 0.9 copy-done.2
  43.3 0.0 copy-start.3
  43.3 1.1 copy-done.3
  44.4 0.0 copy-start.8
  44.4 1.1 copy-done.8
  45.6 2.0 %shard_map.68 = bf16[32,2,16,768]{3,2,1,0:T(8,128)(2,1)} custom-call(s32[3]{0:T(128)S(1)} %pad_add_fusion.place, bf16[32,16,768]{2,1,0:T(8,128)(2,1)S(1)} %copy-done.3, bf16[512,768]{1,0:T(8,128)(2,1)S(1)} %copy-done.8), custom_call_target="tpu_custom_call" | custom-call | bytes 3145728 | tf_op jit(solution)/shard_map/pallas_call | solution.py:38
  47.5 12.6 %all-to-all-start.1 = ((bf16[32,2,16,768]{3,2,1,0:T(8,128)(2,1)}), bf16[32,2,16,768]{3,2,1,0:T(8,128)(2,1)}, u32[]{:S(2)}, u32[]{:S(2)}) async-start(bf16[32,2,16,768]{3,2,1,0:T(8,128)(2,1)} %shard_map.68), calls=%async_computation.1 | async-start | bytes 3145728 | tf_op jit(solution)/shard_map/all_to_all | solution.py:22
  60.1 0.0 copy-start.11
  60.1 0.0 copy-start.10
  60.2 3.6 %copy.11 = bf16[64,24,1024]{2,0,1:T(8,128)(2,1)S(1)} copy(bf16[64,24,1024]{2,1,0:T(8,128)(2,1)} %param.8) | data formatting | bytes 6291456 | tf_op args[3]
  63.8 1.0 collective-permute-start.1
  64.8 0.0 copy-done.11
  64.8 0.7 dynamic_slice.3
  65.5 0.1 fusion.3
  65.6 0.6 gather_fusion
  66.2 0.0 copy-done.10
  66.2 0.1 copy.8.vir_col
  66.4 0.7 broadcast_add_fusion.energy
  67.1 21.3 %all-to-all-done.1.rows = bf16[32,2,16,768]{3,2,1,0:T(8,128)(2,1)} async-done(((bf16[32,2,16,768]{3,2,1,0:T(8,128)(2,1)}), bf16[32,2,16,768]{3,2,1,0:T(8,128)(2,1)}, u32[]{:S(2)}, u32[]{:S(2)}) %all-to-all-start.1) | async-done | bytes 1572896 | tf_op jit(solution)/shard_map/all_to_all | solution.py:22
  88.4 0.0 copy-start.4
  88.4 1.1 copy-done.4
  89.5 0.0 copy-start.9
  89.5 1.1 copy-done.9
  90.6 6.3 %shard_map.69.dens = bf16[32,4,24,128]{3,2,1,0:T(8,128)(2,1)S(1)} custom-call(f32[3]{0:T(128)S(1)} %broadcast_add_fusion.energy, f32[1,512]{1,0:T(1,128)S(1)} %bitcast.24, f32[512,1]{1,0:T(8,128)S(1)} %copy.8.vir_col, bf16[32,2,16,768]{3,2,1,0:T(8,128)(2,1)} %all-to-all-done.1.rows, bf16[512,768]{1,0:T(8,128)(2,1)S(1)} %bitcast.22, ...), custom_call_target="tpu_custom_call" | custom-call | flops 3623878656 | bytes 3932160 | tf_op jit(solution)/shard_map/pallas_call | solution.py:38
  96.9 0.0 copy-start
  97.0 0.9 copy-done
  97.8 21.8 %all-to-all-start.2 = ((bf16[128,24,128]{2,1,0:T(8,128)(2,1)}), bf16[128,24,128]{2,1,0:T(8,128)(2,1)}, u32[]{:S(2)}, u32[]{:S(2)}) async-start(bf16[128,24,128]{2,1,0:T(8,128)(2,1)} %bitcast.19), calls=%async_computation.2 | async-start | bytes 1572864 | tf_op jit(solution)/shard_map/all_to_all | solution.py:22
  119.7 0.0 copy-start.1
  119.7 1.2 copy-done.1
  120.8 3.6 %shard_map.71 = (f32[16,8,24,128]{3,2,1,0:T(8,128)S(1)}, bf16[16,8,24,128]{3,2,1,0:T(8,128)(2,1)S(1)}) custom-call(s32[3]{0:T(128)S(1)} %pad_add_fusion.place, bf16[32,4,24,128]{3,2,1,0:T(8,128)(2,1)S(1)} %copy-done.1, bf16[32,2,16,768]{3,2,1,0:T(8,128)(2,1)} %all-to-all-done.1.rows), custom_call_target="tpu_custom_call" | custom-call | flops 603979776 | bytes 3932160 | tf_op jit(solution)/shard_map/pallas_call | solution.py:38
  124.5 2.0 %collective-permute-start.2 = (bf16[16,8,24,128]{3,2,1,0:T(8,128)(2,1)S(1)}, bf16[16,8,24,128]{3,2,1,0:T(8,128)(2,1)S(1)}, u32[]{:S(2)}, u32[]{:S(2)}) collective-permute-start(bf16[16,8,24,128]{3,2,1,0:T(8,128)(2,1)S(1)} %get-tuple-element.7), channel_id=1, source_target_pairs={{0,1},{1,0},{2,3},{3,2},{4,5},{5,4},{6,7},{7,6},{8,9},{9,8},{10,11... | collective-permute-start | bytes 2359304 | tf_op jit(solution)/shard_map/ppermute | solution.py:26
  126.5 1.9 %collective-permute-done.2.far = bf16[16,8,24,128]{3,2,1,0:T(8,128)(2,1)S(1)} collective-permute-done((bf16[16,8,24,128]{3,2,1,0:T(8,128)(2,1)S(1)}, bf16[16,8,24,128]{3,2,1,0:T(8,128)(2,1)S(1)}, u32[]{:S(2)}, u32[]{:S(2)}) %collective-permute-start.2) | collective-permute-done | bytes 786464 | tf_op jit(solution)/shard_map/ppermute | solution.py:26
  128.4 1.4 shard_map.72
  129.8 0.0 copy-start.5
  129.8 0.9 copy-done.5
  130.7 0.8 collective-permute-start.3
  131.5 0.0 collective-permute-done.1.other_ints
  131.5 11.0 %all-to-all-done.2.moved = bf16[128,24,128]{2,1,0:T(8,128)(2,1)} async-done(((bf16[128,24,128]{2,1,0:T(8,128)(2,1)}), bf16[128,24,128]{2,1,0:T(8,128)(2,1)}, u32[]{:S(2)}, u32[]{:S(2)}) %all-to-all-start.2) | async-done | bytes 786464 | tf_op jit(solution)/shard_map/all_to_all | solution.py:22
  142.5 0.0 copy-start.6
  142.5 3.6 %shard_map.70.lag = f32[32,2,4,4,128]{4,3,2,1,0:T(4,128)S(1)} custom-call(s32[3]{0:T(128)S(1)} %pad_add_fusion.place, bf16[128,24,128]{2,1,0:T(8,128)(2,1)} %all-to-all-done.2.moved, bf16[24,64,1024]{2,1,0:T(8,128)(2,1)S(1)} %bitcast.18, bf16[24,64,1024]{2,1,0:T(8,128)(2,1)} %collective-permute-done.1.other_ints), custom_call_target="tpu_custom_call" | custom-call | flops 805306368 | bytes 7864320 | tf_op jit(solution)/shard_map/pallas_call | solution.py:38
  146.2 0.0 collective-permute-done.3.recv
  146.2 0.0 copy-done.6
  146.2 0.1 shard_map.73
  146.3 19.9 %all_to_all.25.got = bf16[32,80,128]{2,1,0:T(8,128)(2,1)S(1)} all-to-all(bf16[32,80,128]{2,1,0:T(8,128)(2,1)S(1)} %shard_map.73), channel_id=1, replica_groups=mesh['x'=4,'zh'=2,'yh'=2,'yl'=2,'zl'=4,'core'=2] {'x','yh','yl','core'}, dimensions={0} | all-to-all | bytes 1310720 | tf_op jit(solution)/shard_map/all_to_all | solution.py:22
  166.2 0.1 shard_map.74
  166.3 12.3 %all_to_all.26.got = f32[8,32,128]{2,1,0:T(8,128)S(1)} all-to-all(f32[8,32,128]{2,1,0:T(8,128)S(1)} %shard_map.74), channel_id=1, replica_groups=mesh['x'=4,'zh'=2,'yh'=2,'yl'=2,'zl'=4,'core'=2] {'zh','zl'}, dimensions={0} | all-to-all | bytes 262144 | tf_op jit(solution)/shard_map/all_to_all | solution.py:22
  178.7 0.6 shard_map.75
  (1 shorter events, 0.0 us)
Async XLA Ops:
  0.6 41.8 %all-to-all-start = ((bf16[32,16,768]{2,1,0:T(8,128)(2,1)}), bf16[32,16,768]{2,1,0:T(8,128)(2,1)S(1)}, u32[]{:S(2)}, u32[]{:S(2)}) async-start(bf16[32,16,768]{2,1,0:T(8,128)(2,1)} %bitcast.20), calls=%async_computation | async-start | bytes 1572864 | tf_op jit(solution)/shard_map/all_to_all | solution.py:22
  15.1 26.4 %collective-permute-start = (bf16[512,768]{1,0:T(8,128)(2,1)}, bf16[512,768]{1,0:T(8,128)(2,1)S(1)}, u32[]{:S(2)}, u32[]{:S(2)}) collective-permute-start(bf16[512,768]{1,0:T(8,128)(2,1)} %bitcast.21), channel_id=1, source_target_pairs={{0,8},{8,0},{1,9},{9,1},{2,10},{10,2},{3,11},{11,3},{4,12},{12,4},... | collective-permute-start | bytes 2359304 | tf_op jit(solution)/shard_map/ppermute | solution.py:30
  41.5 0.9 copy-start.7
  42.4 0.9 copy-start.2
  43.3 1.1 copy-start.3
  44.4 1.1 copy-start.8
  47.5 40.8 %all-to-all-start.1 = ((bf16[32,2,16,768]{3,2,1,0:T(8,128)(2,1)}), bf16[32,2,16,768]{3,2,1,0:T(8,128)(2,1)}, u32[]{:S(2)}, u32[]{:S(2)}) async-start(bf16[32,2,16,768]{3,2,1,0:T(8,128)(2,1)} %shard_map.68), calls=%async_computation.1 | async-start | bytes 3145728 | tf_op jit(solution)/shard_map/all_to_all | solution.py:22
  60.1 4.7 %copy-start.11 = (f32[256]{0:T(256)S(1)}, f32[256]{0:T(256)}, u32[]{:S(2)}) copy-start(f32[256]{0:T(256)} %param.6) | copy-start | bytes 3076
  60.1 6.1 %copy-start.10 = (f32[512]{0:T(512)S(1)}, f32[512]{0:T(512)}, u32[]{:S(2)}) copy-start(f32[512]{0:T(512)} %param.7) | copy-start | bytes 6148
  63.8 67.7 %collective-permute-start.1 = (bf16[24,64,1024]{2,1,0:T(8,128)(2,1)S(1)}, bf16[24,64,1024]{2,1,0:T(8,128)(2,1)}, u32[]{:S(2)}, u32[]{:S(2)}) collective-permute-start(bf16[24,64,1024]{2,1,0:T(8,128)(2,1)S(1)} %bitcast.17), channel_id=1, source_target_pairs={{0,1},{1,0},{2,3},{3,2},{4,5},{5,4},{6,7},{7,6},{8,9},{9,8},{10,11... | collective-permute-start | bytes 9437192 | tf_op jit(solution)/shard_map/ppermute | solution.py:26
  88.4 1.1 copy-start.4
  89.5 1.1 copy-start.9
  96.9 0.9 copy-start
  97.8 44.7 %all-to-all-start.2 = ((bf16[128,24,128]{2,1,0:T(8,128)(2,1)}), bf16[128,24,128]{2,1,0:T(8,128)(2,1)}, u32[]{:S(2)}, u32[]{:S(2)}) async-start(bf16[128,24,128]{2,1,0:T(8,128)(2,1)} %bitcast.19), calls=%async_computation.2 | async-start | bytes 1572864 | tf_op jit(solution)/shard_map/all_to_all | solution.py:22
  119.7 1.2 copy-start.1
  124.5 3.9 %collective-permute-start.2 = (bf16[16,8,24,128]{3,2,1,0:T(8,128)(2,1)S(1)}, bf16[16,8,24,128]{3,2,1,0:T(8,128)(2,1)S(1)}, u32[]{:S(2)}, u32[]{:S(2)}) collective-permute-start(bf16[16,8,24,128]{3,2,1,0:T(8,128)(2,1)S(1)} %get-tuple-element.7), channel_id=1, source_target_pairs={{0,1},{1,0},{2,3},{3,2},{4,5},{5,4},{6,7},{7,6},{8,9},{9,8},{10,11... | collective-permute-start | bytes 2359304 | tf_op jit(solution)/shard_map/ppermute | solution.py:26
  129.8 0.9 copy-start.5
  130.7 15.5 %collective-permute-start.3 = (bf16[16,4,24,128]{3,2,1,0:T(8,128)(2,1)}, bf16[16,4,24,128]{3,2,1,0:T(8,128)(2,1)S(1)}, u32[]{:S(2)}, u32[]{:S(2)}) collective-permute-start(bf16[16,4,24,128]{3,2,1,0:T(8,128)(2,1)} %get-tuple-element.9), channel_id=1, source_target_pairs={{0,8},{8,0},{1,9},{9,1},{2,10},{10,2},{3,11},{11,3},{4,12},{12,4},... | collective-permute-start | bytes 1179656 | tf_op jit(solution)/shard_map/ppermute | solution.py:30
  142.5 3.7 %copy-start.6 = (f32[16,4,24,128]{3,2,1,0:T(8,128)S(1)}, f32[16,4,24,128]{3,2,1,0:T(8,128)}, u32[]{:S(2)}) copy-start(f32[16,4,24,128]{3,2,1,0:T(8,128)} %copy-done.5) | copy-start | bytes 2359300

commit v6 on v4

--- a/solution.py
+++ b/solution.py
@@ -9,13 +9,17 @@
 F32 = jnp.float32
 LANES = 128
 VMEM_BYTES = 40 * 1024 * 1024
+PAIR_BYTES = 60 * 1024 * 1024
 CYC = ("x", "zh", "yh", "yl")
 PLANE = ("x", "yh", "yl", "core")
 DEPTH = ("zh", "zl")
 N_Y = 4
+N_STEP = 2
+N_LOAD = 4
 
 vmem = pl.BlockSpec(memory_space=pltpu.VMEM)
 smem = pl.BlockSpec(memory_space=pltpu.SMEM)
+hbm = pl.BlockSpec(memory_space=pltpu.HBM)
 
 
 def exchange_all(x, axes):
@@ -34,60 +38,74 @@
     return lax.dot_general(a, b, (((ca,), (cb,)), ((), ())), preferred_element_type=F32)
 
 
-def call(kernel, outs, scratch, flops, nbytes, *args, specs):
+def call(kernel, outs, scratch, flops, nbytes, *args, specs, out_spec=vmem, grant=VMEM_BYTES):
     return pl.pallas_call(
         kernel,
         out_shape=outs,
         in_specs=specs,
-        out_specs=jax.tree.map(lambda _: vmem, outs),
+        out_specs=jax.tree.map(lambda _: out_spec, outs),
         scratch_shapes=scratch,
-        compiler_params=pltpu.CompilerParams(vmem_limit_bytes=VMEM_BYTES),
+        compiler_params=pltpu.CompilerParams(vmem_limit_bytes=grant),
         cost_estimate=pl.CostEstimate(flops=flops, bytes_accessed=nbytes, transcendentals=0),
     )(*args)
 
 
-def turn_kernel(place, spread, out):
-    n_cyc = spread.shape[0]
+def turn_kernel(place, spread, out, sems):
+    n_pair = spread.shape[0]
+    n_cyc = 2 * n_pair
     shift = place[0]
-
-    def body(pair, carry):
-        for odd in range(2):
-            d = 2 * pair + odd
-            out[d, 0] = spread[lax.rem(d + shift, n_cyc)]
-            out[d, 1] = spread[lax.rem(d + (2 * odd - 1) + n_cyc, n_cyc)]
-        return carry
-
-    lax.fori_loop(0, n_cyc // 2, body, 0)
-
-
-def pair_kernel(energy, vir_row, vir_col, rows, own, mate, out):
+    copies = []
+
+    def copy(src, dst):
+        copies.append(pltpu.make_async_copy(src, dst, sems.at[len(copies)]))
+        copies[-1].start()
+
+    last = n_pair - 1
+    copy(spread.at[pl.ds(1, last), 0], out.at[pl.ds(0, last), 1, 1])
+    copy(spread.at[0, 0], out.at[last, 1, 1])
+    copy(spread.at[pl.ds(0, last), 1], out.at[pl.ds(1, last), 0, 1])
+    copy(spread.at[last, 1], out.at[0, 0, 1])
+    for d in range(n_cyc):
+        src = lax.rem(d + shift, n_cyc)
+        copy(spread.at[lax.div(src, 2), lax.rem(src, 2)], out.at[d // 2, d % 2, 0])
+    for c in copies:
+        c.wait()
+
+
+def pair_kernel(energy, vir_row, vir_col, rows_any, own_any, mate_any, out_any, turned, far, own, mate, out, sems):
     n_cyc, n_h, aux_blk, lanes = out.shape
     n_vir, n_aux = own.shape
-    sub = rows.shape[2]
-    blk = 2 * lanes
-    rows_i = rows[:, 0].reshape(n_vir, n_aux)
-    far = rows[:, 1].reshape(n_vir, n_aux)
-
-    def body(step, carry):
-        start = pl.multiple_of(step * blk, blk)
-        chunk = pl.ds(step * (blk // sub), blk // sub)
-        block_i = rows[chunk, 0].reshape(blk, n_aux)
-        block_far = rows[chunk, 1].reshape(blk, n_aux)
-        vir_sum = vir_col[pl.ds(start, blk), :] + vir_row[...]
+    sub = turned.shape[1]
+    blk = n_vir // N_STEP
+    per = blk // lanes
+    pairs = ((rows_any.at[:, 0], turned), (own_any, own), (mate_any, mate), (rows_any.at[:, 1], far))
+    loads = [pltpu.make_async_copy(src, dst, sems.at[n]) for n, (src, dst) in enumerate(pairs)]
+    for load in loads:
+        load.start()
+    loads[0].wait()
+    rows_i = turned[...].reshape(n_vir, n_aux)
+    stores = []
+    for step in range(N_STEP):
+        chunk = slice(step * blk, (step + 1) * blk)
+        vir_sum = vir_col[chunk, :] + vir_row[...]
+        block_i = rows_i[chunk]
         total = jnp.zeros((blk, n_aux), F32)
-        for t, (block_j, rows_j) in enumerate(
-            ((own[pl.ds(start, blk), :], own[...]), (mate[pl.ds(start, blk), :], mate[...]), (block_far, far))
-        ):
+        for t in range(3):
+            if step == 0:
+                loads[t + 1].wait()
+            rows_j = (own, mate, far)[t][...].reshape(n_vir, n_aux)
             inter = dot(block_i, rows_j, 1, 1)
-            inter_t = dot(block_j, rows_i, 1, 1)
+            inter_t = dot(rows_j[chunk], rows_i, 1, 1)
             combined = ((2.0 * inter - inter_t) / (energy[t] - vir_sum)).astype(BF16)
             total = total + dot(combined, rows_j, 1, 0)
-        for half in range(2):
-            turned = jnp.transpose(total[half * lanes : (half + 1) * lanes])
-            out[:, step * 2 + half] = turned.reshape(n_cyc, aux_blk, lanes).astype(BF16)
-        return carry
-
-    lax.fori_loop(0, n_h // 2, body, 0)
+        for n in range(per):
+            turn = jnp.transpose(total[n * lanes : (n + 1) * lanes])
+            out[:, step * per + n] = turn.reshape(n_cyc, aux_blk, lanes).astype(BF16)
+        part = pl.ds(step * per, per)
+        stores.append(pltpu.make_async_copy(out.at[:, part], out_any.at[:, part], sems.at[4 + step]))
+        stores[-1].start()
+    for store in stores:
+        store.wait()
 
 
 def aux_kernel(place, dens, rows, near, far, acc):
@@ -133,14 +151,25 @@
         send[:, g] = (near[:, other] + far[:, other].astype(F32)).astype(BF16)
 
 
-def lag_kernel(place, moved, ints, other_ints, parts, wide, acc):
-    n_src, aux_blk, lanes = moved.shape
+def lag_kernel(place, moved_any, ints, other_any, parts, wide, acc, moved, other_ints, sems):
+    n_src, aux_blk, lanes = moved_any.shape
     n_orb = ints.shape[2]
     n_zl = parts.shape[2]
     n_cyc = n_src // n_zl
     shift, core = place[0], place[2]
+    first = pltpu.make_async_copy(moved_any, moved, sems.at[0])
+    first.start()
+    loads = []
+    per = aux_blk // N_LOAD
+    for n in range(N_LOAD):
+        part = pl.ds(n * per, per)
+        loads.append(pltpu.make_async_copy(other_any.at[part], other_ints.at[part], sems.at[n + 1]))
+        loads[n].start()
+    first.wait()
     wide[...] = moved[...].reshape(n_src * aux_blk, lanes).astype(F32)
     for p in range(0, aux_blk, 2):
+        if p % per == 0:
+            loads[p // per].wait()
         left, right = [], []
         for q in (p, p + 1):
             x = wide[pl.ds(q, n_src, stride=aux_blk), :]
@@ -231,15 +260,16 @@
     spread = exchange_all(own.reshape(n_cyc, sub, n_aux), CYC)
     turned = call(
         turn_kernel,
-        jax.ShapeDtypeStruct((n_cyc, 2, sub, n_aux), BF16),
-        [],
+        jax.ShapeDtypeStruct((n_cyc // 2, 2, 2, sub, n_aux), BF16),
+        [pltpu.SemaphoreType.DMA((n_cyc + 4,))],
         0,
         8 * n_vir * n_aux,
         place,
-        spread,
+        spread.reshape(n_cyc // 2, 2, sub, n_aux),
         specs=[smem, vmem],
-    )
-    rows = exchange_all(turned, CYC)
+        out_spec=hbm,
+    )
+    rows = exchange_all(turned.reshape(n_cyc, 2, sub, n_aux), CYC)
 
     step = 1 - 2 * yl
     energy_i = occ_energy[jnp.mod(cyc + shift, n_cyc) * n_grp + grp]
@@ -247,7 +277,14 @@
     dens = call(
         pair_kernel,
         jax.ShapeDtypeStruct((n_cyc, n_vir // LANES, aux_blk, LANES), BF16),
-        [],
+        [
+            pltpu.VMEM((n_cyc, sub, n_aux), BF16),
+            pltpu.VMEM((n_cyc, sub, n_aux), BF16),
+            pltpu.VMEM((n_vir, n_aux), BF16),
+            pltpu.VMEM((n_vir, n_aux), BF16),
+            pltpu.VMEM((n_cyc, n_vir // LANES, aux_blk, LANES), BF16),
+            pltpu.SemaphoreType.DMA((4 + N_STEP,)),
+        ],
         18 * n_vir * n_vir * n_aux,
         5 * 2 * n_vir * n_aux,
         energy_i + energy_j,
@@ -256,7 +293,9 @@
         rows,
         own,
         mate,
-        specs=[smem] + [vmem] * 5,
+        specs=[smem, vmem, vmem, hbm, hbm, hbm],
+        out_spec=hbm,
+        grant=PAIR_BYTES,
     )
     moved = exchange_all(dens.reshape(n_cyc * n_zl, aux_blk, LANES), CYC + ("zl",))
 
@@ -294,14 +333,20 @@
     lag = call(
         lag_kernel,
         jax.ShapeDtypeStruct((n_cyc, 2, n_zl, n_zl, LANES), F32),
-        [pltpu.VMEM((n_vir * n_aux // LANES, LANES), F32), pltpu.VMEM((n_cyc * n_zl, n_orb), F32)],
+        [
+            pltpu.VMEM((n_vir * n_aux // LANES, LANES), F32),
+            pltpu.VMEM((n_cyc * n_zl, n_orb), F32),
+            pltpu.VMEM((n_cyc * n_zl, aux_blk, LANES), BF16),
+            pltpu.VMEM(ints.shape, BF16),
+            pltpu.SemaphoreType.DMA((1 + N_LOAD,)),
+        ],
         2 * n_vir * n_aux * n_orb,
         2 * n_vir * n_aux * 10,
         place,
         moved,
         ints,
         other_ints,
-        specs=[smem] + [vmem] * 3,
+        specs=[smem, hbm, vmem, hbm],
     )
     n_rows = 2 * n_zl * n_zl + n_zl // 2 * aux_blk
     parts = call(

time: 164 us -> 164 us (level)
    unnamed x13 -> x11, local copies, waits for them, and re-layouts: 6.58 us -> 5.7 us
  transfers between devices with their start and end apart: 7 -> 7, of which waited for: 4 -> 4; matrix products, arithmetic and copies ran while one was open for 4% -> 4% of each run, Pallas kernels for 9% -> 10%
where the time goes in v6:
time: 164 us
  waiting for transfers between devices  55.1 us (34%)
  starting transfers between devices  47.8 us (29%)
  blocking collectives  30.6 us (19%)
  Pallas kernels  19.6 us (12%)
  local copies, waits for them, and re-layouts  7.83 us (5%)
    all_to_all x3, starting transfers between devices, exchange_all(): return lax.all_to_all(x, axes, split_axis=0, concat_axis=0, tiled=True)  36.7 us
    all_to_all x2, blocking collectives, exchange_all(): return lax.all_to_all(x, axes, split_axis=0, concat_axis=0, tiled=True)  30.6 us
    all_to_all x3, waiting for transfers between devices, exchange_all(): return lax.all_to_all(x, axes, split_axis=0, concat_axis=0, tiled=True)  30.5 us
    ppermute x2, waiting for transfers between devices, swap_yl(): return lax.ppermute(x, 'yl', [(0, 1), (1, 0)])  22.7 us
    pallas_call x8, Pallas kernels, call(): pl.pallas_call(kernel, out_shape=outs, in_specs=specs, out_specs=jax.tree...  19.6 us
    ppermute x2, starting transfers between devices, swap_cores(): return lax.ppermute(x, 'core', [(0, 1), (1, 0)])  9.11 us
    unnamed x11, local copies, waits for them, and re-layouts  5.7 us
  transfers between devices with their start and end apart: 7, of which 4 were waited for; matrix products, arithmetic and copies ran while one was open for 4% of the time, Pallas kernels for 10%

profile of v6, /device:TPU:1, one launch (start us, length us, event | category | flops | bytes accessed | tf_op | source)
XLA Modules:
  0.0 163.7 jit_solution(5276484426475620017)
XLA Ops:
  0.6 14.5 %all-to-all-start = ((bf16[32,16,768]{2,1,0:T(8,128)(2,1)}), bf16[32,16,768]{2,1,0:T(8,128)(2,1)S(1)}, u32[]{:S(2)}, u32[]{:S(2)}) async-start(bf16[32,16,768]{2,1,0:T(8,128)(2,1)} %bitcast.10), calls=%async_computation | async-start | bytes 1572864 | tf_op jit(solution)/shard_map/all_to_all | solution.py:26
  15.8 0.1 pad_add_fusion.place
  15.9 17.1 %all-to-all-done = bf16[32,16,768]{2,1,0:T(8,128)(2,1)S(1)} async-done(((bf16[32,16,768]{2,1,0:T(8,128)(2,1)}), bf16[32,16,768]{2,1,0:T(8,128)(2,1)S(1)}, u32[]{:S(2)}, u32[]{:S(2)}) %all-to-all-start) | async-done | bytes 786464 | tf_op jit(solution)/shard_map/all_to_all | solution.py:26
  33.0 2.1 %shard_map.68 = bf16[16,2,2,16,768]{4,3,2,1,0:T(8,128)(2,1)} custom-call(s32[3]{0:T(128)S(1)} %pad_add_fusion.place, bf16[16,2,16,768]{3,2,1,0:T(8,128)(2,1)S(1)} %bitcast.21), custom_call_target="tpu_custom_call" | custom-call | bytes 3145728 | tf_op jit(solution)/shard_map/pallas_call | solution.py:42
  35.1 4.7 %all-to-all-start.1 = ((bf16[32,2,16,768]{3,2,1,0:T(8,128)(2,1)}), bf16[32,2,16,768]{3,2,1,0:T(8,128)(2,1)}, u32[]{:S(2)}, u32[]{:S(2)}) async-start(bf16[32,2,16,768]{3,2,1,0:T(8,128)(2,1)} %bitcast.12), calls=%async_computation.1 | async-start | bytes 3145728 | tf_op jit(solution)/shard_map/all_to_all | solution.py:26
  39.8 0.0 copy-start.3
  39.8 0.0 copy-start.4
  39.8 3.6 %copy.11 = bf16[64,24,1024]{2,0,1:T(8,128)(2,1)S(1)} copy(bf16[64,24,1024]{2,1,0:T(8,128)(2,1)} %param.8) | data formatting | bytes 6291456 | tf_op args[3]
  43.4 8.3 %collective-permute-start.1 = (bf16[24,64,1024]{2,1,0:T(8,128)(2,1)S(1)}, bf16[24,64,1024]{2,1,0:T(8,128)(2,1)}, u32[]{:S(2)}, u32[]{:S(2)}) collective-permute-start(bf16[24,64,1024]{2,1,0:T(8,128)(2,1)S(1)} %bitcast.19), channel_id=1, source_target_pairs={{0,1},{1,0},{2,3},{3,2},{4,5},{5,4},{6,7},{7,6},{8,9},{9,8},{10,11... | collective-permute-start | bytes 9437192 | tf_op jit(solution)/shard_map/ppermute | solution.py:30
  51.7 1.5 collective-permute-start
  53.1 0.0 copy-done.3
  53.1 0.6 dynamic_slice.3
  53.8 0.1 fusion.3
  53.9 0.6 gather_fusion
  54.5 0.0 copy-done.4
  54.5 0.9 copy.8.vir_col
  55.4 1.1 broadcast_add_fusion.energy
  56.5 22.7 %collective-permute-done.mate_any = bf16[512,768]{1,0:T(8,128)(2,1)} collective-permute-done((bf16[512,768]{1,0:T(8,128)(2,1)}, bf16[512,768]{1,0:T(8,128)(2,1)}, u32[]{:S(2)}, u32[]{:S(2)}) %collective-permute-start) | collective-permute-done | bytes 786464 | tf_op jit(solution)/shard_map/ppermute | solution.py:34
  79.2 0.0 all-to-all-done.1.rows_any.rows
  79.2 8.1 %shard_map.69.dens = bf16[32,4,24,128]{3,2,1,0:T(8,128)(2,1)} custom-call(f32[3]{0:T(128)} %broadcast_add_fusion.energy, f32[1,512]{1,0:T(1,128)} %bitcast.23, f32[512,1]{1,0:T(8,128)} %copy.8.vir_col, bf16[32,2,16,768]{3,2,1,0:T(8,128)(2,1)} %all-to-all-done.1.rows_any.rows, bf16[512,768]{1,0:T(8,128)(2,1)} %bitcast.13.own_any, ...), custom_call_target="tpu_custom_call" | custom-call | flops 3623878656 | bytes 3932160 | tf_op jit(solution)/shard_map/pallas_call | solution.py:42
  87.3 17.4 %all-to-all-start.2 = ((bf16[128,24,128]{2,1,0:T(8,128)(2,1)}), bf16[128,24,128]{2,1,0:T(8,128)(2,1)}, u32[]{:S(2)}, u32[]{:S(2)}) async-start(bf16[128,24,128]{2,1,0:T(8,128)(2,1)} %bitcast.22), calls=%async_computation.2 | async-start | bytes 1572864 | tf_op jit(solution)/shard_map/all_to_all | solution.py:26
  104.8 0.0 copy-start
  104.8 1.2 copy-done
  106.0 3.6 %shard_map.71 = (f32[16,8,24,128]{3,2,1,0:T(8,128)S(1)}, bf16[16,8,24,128]{3,2,1,0:T(8,128)(2,1)S(1)}) custom-call(s32[3]{0:T(128)S(1)} %pad_add_fusion.place, bf16[32,4,24,128]{3,2,1,0:T(8,128)(2,1)S(1)} %copy-done, bf16[32,2,16,768]{3,2,1,0:T(8,128)(2,1)} %all-to-all-done.1.rows_any.rows), custom_call_target="tpu_custom_call" | custom-call | flops 603979776 | bytes 3932160 | tf_op jit(solution)/shard_map/pallas_call | solution.py:42
  109.6 0.9 collective-permute-start.2
  110.5 1.9 %collective-permute-done.2.far = bf16[16,8,24,128]{3,2,1,0:T(8,128)(2,1)S(1)} collective-permute-done((bf16[16,8,24,128]{3,2,1,0:T(8,128)(2,1)S(1)}, bf16[16,8,24,128]{3,2,1,0:T(8,128)(2,1)S(1)}, u32[]{:S(2)}, u32[]{:S(2)}) %collective-permute-start.2) | collective-permute-done | bytes 786464 | tf_op jit(solution)/shard_map/ppermute | solution.py:30
  112.4 1.4 shard_map.72
  113.8 0.0 copy-start.1
  113.8 0.9 copy-done.1
  114.7 0.6 collective-permute-start.3
  115.3 0.0 collective-permute-done.1.other_any
  115.3 13.4 %all-to-all-done.2.moved_any = bf16[128,24,128]{2,1,0:T(8,128)(2,1)} async-done(((bf16[128,24,128]{2,1,0:T(8,128)(2,1)}), bf16[128,24,128]{2,1,0:T(8,128)(2,1)}, u32[]{:S(2)}, u32[]{:S(2)}) %all-to-all-start.2) | async-done | bytes 786464 | tf_op jit(solution)/shard_map/all_to_all | solution.py:26
  128.7 0.0 copy-start.2
  128.7 3.5 %shard_map.70.lag = f32[32,2,4,4,128]{4,3,2,1,0:T(4,128)S(1)} custom-call(s32[3]{0:T(128)S(1)} %pad_add_fusion.place, bf16[128,24,128]{2,1,0:T(8,128)(2,1)} %all-to-all-done.2.moved_any, bf16[24,64,1024]{2,1,0:T(8,128)(2,1)S(1)} %bitcast.20, bf16[24,64,1024]{2,1,0:T(8,128)(2,1)} %collective-permute-done.1.other_any), custom_call_target="tpu_custom_call" | custom-call | flops 805306368 | bytes 7864320 | tf_op jit(solution)/shard_map/pallas_call | solution.py:42
  132.3 0.0 collective-permute-done.3.recv
  132.3 0.0 copy-done.2
  132.3 0.1 shard_map.73
  132.4 18.7 %all_to_all.25.got = bf16[32,80,128]{2,1,0:T(8,128)(2,1)S(1)} all-to-all(bf16[32,80,128]{2,1,0:T(8,128)(2,1)S(1)} %shard_map.73), channel_id=1, replica_groups=mesh['x'=4,'zh'=2,'yh'=2,'yl'=2,'zl'=4,'core'=2] {'x','yh','yl','core'}, dimensions={0} | all-to-all | bytes 1310720 | tf_op jit(solution)/shard_map/all_to_all | solution.py:26
  151.1 0.1 shard_map.74
  151.2 11.9 %all_to_all.26.got = f32[8,32,128]{2,1,0:T(8,128)S(1)} all-to-all(f32[8,32,128]{2,1,0:T(8,128)S(1)} %shard_map.74), channel_id=1, replica_groups=mesh['x'=4,'zh'=2,'yh'=2,'yl'=2,'zl'=4,'core'=2] {'zh','zl'}, dimensions={0} | all-to-all | bytes 262144 | tf_op jit(solution)/shard_map/all_to_all | solution.py:26
  163.1 0.6 shard_map.75
  (1 shorter events, 0.0 us)
Async XLA Ops:
  0.6 32.4 %all-to-all-start = ((bf16[32,16,768]{2,1,0:T(8,128)(2,1)}), bf16[32,16,768]{2,1,0:T(8,128)(2,1)S(1)}, u32[]{:S(2)}, u32[]{:S(2)}) async-start(bf16[32,16,768]{2,1,0:T(8,128)(2,1)} %bitcast.10), calls=%async_computation | async-start | bytes 1572864 | tf_op jit(solution)/shard_map/all_to_all | solution.py:26
  35.1 44.1 %all-to-all-start.1 = ((bf16[32,2,16,768]{3,2,1,0:T(8,128)(2,1)}), bf16[32,2,16,768]{3,2,1,0:T(8,128)(2,1)}, u32[]{:S(2)}, u32[]{:S(2)}) async-start(bf16[32,2,16,768]{3,2,1,0:T(8,128)(2,1)} %bitcast.12), calls=%async_computation.1 | async-start | bytes 3145728 | tf_op jit(solution)/shard_map/all_to_all | solution.py:26
  39.8 13.4 %copy-start.3 = (f32[256]{0:T(256)S(1)}, f32[256]{0:T(256)}, u32[]{:S(2)}) copy-start(f32[256]{0:T(256)} %param.6) | copy-start | bytes 3076
  39.8 14.7 %copy-start.4 = (f32[512]{0:T(512)S(1)}, f32[512]{0:T(512)}, u32[]{:S(2)}) copy-start(f32[512]{0:T(512)} %param.7) | copy-start | bytes 6148
  43.4 71.9 %collective-permute-start.1 = (bf16[24,64,1024]{2,1,0:T(8,128)(2,1)S(1)}, bf16[24,64,1024]{2,1,0:T(8,128)(2,1)}, u32[]{:S(2)}, u32[]{:S(2)}) collective-permute-start(bf16[24,64,1024]{2,1,0:T(8,128)(2,1)S(1)} %bitcast.19), channel_id=1, source_target_pairs={{0,1},{1,0},{2,3},{3,2},{4,5},{5,4},{6,7},{7,6},{8,9},{9,8},{10,11... | collective-permute-start | bytes 9437192 | tf_op jit(solution)/shard_map/ppermute | solution.py:30
  51.7 27.5 %collective-permute-start = (bf16[512,768]{1,0:T(8,128)(2,1)}, bf16[512,768]{1,0:T(8,128)(2,1)}, u32[]{:S(2)}, u32[]{:S(2)}) collective-permute-start(bf16[512,768]{1,0:T(8,128)(2,1)} %bitcast.13.own_any), channel_id=1, source_target_pairs={{0,8},{8,0},{1,9},{9,1},{2,10},{10,2},{3,11},{11,3},{4,12},{12,4},... | collective-permute-start | bytes 2359304 | tf_op jit(solution)/shard_map/ppermute | solution.py:34
  87.3 41.4 %all-to-all-start.2 = ((bf16[128,24,128]{2,1,0:T(8,128)(2,1)}), bf16[128,24,128]{2,1,0:T(8,128)(2,1)}, u32[]{:S(2)}, u32[]{:S(2)}) async-start(bf16[128,24,128]{2,1,0:T(8,128)(2,1)} %bitcast.22), calls=%async_computation.2 | async-start | bytes 1572864 | tf_op jit(solution)/shard_map/all_to_all | solution.py:26
  104.8 1.2 copy-start
  109.6 2.8 %collective-permute-start.2 = (bf16[16,8,24,128]{3,2,1,0:T(8,128)(2,1)S(1)}, bf16[16,8,24,128]{3,2,1,0:T(8,128)(2,1)S(1)}, u32[]{:S(2)}, u32[]{:S(2)}) collective-permute-start(bf16[16,8,24,128]{3,2,1,0:T(8,128)(2,1)S(1)} %get-tuple-element.7), channel_id=1, source_target_pairs={{0,1},{1,0},{2,3},{3,2},{4,5},{5,4},{6,7},{7,6},{8,9},{9,8},{10,11... | collective-permute-start | bytes 2359304 | tf_op jit(solution)/shard_map/ppermute | solution.py:30
  113.8 0.9 copy-start.1
  114.7 17.6 %collective-permute-start.3 = (bf16[16,4,24,128]{3,2,1,0:T(8,128)(2,1)}, bf16[16,4,24,128]{3,2,1,0:T(8,128)(2,1)S(1)}, u32[]{:S(2)}, u32[]{:S(2)}) collective-permute-start(bf16[16,4,24,128]{3,2,1,0:T(8,128)(2,1)} %get-tuple-element.9), channel_id=1, source_target_pairs={{0,8},{8,0},{1,9},{9,1},{2,10},{10,2},{3,11},{11,3},{4,12},{12,4},... | collective-permute-start | bytes 1179656 | tf_op jit(solution)/shard_map/ppermute | solution.py:34
  128.7 3.6 %copy-start.2 = (f32[16,4,24,128]{3,2,1,0:T(8,128)S(1)}, f32[16,4,24,128]{3,2,1,0:T(8,128)}, u32[]{:S(2)}) copy-start(f32[16,4,24,128]{3,2,1,0:T(8,128)} %copy-done.1) | copy-start | bytes 2359300

commit v7 on v4

--- a/solution.py
+++ b/solution.py
@@ -13,9 +13,11 @@
 PLANE = ("x", "yh", "yl", "core")
 DEPTH = ("zh", "zl")
 N_Y = 4
+N_LOAD = 4
 
 vmem = pl.BlockSpec(memory_space=pltpu.VMEM)
 smem = pl.BlockSpec(memory_space=pltpu.SMEM)
+hbm = pl.BlockSpec(memory_space=pl.ANY)
 
 
 def exchange_all(x, axes):
@@ -63,31 +65,16 @@
 def pair_kernel(energy, vir_row, vir_col, rows, own, mate, out):
     n_cyc, n_h, aux_blk, lanes = out.shape
     n_vir, n_aux = own.shape
-    sub = rows.shape[2]
-    blk = 2 * lanes
     rows_i = rows[:, 0].reshape(n_vir, n_aux)
-    far = rows[:, 1].reshape(n_vir, n_aux)
-
-    def body(step, carry):
-        start = pl.multiple_of(step * blk, blk)
-        chunk = pl.ds(step * (blk // sub), blk // sub)
-        block_i = rows[chunk, 0].reshape(blk, n_aux)
-        block_far = rows[chunk, 1].reshape(blk, n_aux)
-        vir_sum = vir_col[pl.ds(start, blk), :] + vir_row[...]
-        total = jnp.zeros((blk, n_aux), F32)
-        for t, (block_j, rows_j) in enumerate(
-            ((own[pl.ds(start, blk), :], own[...]), (mate[pl.ds(start, blk), :], mate[...]), (block_far, far))
-        ):
-            inter = dot(block_i, rows_j, 1, 1)
-            inter_t = dot(block_j, rows_i, 1, 1)
-            combined = ((2.0 * inter - inter_t) / (energy[t] - vir_sum)).astype(BF16)
-            total = total + dot(combined, rows_j, 1, 0)
-        for half in range(2):
-            turned = jnp.transpose(total[half * lanes : (half + 1) * lanes])
-            out[:, step * 2 + half] = turned.reshape(n_cyc, aux_blk, lanes).astype(BF16)
-        return carry
-
-    lax.fori_loop(0, n_h // 2, body, 0)
+    vir_sum = vir_col[...] + vir_row[...]
+    total = jnp.zeros((n_vir, n_aux), F32)
+    for t, rows_j in enumerate((own[...], mate[...], rows[:, 1].reshape(n_vir, n_aux))):
+        inter = dot(rows_i, rows_j, 1, 1)
+        combined = ((2.0 * inter - jnp.transpose(inter)) / (energy[t] - vir_sum)).astype(BF16)
+        total = total + dot(combined, rows_j, 1, 0)
+    for h in range(n_h):
+        turned = jnp.transpose(total[h * lanes : (h + 1) * lanes])
+        out[:, h] = turned.reshape(n_cyc, aux_blk, lanes).astype(BF16)
 
 
 def aux_kernel(place, dens, rows, near, far, acc):
@@ -133,14 +120,25 @@
         send[:, g] = (near[:, other] + far[:, other].astype(F32)).astype(BF16)
 
 
-def lag_kernel(place, moved, ints, other_ints, parts, wide, acc):
-    n_src, aux_blk, lanes = moved.shape
+def lag_kernel(place, moved_any, ints, other_any, parts, wide, acc, moved, other_ints, sems):
+    n_src, aux_blk, lanes = moved_any.shape
     n_orb = ints.shape[2]
     n_zl = parts.shape[2]
     n_cyc = n_src // n_zl
     shift, core = place[0], place[2]
+    first = pltpu.make_async_copy(moved_any, moved, sems.at[0])
+    first.start()
+    loads = []
+    per = aux_blk // N_LOAD
+    for n in range(N_LOAD):
+        part = pl.ds(n * per, per)
+        loads.append(pltpu.make_async_copy(other_any.at[part], other_ints.at[part], sems.at[n + 1]))
+        loads[n].start()
+    first.wait()
     wide[...] = moved[...].reshape(n_src * aux_blk, lanes).astype(F32)
     for p in range(0, aux_blk, 2):
+        if p % per == 0:
+            loads[p // per].wait()
         left, right = [], []
         for q in (p, p + 1):
             x = wide[pl.ds(q, n_src, stride=aux_blk), :]
@@ -294,14 +292,20 @@
     lag = call(
         lag_kernel,
         jax.ShapeDtypeStruct((n_cyc, 2, n_zl, n_zl, LANES), F32),
-        [pltpu.VMEM((n_vir * n_aux // LANES, LANES), F32), pltpu.VMEM((n_cyc * n_zl, n_orb), F32)],
+        [
+            pltpu.VMEM((n_vir * n_aux // LANES, LANES), F32),
+            pltpu.VMEM((n_cyc * n_zl, n_orb), F32),
+            pltpu.VMEM((n_cyc * n_zl, aux_blk, LANES), BF16),
+            pltpu.VMEM(ints.shape, BF16),
+            pltpu.SemaphoreType.DMA((1 + N_LOAD,)),
+        ],
         2 * n_vir * n_aux * n_orb,
         2 * n_vir * n_aux * 10,
         place,
         moved,
         ints,
         other_ints,
-        specs=[smem] + [vmem] * 3,
+        specs=[smem, hbm, vmem, hbm],
     )
     n_rows = 2 * n_zl * n_zl + n_zl // 2 * aux_blk
     parts = call(

time: 164 us -> 162 us (0.988)
  Pallas kernels: 18.2 us -> 16.4 us
    pallas_call x8, Pallas kernels: 18.2 us -> 16.4 us  [call(): pl.pallas_call(kernel, out_shape=outs, in_specs=specs, out_specs=jax.tree...]
  transfers between devices with their start and end apart: 7 -> 7, of which waited for: 4 -> 4; matrix products, arithmetic and copies ran while one was open for 4% -> 4% of each run, Pallas kernels for 9% -> 8%
where the time goes in v7:
time: 162 us; the launch traced here: 161 us
  waiting for transfers between devices  56.3 us (35%)
  starting transfers between devices  47.8 us (30%)
  blocking collectives  30.6 us (19%)
  Pallas kernels  16.4 us (10%)
  local copies, waits for them, and re-layouts  7.98 us (5%)
    all_to_all x3, starting transfers between devices, exchange_all(): return lax.all_to_all(x, axes, split_axis=0, concat_axis=0, tiled=True)  36.5 us
    all_to_all x2, blocking collectives, exchange_all(): return lax.all_to_all(x, axes, split_axis=0, concat_axis=0, tiled=True)  30.6 us
    all_to_all x3, waiting for transfers between devices, exchange_all(): return lax.all_to_all(x, axes, split_axis=0, concat_axis=0, tiled=True)  30.5 us
    ppermute x2, waiting for transfers between devices, swap_yl(): return lax.ppermute(x, 'yl', [(0, 1), (1, 0)])  23.9 us
    pallas_call x8, Pallas kernels, call(): pl.pallas_call(kernel, out_shape=outs, in_specs=specs, out_specs=jax.tree...  16.4 us
    ppermute x2, starting transfers between devices, swap_cores(): return lax.ppermute(x, 'core', [(0, 1), (1, 0)])  9.11 us
    unnamed x13, local copies, waits for them, and re-layouts  6.58 us
  transfers between devices with their start and end apart: 7, of which 4 were waited for; matrix products, arithmetic and copies ran while one was open for 4% of the time, Pallas kernels for 8%

profile of v7, /device:TPU:1, one launch (start us, length us, event | category | flops | bytes accessed | tf_op | source)
XLA Modules:
  0.0 161.4 jit_solution(7032535361650258191)
XLA Ops:
  0.6 14.5 %all-to-all-start = ((bf16[32,16,768]{2,1,0:T(8,128)(2,1)}), bf16[32,16,768]{2,1,0:T(8,128)(2,1)S(1)}, u32[]{:S(2)}, u32[]{:S(2)}) async-start(bf16[32,16,768]{2,1,0:T(8,128)(2,1)} %bitcast.10), calls=%async_computation | async-start | bytes 1572864 | tf_op jit(solution)/shard_map/all_to_all | solution.py:24
  15.8 0.1 pad_add_fusion.place
  15.9 17.1 %all-to-all-done.spread = bf16[32,16,768]{2,1,0:T(8,128)(2,1)S(1)} async-done(((bf16[32,16,768]{2,1,0:T(8,128)(2,1)}), bf16[32,16,768]{2,1,0:T(8,128)(2,1)S(1)}, u32[]{:S(2)}, u32[]{:S(2)}) %all-to-all-start) | async-done | bytes 786464 | tf_op jit(solution)/shard_map/all_to_all | solution.py:24
  33.0 2.0 %shard_map.68 = bf16[32,2,16,768]{3,2,1,0:T(8,128)(2,1)} custom-call(s32[3]{0:T(128)S(1)} %pad_add_fusion.place, bf16[32,16,768]{2,1,0:T(8,128)(2,1)S(1)} %all-to-all-done.spread), custom_call_target="tpu_custom_call" | custom-call | bytes 3145728 | tf_op jit(solution)/shard_map/pallas_call | solution.py:40
  35.0 4.7 %all-to-all-start.1 = ((bf16[32,2,16,768]{3,2,1,0:T(8,128)(2,1)}), bf16[32,2,16,768]{3,2,1,0:T(8,128)(2,1)}, u32[]{:S(2)}, u32[]{:S(2)}) async-start(bf16[32,2,16,768]{3,2,1,0:T(8,128)(2,1)} %shard_map.68), calls=%async_computation.1 | async-start | bytes 3145728 | tf_op jit(solution)/shard_map/all_to_all | solution.py:24
  39.7 0.0 copy-start.5
  39.7 0.0 copy-start.4
  39.7 3.6 %copy.11 = bf16[64,24,1024]{2,0,1:T(8,128)(2,1)S(1)} copy(bf16[64,24,1024]{2,1,0:T(8,128)(2,1)} %param.8) | data formatting | bytes 6291456 | tf_op args[3]
  43.3 8.3 %collective-permute-start.1 = (bf16[24,64,1024]{2,1,0:T(8,128)(2,1)S(1)}, bf16[24,64,1024]{2,1,0:T(8,128)(2,1)}, u32[]{:S(2)}, u32[]{:S(2)}) collective-permute-start(bf16[24,64,1024]{2,1,0:T(8,128)(2,1)S(1)} %bitcast.17), channel_id=1, source_target_pairs={{0,1},{1,0},{2,3},{3,2},{4,5},{5,4},{6,7},{7,6},{8,9},{9,8},{10,11... | collective-permute-start | bytes 9437192 | tf_op jit(solution)/shard_map/ppermute | solution.py:28
  51.6 1.5 collective-permute-start
  53.0 0.0 copy-done.5
  53.0 0.6 dynamic_slice.3
  53.7 0.1 fusion.3
  53.8 0.6 gather_fusion
  54.4 0.0 copy-done.4
  54.4 0.1 copy.8.vir_col
  54.5 0.6 broadcast_add_fusion.energy
  55.2 23.9 %collective-permute-done.mate = bf16[512,768]{1,0:T(8,128)(2,1)} collective-permute-done((bf16[512,768]{1,0:T(8,128)(2,1)}, bf16[512,768]{1,0:T(8,128)(2,1)}, u32[]{:S(2)}, u32[]{:S(2)}) %collective-permute-start) | collective-permute-done | bytes 786464 | tf_op jit(solution)/shard_map/ppermute | solution.py:32
  79.1 0.0 all-to-all-done.1.rows
  79.1 5.0 %shard_map.69.dens = bf16[32,4,24,128]{3,2,1,0:T(8,128)(2,1)S(1)} custom-call(f32[3]{0:T(128)S(1)} %broadcast_add_fusion.energy, f32[1,512]{1,0:T(1,128)S(1)} %bitcast.21, f32[512,1]{1,0:T(8,128)S(1)} %copy.8.vir_col, bf16[32,2,16,768]{3,2,1,0:T(8,128)(2,1)} %all-to-all-done.1.rows, bf16[512,768]{1,0:T(8,128)(2,1)} %bitcast.11.own, ...), custom_call_target="tpu_custom_call" | custom-call | flops 3623878656 | bytes 3932160 | tf_op jit(solution)/shard_map/pallas_call | solution.py:40
  84.1 0.0 copy-start
  84.2 0.9 copy-done
  85.0 17.2 %all-to-all-start.2 = ((bf16[128,24,128]{2,1,0:T(8,128)(2,1)}), bf16[128,24,128]{2,1,0:T(8,128)(2,1)}, u32[]{:S(2)}, u32[]{:S(2)}) async-start(bf16[128,24,128]{2,1,0:T(8,128)(2,1)} %bitcast.19), calls=%async_computation.2 | async-start | bytes 1572864 | tf_op jit(solution)/shard_map/all_to_all | solution.py:24
  102.3 0.0 copy-start.1
  102.3 1.2 copy-done.1
  103.5 3.6 %shard_map.71 = (f32[16,8,24,128]{3,2,1,0:T(8,128)S(1)}, bf16[16,8,24,128]{3,2,1,0:T(8,128)(2,1)S(1)}) custom-call(s32[3]{0:T(128)S(1)} %pad_add_fusion.place, bf16[32,4,24,128]{3,2,1,0:T(8,128)(2,1)S(1)} %copy-done.1, bf16[32,2,16,768]{3,2,1,0:T(8,128)(2,1)} %all-to-all-done.1.rows), custom_call_target="tpu_custom_call" | custom-call | flops 603979776 | bytes 3932160 | tf_op jit(solution)/shard_map/pallas_call | solution.py:40
  107.1 0.9 collective-permute-start.2
  108.0 1.9 %collective-permute-done.2.far = bf16[16,8,24,128]{3,2,1,0:T(8,128)(2,1)S(1)} collective-permute-done((bf16[16,8,24,128]{3,2,1,0:T(8,128)(2,1)S(1)}, bf16[16,8,24,128]{3,2,1,0:T(8,128)(2,1)S(1)}, u32[]{:S(2)}, u32[]{:S(2)}) %collective-permute-start.2) | collective-permute-done | bytes 786464 | tf_op jit(solution)/shard_map/ppermute | solution.py:28
  109.9 1.4 shard_map.72
  111.3 0.0 copy-start.2
  111.3 0.9 copy-done.2
  112.2 0.8 collective-permute-start.3
  113.0 0.0 collective-permute-done.1.other_any
  113.0 13.4 %all-to-all-done.2.moved_any = bf16[128,24,128]{2,1,0:T(8,128)(2,1)} async-done(((bf16[128,24,128]{2,1,0:T(8,128)(2,1)}), bf16[128,24,128]{2,1,0:T(8,128)(2,1)}, u32[]{:S(2)}, u32[]{:S(2)}) %all-to-all-start.2) | async-done | bytes 786464 | tf_op jit(solution)/shard_map/all_to_all | solution.py:24
  126.4 0.0 copy-start.3
  126.4 3.5 %shard_map.70.lag = f32[32,2,4,4,128]{4,3,2,1,0:T(4,128)S(1)} custom-call(s32[3]{0:T(128)S(1)} %pad_add_fusion.place, bf16[128,24,128]{2,1,0:T(8,128)(2,1)} %all-to-all-done.2.moved_any, bf16[24,64,1024]{2,1,0:T(8,128)(2,1)S(1)} %bitcast.18, bf16[24,64,1024]{2,1,0:T(8,128)(2,1)} %collective-permute-done.1.other_any), custom_call_target="tpu_custom_call" | custom-call | flops 805306368 | bytes 7864320 | tf_op jit(solution)/shard_map/pallas_call | solution.py:40
  129.9 0.0 collective-permute-done.3.recv
  129.9 0.0 copy-done.3
  130.0 0.1 shard_map.73
  130.1 18.7 %all_to_all.25.got = bf16[32,80,128]{2,1,0:T(8,128)(2,1)S(1)} all-to-all(bf16[32,80,128]{2,1,0:T(8,128)(2,1)S(1)} %shard_map.73), channel_id=1, replica_groups=mesh['x'=4,'zh'=2,'yh'=2,'yl'=2,'zl'=4,'core'=2] {'x','yh','yl','core'}, dimensions={0} | all-to-all | bytes 1310720 | tf_op jit(solution)/shard_map/all_to_all | solution.py:24
  148.8 0.1 shard_map.74
  148.9 11.9 %all_to_all.26.got = f32[8,32,128]{2,1,0:T(8,128)S(1)} all-to-all(f32[8,32,128]{2,1,0:T(8,128)S(1)} %shard_map.74), channel_id=1, replica_groups=mesh['x'=4,'zh'=2,'yh'=2,'yl'=2,'zl'=4,'core'=2] {'zh','zl'}, dimensions={0} | all-to-all | bytes 262144 | tf_op jit(solution)/shard_map/all_to_all | solution.py:24
  160.8 0.6 shard_map.75
  (1 shorter events, 0.0 us)
Async XLA Ops:
  0.6 32.4 %all-to-all-start = ((bf16[32,16,768]{2,1,0:T(8,128)(2,1)}), bf16[32,16,768]{2,1,0:T(8,128)(2,1)S(1)}, u32[]{:S(2)}, u32[]{:S(2)}) async-start(bf16[32,16,768]{2,1,0:T(8,128)(2,1)} %bitcast.10), calls=%async_computation | async-start | bytes 1572864 | tf_op jit(solution)/shard_map/all_to_all | solution.py:24
  35.0 44.1 %all-to-all-start.1 = ((bf16[32,2,16,768]{3,2,1,0:T(8,128)(2,1)}), bf16[32,2,16,768]{3,2,1,0:T(8,128)(2,1)}, u32[]{:S(2)}, u32[]{:S(2)}) async-start(bf16[32,2,16,768]{3,2,1,0:T(8,128)(2,1)} %shard_map.68), calls=%async_computation.1 | async-start | bytes 3145728 | tf_op jit(solution)/shard_map/all_to_all | solution.py:24
  39.7 13.4 %copy-start.5 = (f32[256]{0:T(256)S(1)}, f32[256]{0:T(256)}, u32[]{:S(2)}) copy-start(f32[256]{0:T(256)} %param.6) | copy-start | bytes 3076
  39.7 14.7 %copy-start.4 = (f32[512]{0:T(512)S(1)}, f32[512]{0:T(512)}, u32[]{:S(2)}) copy-start(f32[512]{0:T(512)} %param.7) | copy-start | bytes 6148
  43.3 69.7 %collective-permute-start.1 = (bf16[24,64,1024]{2,1,0:T(8,128)(2,1)S(1)}, bf16[24,64,1024]{2,1,0:T(8,128)(2,1)}, u32[]{:S(2)}, u32[]{:S(2)}) collective-permute-start(bf16[24,64,1024]{2,1,0:T(8,128)(2,1)S(1)} %bitcast.17), channel_id=1, source_target_pairs={{0,1},{1,0},{2,3},{3,2},{4,5},{5,4},{6,7},{7,6},{8,9},{9,8},{10,11... | collective-permute-start | bytes 9437192 | tf_op jit(solution)/shard_map/ppermute | solution.py:28
  51.6 27.5 %collective-permute-start = (bf16[512,768]{1,0:T(8,128)(2,1)}, bf16[512,768]{1,0:T(8,128)(2,1)}, u32[]{:S(2)}, u32[]{:S(2)}) collective-permute-start(bf16[512,768]{1,0:T(8,128)(2,1)} %bitcast.11.own), channel_id=1, source_target_pairs={{0,8},{8,0},{1,9},{9,1},{2,10},{10,2},{3,11},{11,3},{4,12},{12,4},... | collective-permute-start | bytes 2359304 | tf_op jit(solution)/shard_map/ppermute | solution.py:32
  84.1 0.9 copy-start
  85.0 41.4 %all-to-all-start.2 = ((bf16[128,24,128]{2,1,0:T(8,128)(2,1)}), bf16[128,24,128]{2,1,0:T(8,128)(2,1)}, u32[]{:S(2)}, u32[]{:S(2)}) async-start(bf16[128,24,128]{2,1,0:T(8,128)(2,1)} %bitcast.19), calls=%async_computation.2 | async-start | bytes 1572864 | tf_op jit(solution)/shard_map/all_to_all | solution.py:24
  102.3 1.2 copy-start.1
  107.1 2.8 %collective-permute-start.2 = (bf16[16,8,24,128]{3,2,1,0:T(8,128)(2,1)S(1)}, bf16[16,8,24,128]{3,2,1,0:T(8,128)(2,1)S(1)}, u32[]{:S(2)}, u32[]{:S(2)}) collective-permute-start(bf16[16,8,24,128]{3,2,1,0:T(8,128)(2,1)S(1)} %get-tuple-element.7), channel_id=1, source_target_pairs={{0,1},{1,0},{2,3},{3,2},{4,5},{5,4},{6,7},{7,6},{8,9},{9,8},{10,11... | collective-permute-start | bytes 2359304 | tf_op jit(solution)/shard_map/ppermute | solution.py:28
  111.3 0.9 copy-start.2
  112.2 17.7 %collective-permute-start.3 = (bf16[16,4,24,128]{3,2,1,0:T(8,128)(2,1)}, bf16[16,4,24,128]{3,2,1,0:T(8,128)(2,1)S(1)}, u32[]{:S(2)}, u32[]{:S(2)}) collective-permute-start(bf16[16,4,24,128]{3,2,1,0:T(8,128)(2,1)} %get-tuple-element.9), channel_id=1, source_target_pairs={{0,8},{8,0},{1,9},{9,1},{2,10},{10,2},{3,11},{11,3},{4,12},{12,4},... | collective-permute-start | bytes 1179656 | tf_op jit(solution)/shard_map/ppermute | solution.py:32
  126.4 3.6 %copy-start.3 = (f32[16,4,24,128]{3,2,1,0:T(8,128)S(1)}, f32[16,4,24,128]{3,2,1,0:T(8,128)}, u32[]{:S(2)}) copy-start(f32[16,4,24,128]{3,2,1,0:T(8,128)} %copy-done.2) | copy-start | bytes 2359300

commit v8 on v7

--- a/solution.py
+++ b/solution.py
@@ -8,7 +8,7 @@
 BF16 = jnp.bfloat16
 F32 = jnp.float32
 LANES = 128
-VMEM_BYTES = 40 * 1024 * 1024
+VMEM_BYTES = 50 * 1024 * 1024
 CYC = ("x", "zh", "yh", "yl")
 PLANE = ("x", "yh", "yl", "core")
 DEPTH = ("zh", "zl")
@@ -120,9 +120,9 @@
         send[:, g] = (near[:, other] + far[:, other].astype(F32)).astype(BF16)
 
 
-def lag_kernel(place, moved_any, ints, other_any, parts, wide, acc, moved, other_ints, sems):
+def lag_kernel(place, moved_any, ints_any, other_any, parts, wide, acc, moved, ints, other_ints, sems):
     n_src, aux_blk, lanes = moved_any.shape
-    n_orb = ints.shape[2]
+    n_orb = ints_any.shape[2]
     n_zl = parts.shape[2]
     n_cyc = n_src // n_zl
     shift, core = place[0], place[2]
@@ -132,13 +132,15 @@
     per = aux_blk // N_LOAD
     for n in range(N_LOAD):
         part = pl.ds(n * per, per)
-        loads.append(pltpu.make_async_copy(other_any.at[part], other_ints.at[part], sems.at[n + 1]))
-        loads[n].start()
+        for src, dst in ((ints_any, ints), (other_any, other_ints)):
+            loads.append(pltpu.make_async_copy(src.at[part], dst.at[part], sems.at[len(loads) + 1]))
+            loads[-1].start()
     first.wait()
     wide[...] = moved[...].reshape(n_src * aux_blk, lanes).astype(F32)
     for p in range(0, aux_blk, 2):
         if p % per == 0:
-            loads[p // per].wait()
+            loads[p // per * 2].wait()
+            loads[p // per * 2 + 1].wait()
         left, right = [], []
         for q in (p, p + 1):
             x = wide[pl.ds(q, n_src, stride=aux_blk), :]
@@ -223,7 +225,7 @@
     mate = swap_yl(own)
 
     ints = jnp.transpose(integrals, (1, 0, 2))
-    other_ints = swap_cores(ints)
+    ints, other_ints, mate = lax.optimization_barrier((ints, swap_cores(ints), mate))
 
     sub = n_vir // n_cyc
     spread = exchange_all(own.reshape(n_cyc, sub, n_aux), CYC)
@@ -297,7 +299,8 @@
             pltpu.VMEM((n_cyc * n_zl, n_orb), F32),
             pltpu.VMEM((n_cyc * n_zl, aux_blk, LANES), BF16),
             pltpu.VMEM(ints.shape, BF16),
-            pltpu.SemaphoreType.DMA((1 + N_LOAD,)),
+            pltpu.VMEM(ints.shape, BF16),
+            pltpu.SemaphoreType.DMA((1 + 2 * N_LOAD,)),
         ],
         2 * n_vir * n_aux * n_orb,
         2 * n_vir * n_aux * 10,
@@ -305,7 +308,7 @@
         moved,
         ints,
         other_ints,
-        specs=[smem, hbm, vmem, hbm],
+        specs=[smem, hbm, hbm, hbm],
     )
     n_rows = 2 * n_zl * n_zl + n_zl // 2 * aux_blk
     parts = call(

time: 162 us -> 162 us (level)
    ppermute x2, starting transfers between devices: 9.11 us -> 1.82 us  [swap_cores(): return lax.ppermute(x, 'core', [(0, 1), (1, 0)])]
    all_to_all x3, starting transfers between devices: 36.5 us -> 43.6 us  [exchange_all(): return lax.all_to_all(x, axes, split_axis=0, concat_axis=0, tiled=True)]
    ppermute x2, waiting for transfers between devices: 23.9 us -> 28.4 us  [swap_yl(): return lax.ppermute(x, 'yl', [(0, 1), (1, 0)])]
    all_to_all x3, waiting for transfers between devices: 30.5 us -> 27 us  [exchange_all(): return lax.all_to_all(x, axes, split_axis=0, concat_axis=0, tiled=True)]
    unnamed x13 -> x7, local copies, waits for them, and re-layouts: 6.58 us -> 5.26 us
  transfers between devices with their start and end apart: 7 -> 7, of which waited for: 4 -> 4; matrix products, arithmetic and copies ran while one was open for 4% -> 5% of each run, Pallas kernels for 8% -> 7%
where the time goes in v8:
time: 162 us; the launch traced here: 161 us
  waiting for transfers between devices  57.3 us (35%)
  starting transfers between devices  47.5 us (29%)
  blocking collectives  30.7 us (19%)
  Pallas kernels  17.1 us (11%)
  local copies, waits for them, and re-layouts  6.65 us (4%)
    all_to_all x3, starting transfers between devices, exchange_all(): return lax.all_to_all(x, axes, split_axis=0, concat_axis=0, tiled=True)  43.6 us
    all_to_all x2, blocking collectives, exchange_all(): return lax.all_to_all(x, axes, split_axis=0, concat_axis=0, tiled=True)  30.7 us
    ppermute x2, waiting for transfers between devices, swap_yl(): return lax.ppermute(x, 'yl', [(0, 1), (1, 0)])  28.4 us
    all_to_all x3, waiting for transfers between devices, exchange_all(): return lax.all_to_all(x, axes, split_axis=0, concat_axis=0, tiled=True)  27 us
    pallas_call x8, Pallas kernels, call(): pl.pallas_call(kernel, out_shape=outs, in_specs=specs, out_specs=jax.tree...  17.1 us
    unnamed x7, local copies, waits for them, and re-layouts  5.26 us
  transfers between devices with their start and end apart: 7, of which 4 were waited for; matrix products, arithmetic and copies ran while one was open for 5% of the time, Pallas kernels for 7%

profile of v8, /device:TPU:1, one launch (start us, length us, event | category | flops | bytes accessed | tf_op | source)
XLA Modules:
  0.0 161.5 jit_solution(7581882774169794306)
XLA Ops:
  0.6 14.5 %all-to-all-start = ((bf16[32,16,768]{2,1,0:T(8,128)(2,1)}), bf16[32,16,768]{2,1,0:T(8,128)(2,1)S(1)}, u32[]{:S(2)}, u32[]{:S(2)}) async-start(bf16[32,16,768]{2,1,0:T(8,128)(2,1)} %bitcast.17), calls=%async_computation | async-start | bytes 1572864 | tf_op jit(solution)/shard_map/all_to_all | solution.py:24
  15.1 5.2 %copy.11 = bf16[64,24,1024]{2,0,1:T(8,128)(2,1)} copy(bf16[64,24,1024]{2,1,0:T(8,128)(2,1)} %param.8) | data formatting | bytes 6291456 | tf_op args[3]
  20.4 0.0 copy-start
  20.4 0.0 copy-start.2
  20.4 0.0 copy-start.1
  20.4 1.0 collective-permute-start
  22.0 0.1 pad_add_fusion.place
  22.1 10.9 %all-to-all-done.spread = bf16[32,16,768]{2,1,0:T(8,128)(2,1)S(1)} async-done(((bf16[32,16,768]{2,1,0:T(8,128)(2,1)}), bf16[32,16,768]{2,1,0:T(8,128)(2,1)S(1)}, u32[]{:S(2)}, u32[]{:S(2)}) %all-to-all-start) | async-done | bytes 786464 | tf_op jit(solution)/shard_map/all_to_all | solution.py:24
  33.0 2.0 %shard_map.68 = bf16[32,2,16,768]{3,2,1,0:T(8,128)(2,1)} custom-call(s32[3]{0:T(128)S(1)} %pad_add_fusion.place, bf16[32,16,768]{2,1,0:T(8,128)(2,1)S(1)} %all-to-all-done.spread), custom_call_target="tpu_custom_call" | custom-call | bytes 3145728 | tf_op jit(solution)/shard_map/pallas_call | solution.py:40
  35.0 4.7 %all-to-all-start.1 = ((bf16[32,2,16,768]{3,2,1,0:T(8,128)(2,1)}), bf16[32,2,16,768]{3,2,1,0:T(8,128)(2,1)}, u32[]{:S(2)}, u32[]{:S(2)}) async-start(bf16[32,2,16,768]{3,2,1,0:T(8,128)(2,1)} %shard_map.68), calls=%async_computation.1 | async-start | bytes 3145728 | tf_op jit(solution)/shard_map/all_to_all | solution.py:24
  39.7 0.0 copy-done
  39.7 1.1 collective-permute-start.1
  40.9 0.0 copy-done.2
  40.9 0.6 dynamic_slice.3
  41.5 0.1 fusion.3
  41.6 0.6 gather_fusion
  42.2 0.0 copy-done.1
  42.2 0.1 copy.9.vir_col
  42.4 0.6 broadcast_add_fusion.energy
  43.0 28.4 %collective-permute-done.1.mate = bf16[512,768]{1,0:T(8,128)(2,1)S(1)} collective-permute-done((bf16[512,768]{1,0:T(8,128)(2,1)S(1)}, bf16[512,768]{1,0:T(8,128)(2,1)S(1)}, u32[]{:S(2)}, u32[]{:S(2)}) %collective-permute-start.1) | collective-permute-done | bytes 786464 | tf_op jit(solution)/shard_map/ppermute | solution.py:32
  71.4 0.0 collective-permute-done.other_any
  71.4 0.0 all-to-all-done.1.rows
  71.4 5.6 %shard_map.69.dens = bf16[32,4,24,128]{3,2,1,0:T(8,128)(2,1)} custom-call(f32[3]{0:T(128)S(1)} %broadcast_add_fusion.energy, f32[1,512]{1,0:T(1,128)S(1)} %bitcast.21, f32[512,1]{1,0:T(8,128)S(1)} %copy.9.vir_col, bf16[32,2,16,768]{3,2,1,0:T(8,128)(2,1)} %all-to-all-done.1.rows, bf16[512,768]{1,0:T(8,128)(2,1)S(1)} %bitcast.19, ...), custom_call_target="tpu_custom_call" | custom-call | flops 3623878656 | bytes 3932160 | tf_op jit(solution)/shard_map/pallas_call | solution.py:40
  77.0 24.4 %all-to-all-start.2 = ((bf16[128,24,128]{2,1,0:T(8,128)(2,1)}), bf16[128,24,128]{2,1,0:T(8,128)(2,1)S(1)}, u32[]{:S(2)}, u32[]{:S(2)}) async-start(bf16[128,24,128]{2,1,0:T(8,128)(2,1)} %bitcast.13), calls=%async_computation.2 | async-start | bytes 1572864 | tf_op jit(solution)/shard_map/all_to_all | solution.py:24
  101.4 3.9 %shard_map.71 = (f32[16,8,24,128]{3,2,1,0:T(8,128)S(1)}, bf16[16,8,24,128]{3,2,1,0:T(8,128)(2,1)S(1)}) custom-call(s32[3]{0:T(128)S(1)} %pad_add_fusion.place, bf16[32,4,24,128]{3,2,1,0:T(8,128)(2,1)} %shard_map.69.dens, bf16[32,2,16,768]{3,2,1,0:T(8,128)(2,1)} %all-to-all-done.1.rows), custom_call_target="tpu_custom_call" | custom-call | flops 603979776 | bytes 3932160 | tf_op jit(solution)/shard_map/pallas_call | solution.py:40
  105.3 0.9 collective-permute-start.2
  106.2 1.9 %collective-permute-done.2.far = bf16[16,8,24,128]{3,2,1,0:T(8,128)(2,1)S(1)} collective-permute-done((bf16[16,8,24,128]{3,2,1,0:T(8,128)(2,1)S(1)}, bf16[16,8,24,128]{3,2,1,0:T(8,128)(2,1)S(1)}, u32[]{:S(2)}, u32[]{:S(2)}) %collective-permute-start.2) | collective-permute-done | bytes 786464 | tf_op jit(solution)/shard_map/ppermute | solution.py:28
  108.1 0.7 shard_map.72
  108.8 0.9 collective-permute-start.3
  109.7 16.2 %all-to-all-done.2.moved_any = bf16[128,24,128]{2,1,0:T(8,128)(2,1)S(1)} async-done(((bf16[128,24,128]{2,1,0:T(8,128)(2,1)}), bf16[128,24,128]{2,1,0:T(8,128)(2,1)S(1)}, u32[]{:S(2)}, u32[]{:S(2)}) %all-to-all-start.2) | async-done | bytes 786464 | tf_op jit(solution)/shard_map/all_to_all | solution.py:24
  125.9 4.1 %shard_map.70.lag = f32[32,2,4,4,128]{4,3,2,1,0:T(4,128)S(1)} custom-call(s32[3]{0:T(128)S(1)} %pad_add_fusion.place, bf16[128,24,128]{2,1,0:T(8,128)(2,1)S(1)} %all-to-all-done.2.moved_any, bf16[24,64,1024]{2,1,0:T(8,128)(2,1)} %bitcast.16.ints_any, bf16[24,64,1024]{2,1,0:T(8,128)(2,1)} %collective-permute-done.other_any), custom_call_target="tpu_custom_call" | custom-call | flops 805306368 | bytes 7864320 | tf_op jit(solution)/shard_map/pallas_call | solution.py:40
  130.0 0.0 collective-permute-done.3.recv
  130.0 0.1 shard_map.73
  130.1 18.7 %all_to_all.25.got = bf16[32,80,128]{2,1,0:T(8,128)(2,1)S(1)} all-to-all(bf16[32,80,128]{2,1,0:T(8,128)(2,1)S(1)} %shard_map.73), channel_id=1, replica_groups=mesh['x'=4,'zh'=2,'yh'=2,'yl'=2,'zl'=4,'core'=2] {'x','yh','yl','core'}, dimensions={0} | all-to-all | bytes 1310720 | tf_op jit(solution)/shard_map/all_to_all | solution.py:24
  148.8 0.1 shard_map.74
  148.9 12.0 %all_to_all.26.got = f32[8,32,128]{2,1,0:T(8,128)S(1)} all-to-all(f32[8,32,128]{2,1,0:T(8,128)S(1)} %shard_map.74), channel_id=1, replica_groups=mesh['x'=4,'zh'=2,'yh'=2,'yl'=2,'zl'=4,'core'=2] {'zh','zl'}, dimensions={0} | all-to-all | bytes 262144 | tf_op jit(solution)/shard_map/all_to_all | solution.py:24
  160.9 0.6 shard_map.75
  (1 shorter events, 0.0 us)
Async XLA Ops:
  0.6 32.4 %all-to-all-start = ((bf16[32,16,768]{2,1,0:T(8,128)(2,1)}), bf16[32,16,768]{2,1,0:T(8,128)(2,1)S(1)}, u32[]{:S(2)}, u32[]{:S(2)}) async-start(bf16[32,16,768]{2,1,0:T(8,128)(2,1)} %bitcast.17), calls=%async_computation | async-start | bytes 1572864 | tf_op jit(solution)/shard_map/all_to_all | solution.py:24
  20.4 19.3 %copy-start = (bf16[1,512,768]{2,1,0:T(8,128)(2,1)S(1)}, bf16[1,512,768]{2,1,0:T(8,128)(2,1)}, u32[]{:S(2)}) copy-start(bf16[1,512,768]{2,1,0:T(8,128)(2,1)} %param.5) | copy-start | bytes 2359300
  20.4 20.5 %copy-start.2 = (f32[256]{0:T(256)S(1)}, f32[256]{0:T(256)}, u32[]{:S(2)}) copy-start(f32[256]{0:T(256)} %param.6) | copy-start | bytes 3076
  20.4 21.8 %copy-start.1 = (f32[512]{0:T(512)S(1)}, f32[512]{0:T(512)}, u32[]{:S(2)}) copy-start(f32[512]{0:T(512)} %param.7) | copy-start | bytes 6148
  20.4 51.0 %collective-permute-start = (bf16[24,64,1024]{2,1,0:T(8,128)(2,1)}, bf16[24,64,1024]{2,1,0:T(8,128)(2,1)}, u32[]{:S(2)}, u32[]{:S(2)}) collective-permute-start(bf16[24,64,1024]{2,1,0:T(8,128)(2,1)} %bitcast.16.ints_any), channel_id=1, source_target_pairs={{0,1},{1,0},{2,3},{3,2},{4,5},{5,4},{6,7},{7,6},{8,9},{9,8},{10,11... | collective-permute-start | bytes 9437192 | tf_op jit(solution)/shard_map/ppermute | solution.py:28
  35.0 36.4 %all-to-all-start.1 = ((bf16[32,2,16,768]{3,2,1,0:T(8,128)(2,1)}), bf16[32,2,16,768]{3,2,1,0:T(8,128)(2,1)}, u32[]{:S(2)}, u32[]{:S(2)}) async-start(bf16[32,2,16,768]{3,2,1,0:T(8,128)(2,1)} %shard_map.68), calls=%async_computation.1 | async-start | bytes 3145728 | tf_op jit(solution)/shard_map/all_to_all | solution.py:24
  39.7 31.7 %collective-permute-start.1 = (bf16[512,768]{1,0:T(8,128)(2,1)S(1)}, bf16[512,768]{1,0:T(8,128)(2,1)S(1)}, u32[]{:S(2)}, u32[]{:S(2)}) collective-permute-start(bf16[512,768]{1,0:T(8,128)(2,1)S(1)} %bitcast.18), channel_id=1, source_target_pairs={{0,8},{8,0},{1,9},{9,1},{2,10},{10,2},{3,11},{11,3},{4,12},{12,4},... | collective-permute-start | bytes 2359304 | tf_op jit(solution)/shard_map/ppermute | solution.py:32
  77.0 48.9 %all-to-all-start.2 = ((bf16[128,24,128]{2,1,0:T(8,128)(2,1)}), bf16[128,24,128]{2,1,0:T(8,128)(2,1)S(1)}, u32[]{:S(2)}, u32[]{:S(2)}) async-start(bf16[128,24,128]{2,1,0:T(8,128)(2,1)} %bitcast.13), calls=%async_computation.2 | async-start | bytes 1572864 | tf_op jit(solution)/shard_map/all_to_all | solution.py:24
  105.3 2.8 %collective-permute-start.2 = (bf16[16,8,24,128]{3,2,1,0:T(8,128)(2,1)S(1)}, bf16[16,8,24,128]{3,2,1,0:T(8,128)(2,1)S(1)}, u32[]{:S(2)}, u32[]{:S(2)}) collective-permute-start(bf16[16,8,24,128]{3,2,1,0:T(8,128)(2,1)S(1)} %get-tuple-element.13), channel_id=1, source_target_pairs={{0,1},{1,0},{2,3},{3,2},{4,5},{5,4},{6,7},{7,6},{8,9},{9,8},{10,11... | collective-permute-start | bytes 2359304 | tf_op jit(solution)/shard_map/ppermute | solution.py:28
  108.8 21.2 %collective-permute-start.3 = (bf16[16,4,24,128]{3,2,1,0:T(8,128)(2,1)S(1)}, bf16[16,4,24,128]{3,2,1,0:T(8,128)(2,1)S(1)}, u32[]{:S(2)}, u32[]{:S(2)}) collective-permute-start(bf16[16,4,24,128]{3,2,1,0:T(8,128)(2,1)S(1)} %get-tuple-element.15), channel_id=1, source_target_pairs={{0,8},{8,0},{1,9},{9,1},{2,10},{10,2},{3,11},{11,3},{4,12},{12,4},... | collective-permute-start | bytes 1179656 | tf_op jit(solution)/shard_map/ppermute | solution.py:32

commit v9 on v8

--- a/solution.py
+++ b/solution.py
@@ -13,7 +13,7 @@
 PLANE = ("x", "yh", "yl", "core")
 DEPTH = ("zh", "zl")
 N_Y = 4
-N_LOAD = 4
+N_LOAD = 6
 
 vmem = pl.BlockSpec(memory_space=pltpu.VMEM)
 smem = pl.BlockSpec(memory_space=pltpu.SMEM)
@@ -120,22 +120,19 @@
         send[:, g] = (near[:, other] + far[:, other].astype(F32)).astype(BF16)
 
 
-def lag_kernel(place, moved_any, ints_any, other_any, parts, wide, acc, moved, ints, other_ints, sems):
-    n_src, aux_blk, lanes = moved_any.shape
+def lag_kernel(place, moved, ints_any, other_any, parts, wide, acc, ints, other_ints, sems):
+    n_src, aux_blk, lanes = moved.shape
     n_orb = ints_any.shape[2]
     n_zl = parts.shape[2]
     n_cyc = n_src // n_zl
     shift, core = place[0], place[2]
-    first = pltpu.make_async_copy(moved_any, moved, sems.at[0])
-    first.start()
     loads = []
     per = aux_blk // N_LOAD
     for n in range(N_LOAD):
         part = pl.ds(n * per, per)
         for src, dst in ((ints_any, ints), (other_any, other_ints)):
-            loads.append(pltpu.make_async_copy(src.at[part], dst.at[part], sems.at[len(loads) + 1]))
+            loads.append(pltpu.make_async_copy(src.at[part], dst.at[part], sems.at[len(loads)]))
             loads[-1].start()
-    first.wait()
     wide[...] = moved[...].reshape(n_src * aux_blk, lanes).astype(F32)
     for p in range(0, aux_blk, 2):
         if p % per == 0:
@@ -297,10 +294,9 @@
         [
             pltpu.VMEM((n_vir * n_aux // LANES, LANES), F32),
             pltpu.VMEM((n_cyc * n_zl, n_orb), F32),
-            pltpu.VMEM((n_cyc * n_zl, aux_blk, LANES), BF16),
             pltpu.VMEM(ints.shape, BF16),
             pltpu.VMEM(ints.shape, BF16),
-            pltpu.SemaphoreType.DMA((1 + 2 * N_LOAD,)),
+            pltpu.SemaphoreType.DMA((2 * N_LOAD,)),
         ],
         2 * n_vir * n_aux * n_orb,
         2 * n_vir * n_aux * 10,
@@ -308,7 +304,7 @@
         moved,
         ints,
         other_ints,
-        specs=[smem, hbm, hbm, hbm],
+        specs=[smem, vmem, hbm, hbm],
     )
     n_rows = 2 * n_zl * n_zl + n_zl // 2 * aux_blk
     parts = call(

time: 162 us -> 162 us (level)
  no operation moved by 1% of the time
where the time goes in v9:
time: 162 us; the launch traced here: 161 us
  waiting for transfers between devices  57.3 us (35%)
  starting transfers between devices  47.5 us (29%)
  blocking collectives  30.7 us (19%)
  Pallas kernels  17 us (10%)
  local copies, waits for them, and re-layouts  6.65 us (4%)
    all_to_all x3, starting transfers between devices, exchange_all(): return lax.all_to_all(x, axes, split_axis=0, concat_axis=0, tiled=True)  43.6 us
    all_to_all x2, blocking collectives, exchange_all(): return lax.all_to_all(x, axes, split_axis=0, concat_axis=0, tiled=True)  30.7 us
    ppermute x2, waiting for transfers between devices, swap_yl(): return lax.ppermute(x, 'yl', [(0, 1), (1, 0)])  28.4 us
    all_to_all x3, waiting for transfers between devices, exchange_all(): return lax.all_to_all(x, axes, split_axis=0, concat_axis=0, tiled=True)  27 us
    pallas_call x8, Pallas kernels, call(): pl.pallas_call(kernel, out_shape=outs, in_specs=specs, out_specs=jax.tree...  17 us
    unnamed x7, local copies, waits for them, and re-layouts  5.26 us
  transfers between devices with their start and end apart: 7, of which 4 were waited for; matrix products, arithmetic and copies ran while one was open for 5% of the time, Pallas kernels for 7%

profile of v9, /device:TPU:1, one launch (start us, length us, event | category | flops | bytes accessed | tf_op | source)
XLA Modules:
  0.0 161.4 jit_solution(3610946189717100980)
XLA Ops:
  0.6 14.5 %all-to-all-start = ((bf16[32,16,768]{2,1,0:T(8,128)(2,1)}), bf16[32,16,768]{2,1,0:T(8,128)(2,1)S(1)}, u32[]{:S(2)}, u32[]{:S(2)}) async-start(bf16[32,16,768]{2,1,0:T(8,128)(2,1)} %bitcast.17), calls=%async_computation | async-start | bytes 1572864 | tf_op jit(solution)/shard_map/all_to_all | solution.py:24
  15.1 5.2 %copy.11 = bf16[64,24,1024]{2,0,1:T(8,128)(2,1)} copy(bf16[64,24,1024]{2,1,0:T(8,128)(2,1)} %param.8) | data formatting | bytes 6291456 | tf_op args[3]
  20.4 0.0 copy-start
  20.4 0.0 copy-start.2
  20.4 0.0 copy-start.1
  20.4 1.0 collective-permute-start
  22.0 0.1 pad_add_fusion.place
  22.1 10.9 %all-to-all-done.spread = bf16[32,16,768]{2,1,0:T(8,128)(2,1)S(1)} async-done(((bf16[32,16,768]{2,1,0:T(8,128)(2,1)}), bf16[32,16,768]{2,1,0:T(8,128)(2,1)S(1)}, u32[]{:S(2)}, u32[]{:S(2)}) %all-to-all-start) | async-done | bytes 786464 | tf_op jit(solution)/shard_map/all_to_all | solution.py:24
  33.0 2.0 %shard_map.68 = bf16[32,2,16,768]{3,2,1,0:T(8,128)(2,1)} custom-call(s32[3]{0:T(128)S(1)} %pad_add_fusion.place, bf16[32,16,768]{2,1,0:T(8,128)(2,1)S(1)} %all-to-all-done.spread), custom_call_target="tpu_custom_call" | custom-call | bytes 3145728 | tf_op jit(solution)/shard_map/pallas_call | solution.py:40
  35.0 4.7 %all-to-all-start.1 = ((bf16[32,2,16,768]{3,2,1,0:T(8,128)(2,1)}), bf16[32,2,16,768]{3,2,1,0:T(8,128)(2,1)}, u32[]{:S(2)}, u32[]{:S(2)}) async-start(bf16[32,2,16,768]{3,2,1,0:T(8,128)(2,1)} %shard_map.68), calls=%async_computation.1 | async-start | bytes 3145728 | tf_op jit(solution)/shard_map/all_to_all | solution.py:24
  39.7 0.0 copy-done
  39.7 1.1 collective-permute-start.1
  40.9 0.0 copy-done.2
  40.9 0.6 dynamic_slice.3
  41.5 0.1 fusion.3
  41.6 0.6 gather_fusion
  42.2 0.0 copy-done.1
  42.2 0.1 copy.9.vir_col
  42.4 0.6 broadcast_add_fusion.energy
  43.0 28.4 %collective-permute-done.1.mate = bf16[512,768]{1,0:T(8,128)(2,1)S(1)} collective-permute-done((bf16[512,768]{1,0:T(8,128)(2,1)S(1)}, bf16[512,768]{1,0:T(8,128)(2,1)S(1)}, u32[]{:S(2)}, u32[]{:S(2)}) %collective-permute-start.1) | collective-permute-done | bytes 786464 | tf_op jit(solution)/shard_map/ppermute | solution.py:32
  71.4 0.0 collective-permute-done.other_any
  71.4 0.0 all-to-all-done.1.rows
  71.4 5.6 %shard_map.69.dens = bf16[32,4,24,128]{3,2,1,0:T(8,128)(2,1)} custom-call(f32[3]{0:T(128)S(1)} %broadcast_add_fusion.energy, f32[1,512]{1,0:T(1,128)S(1)} %bitcast.21, f32[512,1]{1,0:T(8,128)S(1)} %copy.9.vir_col, bf16[32,2,16,768]{3,2,1,0:T(8,128)(2,1)} %all-to-all-done.1.rows, bf16[512,768]{1,0:T(8,128)(2,1)S(1)} %bitcast.19, ...), custom_call_target="tpu_custom_call" | custom-call | flops 3623878656 | bytes 3932160 | tf_op jit(solution)/shard_map/pallas_call | solution.py:40
  77.0 24.4 %all-to-all-start.2 = ((bf16[128,24,128]{2,1,0:T(8,128)(2,1)}), bf16[128,24,128]{2,1,0:T(8,128)(2,1)S(1)}, u32[]{:S(2)}, u32[]{:S(2)}) async-start(bf16[128,24,128]{2,1,0:T(8,128)(2,1)} %bitcast.13), calls=%async_computation.2 | async-start | bytes 1572864 | tf_op jit(solution)/shard_map/all_to_all | solution.py:24
  101.4 3.9 %shard_map.71 = (f32[16,8,24,128]{3,2,1,0:T(8,128)S(1)}, bf16[16,8,24,128]{3,2,1,0:T(8,128)(2,1)S(1)}) custom-call(s32[3]{0:T(128)S(1)} %pad_add_fusion.place, bf16[32,4,24,128]{3,2,1,0:T(8,128)(2,1)} %shard_map.69.dens, bf16[32,2,16,768]{3,2,1,0:T(8,128)(2,1)} %all-to-all-done.1.rows), custom_call_target="tpu_custom_call" | custom-call | flops 603979776 | bytes 3932160 | tf_op jit(solution)/shard_map/pallas_call | solution.py:40
  105.3 0.9 collective-permute-start.2
  106.2 1.9 %collective-permute-done.2.far = bf16[16,8,24,128]{3,2,1,0:T(8,128)(2,1)S(1)} collective-permute-done((bf16[16,8,24,128]{3,2,1,0:T(8,128)(2,1)S(1)}, bf16[16,8,24,128]{3,2,1,0:T(8,128)(2,1)S(1)}, u32[]{:S(2)}, u32[]{:S(2)}) %collective-permute-start.2) | collective-permute-done | bytes 786464 | tf_op jit(solution)/shard_map/ppermute | solution.py:28
  108.1 0.7 shard_map.72
  108.8 0.9 collective-permute-start.3
  109.7 16.2 %all-to-all-done.2.moved = bf16[128,24,128]{2,1,0:T(8,128)(2,1)S(1)} async-done(((bf16[128,24,128]{2,1,0:T(8,128)(2,1)}), bf16[128,24,128]{2,1,0:T(8,128)(2,1)S(1)}, u32[]{:S(2)}, u32[]{:S(2)}) %all-to-all-start.2) | async-done | bytes 786464 | tf_op jit(solution)/shard_map/all_to_all | solution.py:24
  125.9 4.0 %shard_map.70.lag = f32[32,2,4,4,128]{4,3,2,1,0:T(4,128)S(1)} custom-call(s32[3]{0:T(128)S(1)} %pad_add_fusion.place, bf16[128,24,128]{2,1,0:T(8,128)(2,1)S(1)} %all-to-all-done.2.moved, bf16[24,64,1024]{2,1,0:T(8,128)(2,1)} %bitcast.16.ints_any, bf16[24,64,1024]{2,1,0:T(8,128)(2,1)} %collective-permute-done.other_any), custom_call_target="tpu_custom_call" | custom-call | flops 805306368 | bytes 7864320 | tf_op jit(solution)/shard_map/pallas_call | solution.py:40
  129.9 0.0 collective-permute-done.3.recv
  129.9 0.1 shard_map.73
  130.0 18.7 %all_to_all.25.got = bf16[32,80,128]{2,1,0:T(8,128)(2,1)S(1)} all-to-all(bf16[32,80,128]{2,1,0:T(8,128)(2,1)S(1)} %shard_map.73), channel_id=1, replica_groups=mesh['x'=4,'zh'=2,'yh'=2,'yl'=2,'zl'=4,'core'=2] {'x','yh','yl','core'}, dimensions={0} | all-to-all | bytes 1310720 | tf_op jit(solution)/shard_map/all_to_all | solution.py:24
  148.7 0.1 shard_map.74
  148.8 12.0 %all_to_all.26.got = f32[8,32,128]{2,1,0:T(8,128)S(1)} all-to-all(f32[8,32,128]{2,1,0:T(8,128)S(1)} %shard_map.74), channel_id=1, replica_groups=mesh['x'=4,'zh'=2,'yh'=2,'yl'=2,'zl'=4,'core'=2] {'zh','zl'}, dimensions={0} | all-to-all | bytes 262144 | tf_op jit(solution)/shard_map/all_to_all | solution.py:24
  160.8 0.6 shard_map.75
  (1 shorter events, 0.0 us)
Async XLA Ops:
  0.6 32.4 %all-to-all-start = ((bf16[32,16,768]{2,1,0:T(8,128)(2,1)}), bf16[32,16,768]{2,1,0:T(8,128)(2,1)S(1)}, u32[]{:S(2)}, u32[]{:S(2)}) async-start(bf16[32,16,768]{2,1,0:T(8,128)(2,1)} %bitcast.17), calls=%async_computation | async-start | bytes 1572864 | tf_op jit(solution)/shard_map/all_to_all | solution.py:24
  20.4 19.3 %copy-start = (bf16[1,512,768]{2,1,0:T(8,128)(2,1)S(1)}, bf16[1,512,768]{2,1,0:T(8,128)(2,1)}, u32[]{:S(2)}) copy-start(bf16[1,512,768]{2,1,0:T(8,128)(2,1)} %param.5) | copy-start | bytes 2359300
  20.4 20.5 %copy-start.2 = (f32[256]{0:T(256)S(1)}, f32[256]{0:T(256)}, u32[]{:S(2)}) copy-start(f32[256]{0:T(256)} %param.6) | copy-start | bytes 3076
  20.4 21.8 %copy-start.1 = (f32[512]{0:T(512)S(1)}, f32[512]{0:T(512)}, u32[]{:S(2)}) copy-start(f32[512]{0:T(512)} %param.7) | copy-start | bytes 6148
  20.4 51.0 %collective-permute-start = (bf16[24,64,1024]{2,1,0:T(8,128)(2,1)}, bf16[24,64,1024]{2,1,0:T(8,128)(2,1)}, u32[]{:S(2)}, u32[]{:S(2)}) collective-permute-start(bf16[24,64,1024]{2,1,0:T(8,128)(2,1)} %bitcast.16.ints_any), channel_id=1, source_target_pairs={{0,1},{1,0},{2,3},{3,2},{4,5},{5,4},{6,7},{7,6},{8,9},{9,8},{10,11... | collective-permute-start | bytes 9437192 | tf_op jit(solution)/shard_map/ppermute | solution.py:28
  35.0 36.4 %all-to-all-start.1 = ((bf16[32,2,16,768]{3,2,1,0:T(8,128)(2,1)}), bf16[32,2,16,768]{3,2,1,0:T(8,128)(2,1)}, u32[]{:S(2)}, u32[]{:S(2)}) async-start(bf16[32,2,16,768]{3,2,1,0:T(8,128)(2,1)} %shard_map.68), calls=%async_computation.1 | async-start | bytes 3145728 | tf_op jit(solution)/shard_map/all_to_all | solution.py:24
  39.7 31.7 %collective-permute-start.1 = (bf16[512,768]{1,0:T(8,128)(2,1)S(1)}, bf16[512,768]{1,0:T(8,128)(2,1)S(1)}, u32[]{:S(2)}, u32[]{:S(2)}) collective-permute-start(bf16[512,768]{1,0:T(8,128)(2,1)S(1)} %bitcast.18), channel_id=1, source_target_pairs={{0,8},{8,0},{1,9},{9,1},{2,10},{10,2},{3,11},{11,3},{4,12},{12,4},... | collective-permute-start | bytes 2359304 | tf_op jit(solution)/shard_map/ppermute | solution.py:32
  77.0 48.9 %all-to-all-start.2 = ((bf16[128,24,128]{2,1,0:T(8,128)(2,1)}), bf16[128,24,128]{2,1,0:T(8,128)(2,1)S(1)}, u32[]{:S(2)}, u32[]{:S(2)}) async-start(bf16[128,24,128]{2,1,0:T(8,128)(2,1)} %bitcast.13), calls=%async_computation.2 | async-start | bytes 1572864 | tf_op jit(solution)/shard_map/all_to_all | solution.py:24
  105.3 2.8 %collective-permute-start.2 = (bf16[16,8,24,128]{3,2,1,0:T(8,128)(2,1)S(1)}, bf16[16,8,24,128]{3,2,1,0:T(8,128)(2,1)S(1)}, u32[]{:S(2)}, u32[]{:S(2)}) collective-permute-start(bf16[16,8,24,128]{3,2,1,0:T(8,128)(2,1)S(1)} %get-tuple-element.13), channel_id=1, source_target_pairs={{0,1},{1,0},{2,3},{3,2},{4,5},{5,4},{6,7},{7,6},{8,9},{9,8},{10,11... | collective-permute-start | bytes 2359304 | tf_op jit(solution)/shard_map/ppermute | solution.py:28
  108.8 21.1 %collective-permute-start.3 = (bf16[16,4,24,128]{3,2,1,0:T(8,128)(2,1)S(1)}, bf16[16,4,24,128]{3,2,1,0:T(8,128)(2,1)S(1)}, u32[]{:S(2)}, u32[]{:S(2)}) collective-permute-start(bf16[16,4,24,128]{3,2,1,0:T(8,128)(2,1)S(1)} %get-tuple-element.15), channel_id=1, source_target_pairs={{0,8},{8,0},{1,9},{9,1},{2,10},{10,2},{3,11},{11,3},{4,12},{12,4},... | collective-permute-start | bytes 1179656 | tf_op jit(solution)/shard_map/ppermute | solution.py:32
